TPU v7x, 512 devices: a whole 4x8x8 slice. The times are simulated.
512 devices in a mesh: ctx: 128 (over x, y_lo, z, core), tp: 4 (over y_hi).
Axes of the slice: x: 4, y: 8 (y_hi: 4, y_lo: 2; y = y_hi * 2 + y_lo), z: 8, core: 2. Of those that a mesh axis runs over, the one named last changes fastest.
Arguments:
- queries: bfloat16 [8192, 1792], P('ctx', 'tp'), may hold values from -9 to 9
- keys: bfloat16 [8192, 1792], P('ctx', 'tp'), may hold values from -6 to 6
- values: bfloat16 [8192, 1792], P('ctx', 'tp'), may hold values from -6 to 6
- out_weight: bfloat16 [1792, 3584], P('tp'), may hold values from -0.125 to 0.125
Outputs:
- projected: bfloat16 [8192, 3584], P('ctx', 'tp')
All inputs are finite; a program needn't handle non-finite values.
Results may differ from a plain program's by a relative error of at most 0.015.
Values may be sent and summed in bfloat16 or wider, within the bound.
No kernel may reach another device: no remote copies, remote signals or barrier semaphores. Data moves between devices by JAX's collectives and lax.ppermute only.
A program may use at most 128 MiB of HBM per device.

v0:
```python
import jax
import jax.numpy as jnp
from jax import lax
from jax.sharding import PartitionSpec as P

HEAD_DIM = 112


NEG_FILL = -1e30


def swapped(block, axis, distance):
    count = lax.axis_size(axis)
    route = []
    for low in range(count):
        high = low | 1 << distance
        if high != low and high < count:
            route += [(low, high), (high, low)]
    return lax.ppermute(block, axis, route)


def key_positions(gathered_rows, row_count, half_rows, ctx_count):
    shard = gathered_rows // row_count
    offset = gathered_rows - shard * row_count
    return jnp.where(
        offset < half_rows, shard * row_count + offset, (ctx_count - 1 - shard) * row_count + offset
    )


def update_half(running, queries_half, query_pos, keys_block, values_block, key_pos, score_scale):

    def advance(softmax_state):
        row_max, row_total, weighted = softmax_state
        scores = (
            jnp.einsum("qhd,khd->hqk", queries_half, keys_block, preferred_element_type=jnp.float32)
            * score_scale
        )
        causal = query_pos[None, :, None] >= key_pos[None, None, :]
        new_max = jnp.maximum(row_max, jnp.max(jnp.where(causal, scores, NEG_FILL), axis=2))
        raw_weights = jnp.where(causal, jnp.exp(scores - new_max[:, :, None]), 0.0)
        row_total = jnp.sum(raw_weights, axis=2)
        weighted = jnp.einsum(
            "hqk,khd->hqd",
            raw_weights.astype(jnp.bfloat16),
            values_block,
            preferred_element_type=jnp.float32,
        )
        return (new_max, row_total, weighted)

    def keep_state(softmax_state):
        return softmax_state

    return lax.cond(jnp.min(key_pos) <= jnp.max(query_pos), advance, keep_state, running)


def finish(softmax_state):
    row_max, row_total, weighted = softmax_state
    result = weighted / row_total[:, :, None]
    return jnp.transpose(result, (1, 0, 2)).reshape(
        result.shape[1], result.shape[0] * result.shape[2]
    )


def swap_stacked(stacked, bit_total):
    for bit_number in range(bit_total):
        stacked = swapped(stacked, "ctx", bit_number)
    return stacked


def return_attention(later_half, bit_total):
    for bit_number in range(bit_total):
        later_half = swapped(later_half, "ctx", bit_number)
    return later_half


def project(attention, out_weight):
    partial_sums = jnp.dot(attention, out_weight, preferred_element_type=jnp.float32)
    return lax.psum_scatter(
        partial_sums.astype(jnp.bfloat16), "tp", scatter_dimension=1, tiled=True
    )


def shards(queries, keys, values, out_weight):
    row_count, features = queries.shape
    half_rows = row_count // 2
    head_count = features // HEAD_DIM
    ctx_count = lax.axis_size("ctx")
    ctx_index = lax.axis_index("ctx")
    bit_total = ctx_count.bit_length() - 1
    offsets = jnp.arange(row_count, dtype=jnp.int32)
    own_pos = ctx_index * row_count + offsets
    mirror_pos = jnp.where(
        offsets < half_rows, own_pos, (ctx_count - 1 - ctx_index) * row_count + offsets
    )
    stacked = jnp.stack([queries[half_rows:], keys[half_rows:], values[half_rows:]])
    arrived = swap_stacked(stacked, bit_total)
    query_rows = jnp.concatenate([queries[:half_rows], arrived[0]], axis=0)
    key_rows = jnp.concatenate([keys[:half_rows], arrived[1]], axis=0)
    value_rows = jnp.concatenate([values[:half_rows], arrived[2]], axis=0)
    query_heads = query_rows.reshape(row_count, head_count, HEAD_DIM)
    query_first = query_heads[:half_rows]
    query_later = query_heads[half_rows:]
    pos_first = mirror_pos[:half_rows]
    pos_later = mirror_pos[half_rows:]
    score_scale = 1.0 / HEAD_DIM**0.5
    start_state = (
        jnp.full((head_count, half_rows), NEG_FILL, jnp.float32),
        jnp.zeros((head_count, half_rows), jnp.float32),
        jnp.zeros((head_count, half_rows, HEAD_DIM), jnp.float32),
    )
    keys_block = lax.all_gather(key_rows, "ctx", axis=0, tiled=True)
    values_block = lax.all_gather(value_rows, "ctx", axis=0, tiled=True)
    size_rows = keys_block.shape[0]
    key_pos = key_positions(jnp.arange(size_rows, dtype=jnp.int32), row_count, half_rows, ctx_count)
    keys_heads = keys_block.reshape(size_rows, head_count, HEAD_DIM)
    values_heads = values_block.reshape(size_rows, head_count, HEAD_DIM)
    state_first = update_half(
        start_state, query_first, pos_first, keys_heads, values_heads, key_pos, score_scale
    )
    state_later = update_half(
        start_state, query_later, pos_later, keys_heads, values_heads, key_pos, score_scale
    )
    attention = jnp.concatenate([finish(state_first), finish(state_later)], axis=0).astype(
        jnp.bfloat16
    )
    returned = return_attention(attention[half_rows:], bit_total)
    restored = jnp.concatenate([attention[:half_rows], returned], axis=0)
    return project(restored, out_weight)


def solution(mesh):
    placed = (P("ctx", "tp"), P("ctx", "tp"), P("ctx", "tp"), P("tp", None))
    return jax.shard_map(
        shards, mesh=mesh, in_specs=placed, out_specs=P("ctx", "tp"), check_vma=False
    )
```

profile of v0, /device:TPU:56, one launch (start us, length us, event | category | flops | bytes accessed | tf_op | source)
XLA Modules:
  0.0 634.5 jit_solution(4495061184698110682)
XLA Ops:
  11.6 4.3 collective-permute-start.1
  18.9 6.1 collective-permute-start.2
  25.0 4.7 collective-permute-done.2
  29.7 8.4 %collective-permute-start.3 = (bf16[3,32,448]{2,1,0:T(8,128)(2,1)S(1)}, bf16[3,32,448]{2,1,0:T(8,128)(2,1)S(1)}, u32[]{:S(2)}, u32[]{:S(2)}) collective-permute-start(bf16[3,32,448]{2,1,0:T(8,128)(2,1)S(1)} %collective-permute-done.2), channel_id=1, source_target_pairs={{0,32},{32,0},{4,36},{36,4},{8,40},{40,8},{12,44},{44,12},{16,48},... | collective-permute-start | bytes 258056 | tf_op jit(solution)/shard_map/ppermute | solution.py:19
  44.0 3.2 collective-permute-done.4
  47.2 3.4 collective-permute-start.5
  53.7 5.3 collective-permute-start.6
  66.6 220.5 %all-gather.5.cloned.1.call-done = bf16[8192,448]{1,0:T(8,128)(2,1)} async-done(((bf16[64,448]{1,0:T(8,128)(2,1)}), bf16[8192,448]{1,0:T(8,128)(2,1)}) %all-gather.5.cloned.1.call-update) | async-done | bytes 7340048 | tf_op jit(solution)/shard_map/all_gather | solution.py:112
  287.2 10.9 %copy.16 = bf16[8192,448]{0,1:T(8,128)(2,1)} copy(bf16[8192,448]{1,0:T(8,128)(2,1)} %all-gather.5.cloned.1.call-done) | data formatting | bytes 14680064 | tf_op jit(solution)/shard_map/all_gather | solution.py:112
  298.1 213.2 %all-gather.3.cloned.1.call-done = bf16[8192,448]{1,0:T(8,128)(2,1)} async-done(((bf16[64,448]{1,0:T(8,128)(2,1)}), bf16[8192,448]{1,0:T(8,128)(2,1)}) %all-gather.3.cloned.1.call-update) | async-done | bytes 7340048 | tf_op jit(solution)/shard_map/all_gather | solution.py:111
  511.3 11.0 %copy.15 = bf16[8192,448]{0,1:T(8,128)(2,1)} copy(bf16[8192,448]{1,0:T(8,128)(2,1)} %all-gather.3.cloned.1.call-done) | data formatting | bytes 14680064 | tf_op jit(solution)/shard_map/all_gather | solution.py:111
  522.3 12.1 %conditional.3 = (f32[4,32]{1,0:T(4,128)S(1)}, f32[4,32,112]{2,1,0:T(8,128)}) conditional(s32[]{:T(128)} %convert_element_type.17, () %tuple.23, (s32[32]{0:T(128)S(1)}, s32[8192]{0:T(1024)S(1)}, bf16[3,32,448]{2,1,0:T(8,128)(2,1)}, bf16[8192,4,112]{0,2,1:T(8,128)(2,1)}, bf16[8192,4,112]{0,2,1:T(8,128)(2,1)}) %tuple.49), branch_computations={%region_7.8_spmd, %region_8.11_spmd} | conditional | flops 479461248 | bytes 57908396 | solution.py:53
  524.7 4.8 select_reduce_fusion.1
  529.9 3.4 fusion.11
  538.5 3.8 collective-permute-start.8
  544.3 4.7 collective-permute-start.9
  551.0 6.0 collective-permute-start.10
  557.0 3.7 collective-permute-done.10
  560.7 5.0 collective-permute-start.11
  571.9 10.8 %conditional.2 = (f32[4,32]{1,0:T(4,128)S(1)}, f32[4,32,112]{2,1,0:T(8,128)}) conditional(s32[]{:T(128)} %convert_element_type.16, () %tuple.21, (s32[32]{0:T(128)S(1)}, s32[8192]{0:T(1024)S(1)}, bf16[64,448]{1,0:T(8,128)(2,1)}, bf16[8192,4,112]{0,2,1:T(8,128)(2,1)}, bf16[8192,4,112]{0,2,1:T(8,128)(2,1)}) %tuple.48), branch_computations={%region_2.3_spmd, %region_3.6_spmd} | conditional | flops 479461248 | bytes 57908396 | solution.py:53
  573.0 4.8 select_reduce_fusion
  578.2 3.4 fusion.2
  582.7 4.1 collective-permute-start.13
  594.0 32.3 %reduce-scatter.4.cloned.1.call-done = bf16[896,64]{1,0:T(8,128)(2,1)} async-done(((bf16[3584,64]{1,0:T(8,128)(2,1)}), bf16[896,64]{1,0:T(8,128)(2,1)}) %reduce-scatter.4.cloned.1.call-update) | async-done | bytes 114704
  (58 shorter events, 51.6 us)
Async XLA Ops:
  6.5 583.7 %copy-start = (bf16[448,3584]{1,0:T(8,128)(2,1)S(1)}, bf16[448,3584]{1,0:T(8,128)(2,1)}, u32[]{:S(2)}) copy-start(bf16[448,3584]{1,0:T(8,128)(2,1)} %param.11) | copy-start | bytes 9633796
  6.5 280.6 %all-gather.5.cloned.1.call-start = ((), (), s32[]{:S(2)}) async-start(), calls=%async_computation.2 | async-start | bytes 8454144 | tf_op jit(solution)/shard_map/all_gather | solution.py:112
  8.4 3.2 collective-permute-start
  11.6 7.4 %collective-permute-start.1 = (bf16[3,32,448]{2,1,0:T(8,128)(2,1)S(1)}, bf16[3,32,448]{2,1,0:T(8,128)(2,1)S(1)}, u32[]{:S(2)}, u32[]{:S(2)}) collective-permute-start(bf16[3,32,448]{2,1,0:T(8,128)(2,1)S(1)} %collective-permute-done), channel_id=1, source_target_pairs={{0,8},{8,0},{4,12},{12,4},{16,24},{24,16},{20,28},{28,20},{32,40},... | collective-permute-start | bytes 258056 | tf_op jit(solution)/shard_map/ppermute | solution.py:19
  18.9 10.8 %collective-permute-start.2 = (bf16[3,32,448]{2,1,0:T(8,128)(2,1)S(1)}, bf16[3,32,448]{2,1,0:T(8,128)(2,1)S(1)}, u32[]{:S(2)}, u32[]{:S(2)}) collective-permute-start(bf16[3,32,448]{2,1,0:T(8,128)(2,1)S(1)} %collective-permute-done.1), channel_id=1, source_target_pairs={{0,16},{16,0},{4,20},{20,4},{8,24},{24,8},{12,28},{28,12},{32,48},... | collective-permute-start | bytes 258056 | tf_op jit(solution)/shard_map/ppermute | solution.py:19
  29.7 11.0 %collective-permute-start.3 = (bf16[3,32,448]{2,1,0:T(8,128)(2,1)S(1)}, bf16[3,32,448]{2,1,0:T(8,128)(2,1)S(1)}, u32[]{:S(2)}, u32[]{:S(2)}) collective-permute-start(bf16[3,32,448]{2,1,0:T(8,128)(2,1)S(1)} %collective-permute-done.2), channel_id=1, source_target_pairs={{0,32},{32,0},{4,36},{36,4},{8,40},{40,8},{12,44},{44,12},{16,48},... | collective-permute-start | bytes 258056 | tf_op jit(solution)/shard_map/ppermute | solution.py:19
  40.7 6.5 %collective-permute-start.4 = (bf16[3,32,448]{2,1,0:T(8,128)(2,1)S(1)}, bf16[3,32,448]{2,1,0:T(8,128)(2,1)S(1)}, u32[]{:S(2)}, u32[]{:S(2)}) collective-permute-start(bf16[3,32,448]{2,1,0:T(8,128)(2,1)S(1)} %collective-permute-done.3), channel_id=1, source_target_pairs={{0,64},{64,0},{4,68},{68,4},{8,72},{72,8},{12,76},{76,12},{16,80},... | collective-permute-start | bytes 258056 | tf_op jit(solution)/shard_map/ppermute | solution.py:19
  47.2 6.5 %collective-permute-start.5 = (bf16[3,32,448]{2,1,0:T(8,128)(2,1)S(1)}, bf16[3,32,448]{2,1,0:T(8,128)(2,1)S(1)}, u32[]{:S(2)}, u32[]{:S(2)}) collective-permute-start(bf16[3,32,448]{2,1,0:T(8,128)(2,1)S(1)} %collective-permute-done.4), channel_id=1, source_target_pairs={{0,128},{128,0},{4,132},{132,4},{8,136},{136,8},{12,140},{140,12},... | collective-permute-start | bytes 258056 | tf_op jit(solution)/shard_map/ppermute | solution.py:19
  53.7 8.0 %collective-permute-start.6 = (bf16[3,32,448]{2,1,0:T(8,128)(2,1)S(1)}, bf16[3,32,448]{2,1,0:T(8,128)(2,1)S(1)}, u32[]{:S(2)}, u32[]{:S(2)}) collective-permute-start(bf16[3,32,448]{2,1,0:T(8,128)(2,1)S(1)} %collective-permute-done.5), channel_id=1, source_target_pairs={{0,256},{256,0},{4,260},{260,4},{8,264},{264,8},{12,268},{268,12},... | collective-permute-start | bytes 258056 | tf_op jit(solution)/shard_map/ppermute | solution.py:19
  61.7 0.6 copy-start.3
  63.0 448.3 %all-gather.3.cloned.1.call-start = ((), (), s32[]{:S(2)}) async-start(), calls=%async_computation.1 | async-start | bytes 8454144 | tf_op jit(solution)/shard_map/all_gather | solution.py:111
  63.8 562.5 %reduce-scatter.4.cloned.1.call-start = ((), (), s32[]{:S(2)}) async-start(), calls=%async_computation.3 | async-start | bytes 1146880
  524.7 5.2 copy-start.1
  535.4 3.1 collective-permute-start.7
  538.5 5.8 collective-permute-start.8
  544.3 6.7 %collective-permute-start.9 = (bf16[32,448]{1,0:T(8,128)(2,1)S(1)}, bf16[32,448]{1,0:T(8,128)(2,1)S(1)}, u32[]{:S(2)}, u32[]{:S(2)}) collective-permute-start(bf16[32,448]{1,0:T(8,128)(2,1)S(1)} %collective-permute-done.8), channel_id=1, source_target_pairs={{0,16},{16,0},{4,20},{20,4},{8,24},{24,8},{12,28},{28,12},{32,48},... | collective-permute-start | bytes 86024 | tf_op jit(solution)/shard_map/ppermute | solution.py:19
  551.0 9.7 %collective-permute-start.10 = (bf16[32,448]{1,0:T(8,128)(2,1)S(1)}, bf16[32,448]{1,0:T(8,128)(2,1)S(1)}, u32[]{:S(2)}, u32[]{:S(2)}) collective-permute-start(bf16[32,448]{1,0:T(8,128)(2,1)S(1)} %collective-permute-done.9), channel_id=1, source_target_pairs={{0,32},{32,0},{4,36},{36,4},{8,40},{40,8},{12,44},{44,12},{16,48},... | collective-permute-start | bytes 86024 | tf_op jit(solution)/shard_map/ppermute | solution.py:19
  560.7 7.0 %collective-permute-start.11 = (bf16[32,448]{1,0:T(8,128)(2,1)S(1)}, bf16[32,448]{1,0:T(8,128)(2,1)}, u32[]{:S(2)}, u32[]{:S(2)}) collective-permute-start(bf16[32,448]{1,0:T(8,128)(2,1)S(1)} %collective-permute-done.10), channel_id=1, source_target_pairs={{0,64},{64,0},{4,68},{68,4},{8,72},{72,8},{12,76},{76,12},{16,80},... | collective-permute-start | bytes 86024 | tf_op jit(solution)/shard_map/ppermute | solution.py:19
  567.7 15.0 %collective-permute-start.12 = (bf16[32,448]{1,0:T(8,128)(2,1)}, bf16[32,448]{1,0:T(8,128)(2,1)}, u32[]{:S(2)}, u32[]{:S(2)}) collective-permute-start(bf16[32,448]{1,0:T(8,128)(2,1)} %collective-permute-done.11), channel_id=1, source_target_pairs={{0,128},{128,0},{4,132},{132,4},{8,136},{136,8},{12,140},{140,12},... | collective-permute-start | bytes 86024 | tf_op jit(solution)/shard_map/ppermute | solution.py:19
  573.0 5.2 copy-start.2
  582.7 7.5 %collective-permute-start.13 = (bf16[32,448]{1,0:T(8,128)(2,1)}, bf16[32,448]{1,0:T(8,128)(2,1)S(1)}, u32[]{:S(2)}, u32[]{:S(2)}) collective-permute-start(bf16[32,448]{1,0:T(8,128)(2,1)} %collective-permute-done.12), channel_id=1, source_target_pairs={{0,256},{256,0},{4,260},{260,4},{8,264},{264,8},{12,268},{268,12},... | collective-permute-start | bytes 86024 | tf_op jit(solution)/shard_map/ppermute | solution.py:19
Sparse Core Ops, SparseCore 0:
  63.1 223.9 all-gather.4
  289.3 221.8 all-gather.2
  594.1 32.0 reduce-scatter.3
where the time goes:
time: 638 us; the launch traced here: 634 us
  waiting for transfers between devices  500 us (78%)
  starting transfers between devices  61.1 us (10%)
  local copies, waits for them, and re-layouts  32.3 us (5%)
  matrix products  17.9 us (3%)
  between operations  15.9 us (2%)
  other arithmetic  7.26 us (1%)
    all_gather x1, waiting for transfers between devices, shards(): values_block = lax.all_gather(value_rows, 'ctx', axis=0, tiled=True)  221 us
    all_gather x1, waiting for transfers between devices, shards(): keys_block = lax.all_gather(key_rows, 'ctx', axis=0, tiled=True)  213 us
    ppermute x14, starting transfers between devices, swapped(): return lax.ppermute(block, axis, route)  61 us
    ppermute x14, waiting for transfers between devices, swapped(): return lax.ppermute(block, axis, route)  33.9 us
    unnamed x4, waiting for transfers between devices  32.4 us
  transfers between devices with their start and end apart: 17, of which 16 were waited for; matrix products, arithmetic and copies ran while one was open for 4% of the time, Pallas kernels for 0%

commit v1 on v0

v1 whole, which is shorter than its diff:
```python
import math

import jax
import jax.numpy as jnp
from jax import lax
from jax.experimental import pallas as pl
from jax.experimental.pallas import tpu as pltpu
from jax.sharding import Mesh, PartitionSpec as P

HEAD_DIM = 112
LANES = 128
NEG_FILL = -1e30
NEG_CLAMP = -1e29
AXES = ("x", "yl", "zh", "zl", "core", "tp")
CTX = AXES[:5]
QUERY_AXES = ("x", "yl", "zl", "core")
KEY_AXES = ("x", "zh")
VMEM_LIMIT = 48 * 1024 * 1024
EXP2_SCALE = math.log2(math.e) / HEAD_DIM**0.5


def pack_kernel(copies, x_refs, out_ref):
    for head in range(out_ref.shape[0]):
        parts = []
        for x_ref in x_refs:
            own = x_ref[:, head * HEAD_DIM : (head + 1) * HEAD_DIM]
            parts += [own, jnp.zeros((own.shape[0], LANES - HEAD_DIM), own.dtype)]
        block = jnp.concatenate(parts, axis=1)
        for copy in range(copies):
            out_ref[head, copy] = block


def pack(arrays, heads, copies):
    rows = arrays[0].shape[0]

    def body(*refs):
        pack_kernel(copies, refs[:-1], refs[-1])

    return pl.pallas_call(
        body,
        out_shape=jax.ShapeDtypeStruct(
            (heads, copies, rows, LANES * len(arrays)), arrays[0].dtype
        ),
        compiler_params=pltpu.CompilerParams(vmem_limit_bytes=VMEM_LIMIT),
    )(*arrays)


def attend_kernel(x_size, rows, q_ref, kv_ref, out_ref):
    yl, zh, zl, core = (lax.axis_index(name) for name in ("yl", "zh", "zl", "core"))
    block = 4 * rows
    key_count = 4 * rows
    delta = zh * 4 * rows - yl * 16 * rows - zl * 2 * rows - core * rows
    query_at = lax.broadcasted_iota(jnp.int32, (block, key_count), 0)
    key_at = lax.broadcasted_iota(jnp.int32, (block, key_count), 1)
    key_at = (key_at // rows) * (4 * rows) + key_at % rows
    distance = query_at - key_at + delta
    lane = lax.broadcasted_iota(jnp.int32, (block, LANES), 1)
    for x_at in range(x_size):
        known = x_at * key_count
        total = known + key_count
        keys = kv_ref[:total, :LANES]
        values = kv_ref[:total, LANES:]
        lane_v = lax.broadcasted_iota(jnp.int32, (total, LANES), 1)
        values = jnp.where(lane_v == HEAD_DIM, jnp.ones_like(values), values)
        for yl_at in range(2):
            start = (x_at * 2 + yl_at) * block
            queries = q_ref[start : start + block, :]
            scores = lax.dot_general(
                queries, keys, (((1,), (1,)), ((), ())), preferred_element_type=jnp.float32
            )
            last = jnp.where(distance + yl_at * 16 * rows >= 0, scores[:, known:], NEG_FILL)
            if known:
                scores = jnp.concatenate([scores[:, :known], last], axis=1)
            else:
                scores = last
            top = jnp.maximum(jnp.max(scores, axis=1, keepdims=True), NEG_CLAMP)
            weights = jnp.exp2((scores - top) * EXP2_SCALE)
            weighted = jnp.dot(
                weights.astype(jnp.bfloat16), values, preferred_element_type=jnp.float32
            )
            row_total = weighted[:, HEAD_DIM : HEAD_DIM + 1]
            some = row_total > 0.0
            safe = jnp.where(some, row_total, 1.0)
            level = jnp.where(some, top * EXP2_SCALE + jnp.log2(safe), NEG_FILL)
            high = level.astype(jnp.bfloat16).astype(jnp.float32)
            rest = level - high
            middle = rest.astype(jnp.bfloat16).astype(jnp.float32)
            low = rest - middle
            result = weighted * (1.0 / safe)
            result = jnp.where(lane < HEAD_DIM, result, 0.0)
            result = jnp.where(lane == HEAD_DIM, high, result)
            result = jnp.where(lane == HEAD_DIM + 1, middle, result)
            result = jnp.where(lane == HEAD_DIM + 2, low, result)
            out_ref[start : start + block, :] = result.astype(out_ref.dtype)


def attend(queries, keys_values, x_size, rows):
    def body(q_ref, kv_ref, out_ref):
        attend_kernel(x_size, rows, q_ref, kv_ref, out_ref)

    return pl.pallas_call(
        body,
        out_shape=jax.ShapeDtypeStruct(queries.shape, queries.dtype),
        compiler_params=pltpu.CompilerParams(vmem_limit_bytes=VMEM_LIMIT),
    )(queries, keys_values)


def project_kernel(heads, groups, rows, parts_ref, weight_ref, out_ref, attention_ref):
    @pl.when(pl.program_id(0) == 0)
    def _():
        for head in range(heads):
            levels = []
            blocks = []
            for group in range(groups):
                start = (head * groups + group) * rows
                part = parts_ref[start : start + rows, :].astype(jnp.float32)
                blocks.append(part)
                levels.append(
                    part[:, HEAD_DIM : HEAD_DIM + 1]
                    + part[:, HEAD_DIM + 1 : HEAD_DIM + 2]
                    + part[:, HEAD_DIM + 2 : HEAD_DIM + 3]
                )
            top = levels[0]
            for level in levels[1:]:
                top = jnp.maximum(top, level)
            share_sum = jnp.zeros_like(top)
            mixed = jnp.zeros_like(blocks[0])
            for level, part in zip(levels, blocks):
                share = jnp.exp2(level - top)
                share_sum = share_sum + share
                mixed = mixed + share * part
            mixed = mixed / share_sum
            attention_ref[:, head * HEAD_DIM : (head + 1) * HEAD_DIM] = mixed[
                :, :HEAD_DIM
            ].astype(attention_ref.dtype)

    out_ref[0] = jnp.dot(
        attention_ref[...], weight_ref[...], preferred_element_type=jnp.float32
    ).astype(out_ref.dtype)


def project(parts, out_weight, heads, groups, rows, tp_size):
    features, columns = out_weight.shape
    width = columns // tp_size

    def body(parts_ref, weight_ref, out_ref, attention_ref):
        project_kernel(heads, groups, rows, parts_ref, weight_ref, out_ref, attention_ref)

    return pl.pallas_call(
        body,
        grid=(tp_size,),
        in_specs=[
            pl.BlockSpec(parts.shape, lambda i: (0, 0)),
            pl.BlockSpec((features, width), lambda i: (0, i)),
        ],
        out_specs=pl.BlockSpec((1, rows, width), lambda i: (i, 0, 0)),
        out_shape=jax.ShapeDtypeStruct((tp_size, rows, width), jnp.bfloat16),
        scratch_shapes=[pltpu.VMEM((rows, features), jnp.bfloat16)],
        compiler_params=pltpu.CompilerParams(vmem_limit_bytes=VMEM_LIMIT),
    )(parts, out_weight)


def shards(queries, keys, values, out_weight):
    rows, features = queries.shape
    heads = features // HEAD_DIM
    x_size = lax.axis_size("x")
    key_groups = lax.axis_size("yl") * lax.axis_size("zl") * lax.axis_size("core")
    key_parts = lax.axis_size("zh")
    tp_size = lax.axis_size("tp")

    sent_q = pack([queries], heads, key_groups).reshape(heads * key_groups, rows, LANES)
    sent_kv = pack([keys, values], heads, key_parts).reshape(heads * key_parts, rows, 2 * LANES)
    got_q = lax.all_to_all(sent_q, QUERY_AXES, 0, 0, tiled=True)
    got_kv = lax.all_to_all(sent_kv, KEY_AXES, 0, 0, tiled=True)
    partial = attend(
        got_q.reshape(-1, LANES), got_kv.reshape(-1, 2 * LANES), x_size, rows
    )
    returned = lax.all_to_all(
        partial.reshape(heads * key_groups, rows, LANES), QUERY_AXES, 0, 0, tiled=True
    )
    shares = project(
        returned.reshape(-1, LANES), out_weight, heads, key_groups, rows, tp_size
    )
    arrived = lax.all_to_all(shares, "tp", 0, 0, tiled=True)
    return jnp.sum(arrived.astype(jnp.float32), axis=0).astype(jnp.bfloat16)


def solution(mesh):
    split = Mesh(mesh.devices.reshape(4, 2, 4, 2, 2, 4), AXES)
    placed = (P(CTX, "tp"), P(CTX, "tp"), P(CTX, "tp"), P("tp", None))
    return jax.shard_map(
        shards, mesh=split, in_specs=placed, out_specs=P(CTX, "tp"), check_vma=False
    )
```

time: 638 us -> 94.2 us (0.15)
  the two profiles are of different devices: /device:TPU:56 before, /device:TPU:1 now
where the time goes in v1:
time: 94.2 us; the launch traced here: 93.6 us
  blocking collectives  54.2 us (58%)
  starting transfers between devices  13.6 us (14%)
  waiting for transfers between devices  13.6 us (14%)
  Pallas kernels  7.33 us (8%)
  local copies, waits for them, and re-layouts  4.1 us (4%)
    all_to_all x1, blocking collectives, shards(): arrived = lax.all_to_all(shares, 'tp', 0, 0, tiled=True)  20.2 us
    all_to_all x1, blocking collectives, shards(): got_q = lax.all_to_all(sent_q, QUERY_AXES, 0, 0, tiled=True)  19.6 us
    all_to_all x1, blocking collectives, shards(): lax.all_to_all(partial.reshape(heads * key_groups, rows, LANES), QUERY_AX...  14.5 us
    all_to_all x1, waiting for transfers between devices, shards(): got_kv = lax.all_to_all(sent_kv, KEY_AXES, 0, 0, tiled=True)  13.6 us
    all_to_all x1, starting transfers between devices, shards(): got_kv = lax.all_to_all(sent_kv, KEY_AXES, 0, 0, tiled=True)  13.6 us
    pallas_call x1, Pallas kernels, attend(): pl.pallas_call(body, out_shape=jax.ShapeDtypeStruct(queries.shape, querie...  4.47 us
    unnamed x12, local copies, waits for them, and re-layouts  4.1 us
    pallas_call x1, Pallas kernels, project(): pl.pallas_call(body, grid=(tp_size,), in_specs=[pl.BlockSpec(parts.shape,...  2.63 us
  transfers between devices with their start and end apart: 1, of which 1 were waited for; matrix products, arithmetic and copies ran while one was open for 0% of the time, Pallas kernels for 0%

profile of v1, /device:TPU:1, one launch (start us, length us, event | category | flops | bytes accessed | tf_op | source)
XLA Modules:
  0.0 93.6 jit_solution(14599238082558529336)
XLA Ops:
  0.0 0.0 copy-start.3
  0.0 0.8 copy-done.3
  0.8 0.0 copy-start.4
  0.8 0.8 copy-done.4
  1.7 0.0 copy-start
  1.7 0.1 shard_map.47
  1.8 0.0 copy-start.1
  1.8 0.8 copy-done.1
  2.6 13.6 %all-to-all-start.1 = ((bf16[16,64,256]{2,1,0:T(8,128)(2,1)}), bf16[16,64,256]{2,1,0:T(8,128)(2,1)}, u32[]{:S(2)}, u32[]{:S(2)}) async-start(bf16[16,64,256]{2,1,0:T(8,128)(2,1)} %bitcast.8), calls=%async_computation.1 | async-start | bytes 1048576 | tf_op jit(solution)/shard_map/all_to_all | solution.py:174
  16.2 0.0 copy-start.5
  16.2 0.8 copy-done.5
  17.1 0.1 shard_map.46
  17.2 0.0 copy-start.2
  17.2 0.8 copy-done.2
  18.0 13.6 %all-to-all-done.1 = bf16[16,64,256]{2,1,0:T(8,128)(2,1)} async-done(((bf16[16,64,256]{2,1,0:T(8,128)(2,1)}), bf16[16,64,256]{2,1,0:T(8,128)(2,1)}, u32[]{:S(2)}, u32[]{:S(2)}) %all-to-all-start.1) | async-done | bytes 524320 | tf_op jit(solution)/shard_map/all_to_all | solution.py:174
  31.6 19.6 %all_to_all.20 = bf16[32,64,128]{2,1,0:T(8,128)(2,1)S(1)} all-to-all(bf16[32,64,128]{2,1,0:T(8,128)(2,1)} %bitcast.9), channel_id=1, replica_groups=mesh['x'=4,'yl'=2,'zh'=4,'zl'=2,'core'=2,'tp'=4] {'x','yl','zl','core'}, dimensions={0} | all-to-all | bytes 1048576 | tf_op jit(solution)/shard_map/all_to_all | solution.py:173
  51.2 4.5 %shard_map.48 = bf16[2048,128]{1,0:T(8,128)(2,1)S(1)} custom-call(bf16[2048,128]{1,0:T(8,128)(2,1)S(1)} %bitcast.6, bf16[1024,256]{1,0:T(8,128)(2,1)} %bitcast.3.kv_ref), custom_call_target="tpu_custom_call" | custom-call | tf_op jit(solution)/shard_map/pallas_call | solution.py:101
  55.6 14.5 %all_to_all.21 = bf16[32,64,128]{2,1,0:T(8,128)(2,1)S(1)} all-to-all(bf16[32,64,128]{2,1,0:T(8,128)(2,1)S(1)} %bitcast.7), channel_id=1, replica_groups=mesh['x'=4,'yl'=2,'zh'=4,'zl'=2,'core'=2,'tp'=4] {'x','yl','zl','core'}, dimensions={0} | all-to-all | bytes 1048576 | tf_op jit(solution)/shard_map/all_to_all | solution.py:178
  70.1 0.0 copy-done
  70.1 2.6 %shard_map.49 = bf16[4,64,896]{2,1,0:T(8,128)(2,1)S(1)} custom-call(bf16[2048,128]{1,0:T(8,128)(2,1)S(1)} %bitcast.10, bf16[448,3584]{1,0:T(8,128)(2,1)S(1)} %copy-done), custom_call_target="tpu_custom_call" | custom-call | tf_op jit(solution)/shard_map/pallas_call | solution.py:149
  72.8 20.2 %all_to_all.22 = bf16[4,64,896]{2,1,0:T(8,128)(2,1)S(1)} all-to-all(bf16[4,64,896]{2,1,0:T(8,128)(2,1)S(1)} %shard_map.49), channel_id=1, replica_groups=mesh['x'=4,'yl'=2,'zh'=4,'zl'=2,'core'=2,'tp'=4] {'tp'}, dimensions={0} | all-to-all | bytes 917504 | tf_op jit(solution)/shard_map/all_to_all | solution.py:184
  92.9 0.7 reduce_sum.12
Async XLA Ops:
  0.0 0.8 copy-start.3
  0.8 0.8 copy-start.4
  1.7 68.4 %copy-start = (bf16[448,3584]{1,0:T(8,128)(2,1)S(1)}, bf16[448,3584]{1,0:T(8,128)(2,1)}, u32[]{:S(2)}) copy-start(bf16[448,3584]{1,0:T(8,128)(2,1)} %weight_ref.1) | copy-start | bytes 9633796
  1.8 0.8 copy-start.1
  2.6 29.0 %all-to-all-start.1 = ((bf16[16,64,256]{2,1,0:T(8,128)(2,1)}), bf16[16,64,256]{2,1,0:T(8,128)(2,1)}, u32[]{:S(2)}, u32[]{:S(2)}) async-start(bf16[16,64,256]{2,1,0:T(8,128)(2,1)} %bitcast.8), calls=%async_computation.1 | async-start | bytes 1048576 | tf_op jit(solution)/shard_map/all_to_all | solution.py:174
  16.2 0.8 copy-start.5
  17.2 0.8 copy-start.2

commit v2 on v1

--- a/solution.py
+++ b/solution.py
@@ -13,47 +13,55 @@
 NEG_CLAMP = -1e29
 AXES = ("x", "yl", "zh", "zl", "core", "tp")
 CTX = AXES[:5]
-QUERY_AXES = ("x", "yl", "zl", "core")
-KEY_AXES = ("x", "zh")
+QUERY_AXES = ("x", "zh")
+KEY_AXES = ("x", "yl", "zl", "core")
 VMEM_LIMIT = 48 * 1024 * 1024
 EXP2_SCALE = math.log2(math.e) / HEAD_DIM**0.5
 
 
-def pack_kernel(copies, x_refs, out_ref):
-    for head in range(out_ref.shape[0]):
-        parts = []
-        for x_ref in x_refs:
-            own = x_ref[:, head * HEAD_DIM : (head + 1) * HEAD_DIM]
-            parts += [own, jnp.zeros((own.shape[0], LANES - HEAD_DIM), own.dtype)]
-        block = jnp.concatenate(parts, axis=1)
-        for copy in range(copies):
-            out_ref[head, copy] = block
-
-
-def pack(arrays, heads, copies):
-    rows = arrays[0].shape[0]
-
-    def body(*refs):
-        pack_kernel(copies, refs[:-1], refs[-1])
+def pack_kernel(rows, held, q_out, kv_out):
+    for head in range(q_out.shape[0]):
+        columns = slice(head * HEAD_DIM, (head + 1) * HEAD_DIM)
+        key, value, query = (
+            held[part * rows : (part + 1) * rows, columns] for part in range(3)
+        )
+        gap = jnp.zeros((rows, LANES - HEAD_DIM), key.dtype)
+        pair = jnp.concatenate([key, gap, value, gap], axis=1)
+        query = jnp.concatenate([query, gap], axis=1)
+        for copy in range(kv_out.shape[1]):
+            kv_out[head, copy] = pair
+        for copy in range(q_out.shape[1]):
+            q_out[head, copy] = query
+
+
+def pack(queries, keys, values, heads, query_copies, key_copies):
+    rows = queries.shape[0]
+    kind = queries.dtype
+
+    def body(held, q_out, kv_out):
+        pack_kernel(rows, held, q_out, kv_out)
 
     return pl.pallas_call(
         body,
-        out_shape=jax.ShapeDtypeStruct(
-            (heads, copies, rows, LANES * len(arrays)), arrays[0].dtype
+        out_shape=(
+            jax.ShapeDtypeStruct((heads, query_copies, rows, LANES), kind),
+            jax.ShapeDtypeStruct((heads, key_copies, rows, 2 * LANES), kind),
         ),
         compiler_params=pltpu.CompilerParams(vmem_limit_bytes=VMEM_LIMIT),
-    )(*arrays)
+    )(jnp.concatenate([keys, values, queries], axis=0))
 
 
 def attend_kernel(x_size, rows, q_ref, kv_ref, out_ref):
     yl, zh, zl, core = (lax.axis_index(name) for name in ("yl", "zh", "zl", "core"))
     block = 4 * rows
-    key_count = 4 * rows
-    delta = zh * 4 * rows - yl * 16 * rows - zl * 2 * rows - core * rows
+    coarse = 16 * rows
+    key_count = 2 * block
+    delta = yl * coarse + zl * 2 * rows + core * rows - zh * block
     query_at = lax.broadcasted_iota(jnp.int32, (block, key_count), 0)
+    query_at = (query_at // rows) * block + query_at % rows
     key_at = lax.broadcasted_iota(jnp.int32, (block, key_count), 1)
-    key_at = (key_at // rows) * (4 * rows) + key_at % rows
-    distance = query_at - key_at + delta
+    key_at = (key_at // block) * coarse + key_at % block
+    kept = query_at - key_at + delta >= 0
     lane = lax.broadcasted_iota(jnp.int32, (block, LANES), 1)
     for x_at in range(x_size):
         known = x_at * key_count
@@ -62,13 +70,12 @@
         values = kv_ref[:total, LANES:]
         lane_v = lax.broadcasted_iota(jnp.int32, (total, LANES), 1)
         values = jnp.where(lane_v == HEAD_DIM, jnp.ones_like(values), values)
-        for yl_at in range(2):
-            start = (x_at * 2 + yl_at) * block
+        for start in (x_at * block,):
             queries = q_ref[start : start + block, :]
             scores = lax.dot_general(
                 queries, keys, (((1,), (1,)), ((), ())), preferred_element_type=jnp.float32
             )
-            last = jnp.where(distance + yl_at * 16 * rows >= 0, scores[:, known:], NEG_FILL)
+            last = jnp.where(kept, scores[:, known:], NEG_FILL)
             if known:
                 scores = jnp.concatenate([scores[:, :known], last], axis=1)
             else:
@@ -164,22 +171,25 @@
     rows, features = queries.shape
     heads = features // HEAD_DIM
     x_size = lax.axis_size("x")
-    key_groups = lax.axis_size("yl") * lax.axis_size("zl") * lax.axis_size("core")
-    key_parts = lax.axis_size("zh")
+    query_copies = lax.axis_size("zh")
+    key_copies = lax.axis_size("yl") * lax.axis_size("zl") * lax.axis_size("core")
     tp_size = lax.axis_size("tp")
 
-    sent_q = pack([queries], heads, key_groups).reshape(heads * key_groups, rows, LANES)
-    sent_kv = pack([keys, values], heads, key_parts).reshape(heads * key_parts, rows, 2 * LANES)
-    got_q = lax.all_to_all(sent_q, QUERY_AXES, 0, 0, tiled=True)
-    got_kv = lax.all_to_all(sent_kv, KEY_AXES, 0, 0, tiled=True)
+    sent_q, sent_kv = pack(queries, keys, values, heads, query_copies, key_copies)
+    got_q = lax.all_to_all(
+        sent_q.reshape(heads * query_copies, rows, LANES), QUERY_AXES, 0, 0, tiled=True
+    )
+    got_kv = lax.all_to_all(
+        sent_kv.reshape(heads * key_copies, rows, 2 * LANES), KEY_AXES, 0, 0, tiled=True
+    )
     partial = attend(
         got_q.reshape(-1, LANES), got_kv.reshape(-1, 2 * LANES), x_size, rows
     )
     returned = lax.all_to_all(
-        partial.reshape(heads * key_groups, rows, LANES), QUERY_AXES, 0, 0, tiled=True
+        partial.reshape(heads * query_copies, rows, LANES), QUERY_AXES, 0, 0, tiled=True
     )
     shares = project(
-        returned.reshape(-1, LANES), out_weight, heads, key_groups, rows, tp_size
+        returned.reshape(-1, LANES), out_weight, heads, query_copies, rows, tp_size
     )
     arrived = lax.all_to_all(shares, "tp", 0, 0, tiled=True)
     return jnp.sum(arrived.astype(jnp.float32), axis=0).astype(jnp.bfloat16)

time: 94.2 us -> 91 us (0.966)
  the two profiles are of different devices: /device:TPU:1 before, /device:TPU:8 now
where the time goes in v2:
time: 91 us; the launch traced here: 90.8 us
  blocking collectives  84 us (92%)
  Pallas kernels  4.99 us (5%)
  other arithmetic  1.79 us (2%)
    all_to_all x1, blocking collectives, shards(): lax.all_to_all(sent_q.reshape(heads * query_copies, rows, LANES), QUERY_A...  26.1 us
    all_to_all x1, blocking collectives, shards(): arrived = lax.all_to_all(shares, 'tp', 0, 0, tiled=True)  21.1 us
    all_to_all x1, blocking collectives, shards(): lax.all_to_all(sent_kv.reshape(heads * key_copies, rows, 2 * LANES), KEY_...  19.5 us
    all_to_all x1, blocking collectives, shards(): lax.all_to_all(partial.reshape(heads * query_copies, rows, LANES), QUERY_...  17.2 us
    pallas_call x1, Pallas kernels, attend(): pl.pallas_call(body, out_shape=jax.ShapeDtypeStruct(queries.shape, querie...  2.55 us
    pallas_call x1, Pallas kernels, project(): pl.pallas_call(body, grid=(tp_size,), in_specs=[pl.BlockSpec(parts.shape,...  2.28 us

profile of v2, /device:TPU:8, one launch (start us, length us, event | category | flops | bytes accessed | tf_op | source)
XLA Modules:
  0.0 90.8 jit_solution(17102602250264166090)
XLA Ops:
  0.0 0.0 copy-start
  0.0 1.1 %pad_maximum_fusion.held = bf16[192,448]{1,0:T(8,128)(2,1)S(1)} fusion(bf16[64,448]{1,0:T(8,128)(2,1)} %param.4, bf16[64,448]{1,0:T(8,128)(2,1)} %param.6, bf16[64,448]{1,0:T(8,128)(2,1)} %param.5), kind=kLoop, calls=%fused_computation | loop fusion | flops 516096 | bytes 344064 | tf_op jit(solution)/shard_map/concatenate | solution.py:51
  1.1 0.2 shard_map.46
  1.2 26.1 %all_to_all.20 = bf16[16,64,128]{2,1,0:T(8,128)(2,1)S(1)} all-to-all(bf16[16,64,128]{2,1,0:T(8,128)(2,1)S(1)} %bitcast.11), channel_id=1, replica_groups=mesh['x'=4,'yl'=2,'zh'=4,'zl'=2,'core'=2,'tp'=4] {'x','zh'}, dimensions={0} | all-to-all | bytes 524288 | tf_op jit(solution)/shard_map/all_to_all | solution.py:179
  27.3 19.5 %all_to_all.21 = bf16[32,64,256]{2,1,0:T(8,128)(2,1)S(1)} all-to-all(bf16[32,64,256]{2,1,0:T(8,128)(2,1)S(1)} %bitcast.7), channel_id=1, replica_groups=mesh['x'=4,'yl'=2,'zh'=4,'zl'=2,'core'=2,'tp'=4] {'x','yl','zl','core'}, dimensions={0} | all-to-all | bytes 2097152 | tf_op jit(solution)/shard_map/all_to_all | solution.py:182
  46.9 2.6 %shard_map.47 = bf16[1024,128]{1,0:T(8,128)(2,1)S(1)} custom-call(bf16[1024,128]{1,0:T(8,128)(2,1)S(1)} %bitcast.8, bf16[2048,256]{1,0:T(8,128)(2,1)S(1)} %bitcast.6), custom_call_target="tpu_custom_call" | custom-call | tf_op jit(solution)/shard_map/pallas_call | solution.py:108
  49.4 17.2 %all_to_all.22 = bf16[16,64,128]{2,1,0:T(8,128)(2,1)S(1)} all-to-all(bf16[16,64,128]{2,1,0:T(8,128)(2,1)S(1)} %bitcast.9), channel_id=1, replica_groups=mesh['x'=4,'yl'=2,'zh'=4,'zl'=2,'core'=2,'tp'=4] {'x','zh'}, dimensions={0} | all-to-all | bytes 524288 | tf_op jit(solution)/shard_map/all_to_all | solution.py:188
  66.7 0.0 copy-done
  66.7 2.3 %shard_map.48 = bf16[4,64,896]{2,1,0:T(8,128)(2,1)S(1)} custom-call(bf16[1024,128]{1,0:T(8,128)(2,1)S(1)} %bitcast.10, bf16[448,3584]{1,0:T(8,128)(2,1)S(1)} %copy-done), custom_call_target="tpu_custom_call" | custom-call | tf_op jit(solution)/shard_map/pallas_call | solution.py:156
  68.9 21.1 %all_to_all.23 = bf16[4,64,896]{2,1,0:T(8,128)(2,1)S(1)} all-to-all(bf16[4,64,896]{2,1,0:T(8,128)(2,1)S(1)} %shard_map.48), channel_id=1, replica_groups=mesh['x'=4,'yl'=2,'zh'=4,'zl'=2,'core'=2,'tp'=4] {'tp'}, dimensions={0} | all-to-all | bytes 917504 | tf_op jit(solution)/shard_map/all_to_all | solution.py:194
  90.1 0.7 reduce_sum.12
Async XLA Ops:
  0.0 66.7 %copy-start = (bf16[448,3584]{1,0:T(8,128)(2,1)S(1)}, bf16[448,3584]{1,0:T(8,128)(2,1)}, u32[]{:S(2)}) copy-start(bf16[448,3584]{1,0:T(8,128)(2,1)} %weight_ref.1) | copy-start | bytes 9633796

commit v3 on v2

--- a/solution.py
+++ b/solution.py
@@ -9,12 +9,13 @@
 
 HEAD_DIM = 112
 LANES = 128
+TOTAL, TOTAL_LOW, SHIFT = HEAD_DIM, HEAD_DIM + 1, HEAD_DIM + 2
 NEG_FILL = -1e30
 NEG_CLAMP = -1e29
 AXES = ("x", "yl", "zh", "zl", "core", "tp")
 CTX = AXES[:5]
-QUERY_AXES = ("x", "zh")
-KEY_AXES = ("x", "yl", "zl", "core")
+QUERY_AXES = ("x", "yl", "zl", "core")
+KEY_AXES = ("x", "zh")
 VMEM_LIMIT = 48 * 1024 * 1024
 EXP2_SCALE = math.log2(math.e) / HEAD_DIM**0.5
 
@@ -26,7 +27,7 @@
             held[part * rows : (part + 1) * rows, columns] for part in range(3)
         )
         gap = jnp.zeros((rows, LANES - HEAD_DIM), key.dtype)
-        pair = jnp.concatenate([key, gap, value, gap], axis=1)
+        pair = jnp.concatenate([key, gap, value, jnp.ones_like(gap)], axis=1)
         query = jnp.concatenate([query, gap], axis=1)
         for copy in range(kv_out.shape[1]):
             kv_out[head, copy] = pair
@@ -55,50 +56,38 @@
     yl, zh, zl, core = (lax.axis_index(name) for name in ("yl", "zh", "zl", "core"))
     block = 4 * rows
     coarse = 16 * rows
-    key_count = 2 * block
-    delta = yl * coarse + zl * 2 * rows + core * rows - zh * block
-    query_at = lax.broadcasted_iota(jnp.int32, (block, key_count), 0)
-    query_at = (query_at // rows) * block + query_at % rows
-    key_at = lax.broadcasted_iota(jnp.int32, (block, key_count), 1)
-    key_at = (key_at // block) * coarse + key_at % block
-    kept = query_at - key_at + delta >= 0
+    delta = zh * block - yl * coarse - zl * 2 * rows - core * rows
+    query_at = lax.broadcasted_iota(jnp.int32, (block, block), 0)
+    key_at = lax.broadcasted_iota(jnp.int32, (block, block), 1)
+    key_at = (key_at // rows) * block + key_at % rows
+    distance = query_at - key_at + delta
     lane = lax.broadcasted_iota(jnp.int32, (block, LANES), 1)
     for x_at in range(x_size):
-        known = x_at * key_count
-        total = known + key_count
+        known = x_at * block
+        total = known + block
         keys = kv_ref[:total, :LANES]
         values = kv_ref[:total, LANES:]
-        lane_v = lax.broadcasted_iota(jnp.int32, (total, LANES), 1)
-        values = jnp.where(lane_v == HEAD_DIM, jnp.ones_like(values), values)
-        for start in (x_at * block,):
+        for yl_at in range(2):
+            start = (x_at * 2 + yl_at) * block
             queries = q_ref[start : start + block, :]
             scores = lax.dot_general(
                 queries, keys, (((1,), (1,)), ((), ())), preferred_element_type=jnp.float32
             )
-            last = jnp.where(kept, scores[:, known:], NEG_FILL)
+            last = jnp.where(distance + yl_at * coarse >= 0, scores[:, known:], NEG_FILL)
             if known:
                 scores = jnp.concatenate([scores[:, :known], last], axis=1)
             else:
                 scores = last
-            top = jnp.maximum(jnp.max(scores, axis=1, keepdims=True), NEG_CLAMP)
-            weights = jnp.exp2((scores - top) * EXP2_SCALE)
+            top = jnp.maximum(jnp.max(scores, axis=1, keepdims=True), NEG_CLAMP) * EXP2_SCALE
+            shift = top.astype(jnp.bfloat16).astype(jnp.float32)
+            weights = jnp.exp2(scores * EXP2_SCALE - shift)
             weighted = jnp.dot(
                 weights.astype(jnp.bfloat16), values, preferred_element_type=jnp.float32
             )
-            row_total = weighted[:, HEAD_DIM : HEAD_DIM + 1]
-            some = row_total > 0.0
-            safe = jnp.where(some, row_total, 1.0)
-            level = jnp.where(some, top * EXP2_SCALE + jnp.log2(safe), NEG_FILL)
-            high = level.astype(jnp.bfloat16).astype(jnp.float32)
-            rest = level - high
-            middle = rest.astype(jnp.bfloat16).astype(jnp.float32)
-            low = rest - middle
-            result = weighted * (1.0 / safe)
-            result = jnp.where(lane < HEAD_DIM, result, 0.0)
-            result = jnp.where(lane == HEAD_DIM, high, result)
-            result = jnp.where(lane == HEAD_DIM + 1, middle, result)
-            result = jnp.where(lane == HEAD_DIM + 2, low, result)
-            out_ref[start : start + block, :] = result.astype(out_ref.dtype)
+            rounded = weighted.astype(jnp.bfloat16).astype(jnp.float32)
+            weighted = jnp.where(lane == TOTAL_LOW, weighted - rounded, weighted)
+            weighted = jnp.where(lane == SHIFT, shift, weighted)
+            out_ref[start : start + block, :] = weighted.astype(out_ref.dtype)
 
 
 def attend(queries, keys_values, x_size, rows):
@@ -116,30 +105,25 @@
     @pl.when(pl.program_id(0) == 0)
     def _():
         for head in range(heads):
-            levels = []
-            blocks = []
-            for group in range(groups):
-                start = (head * groups + group) * rows
-                part = parts_ref[start : start + rows, :].astype(jnp.float32)
-                blocks.append(part)
-                levels.append(
-                    part[:, HEAD_DIM : HEAD_DIM + 1]
-                    + part[:, HEAD_DIM + 1 : HEAD_DIM + 2]
-                    + part[:, HEAD_DIM + 2 : HEAD_DIM + 3]
-                )
-            top = levels[0]
-            for level in levels[1:]:
-                top = jnp.maximum(top, level)
-            share_sum = jnp.zeros_like(top)
-            mixed = jnp.zeros_like(blocks[0])
-            for level, part in zip(levels, blocks):
-                share = jnp.exp2(level - top)
-                share_sum = share_sum + share
-                mixed = mixed + share * part
-            mixed = mixed / share_sum
-            attention_ref[:, head * HEAD_DIM : (head + 1) * HEAD_DIM] = mixed[
-                :, :HEAD_DIM
-            ].astype(attention_ref.dtype)
+            parts = [
+                parts_ref[
+                    (head * groups + group) * rows : (head * groups + group + 1) * rows, :
+                ].astype(jnp.float32)
+                for group in range(groups)
+            ]
+            shifts = [part[:, SHIFT : SHIFT + 1] for part in parts]
+            top = shifts[0]
+            for shift in shifts[1:]:
+                top = jnp.maximum(top, shift)
+            mixed = jnp.zeros_like(parts[0])
+            for shift, part in zip(shifts, parts):
+                mixed = mixed + jnp.exp2(shift - top) * part
+            row_total = (
+                mixed[:, TOTAL : TOTAL + 1] + mixed[:, TOTAL_LOW : TOTAL_LOW + 1]
+            )
+            attention_ref[:, head * HEAD_DIM : (head + 1) * HEAD_DIM] = (
+                mixed[:, :HEAD_DIM] / row_total
+            ).astype(attention_ref.dtype)
 
     out_ref[0] = jnp.dot(
         attention_ref[...], weight_ref[...], preferred_element_type=jnp.float32
@@ -171,8 +155,8 @@
     rows, features = queries.shape
     heads = features // HEAD_DIM
     x_size = lax.axis_size("x")
-    query_copies = lax.axis_size("zh")
-    key_copies = lax.axis_size("yl") * lax.axis_size("zl") * lax.axis_size("core")
+    query_copies = lax.axis_size("yl") * lax.axis_size("zl") * lax.axis_size("core")
+    key_copies = lax.axis_size("zh")
     tp_size = lax.axis_size("tp")
 
     sent_q, sent_kv = pack(queries, keys, values, heads, query_copies, key_copies)

time: 91 us -> 90.2 us (level)
  the two profiles are of different devices: /device:TPU:8 before, /device:TPU:1 now
where the time goes in v3:
time: 90.2 us; the launch traced here: 90 us
  blocking collectives  82.5 us (91%)
  Pallas kernels  5.63 us (6%)
  other arithmetic  1.79 us (2%)
    all_to_all x1, blocking collectives, shards(): lax.all_to_all(sent_kv.reshape(heads * key_copies, rows, 2 * LANES), KEY_...  28.6 us
    all_to_all x1, blocking collectives, shards(): arrived = lax.all_to_all(shares, 'tp', 0, 0, tiled=True)  20.2 us
    all_to_all x1, blocking collectives, shards(): lax.all_to_all(sent_q.reshape(heads * query_copies, rows, LANES), QUERY_A...  19.4 us
    all_to_all x1, blocking collectives, shards(): lax.all_to_all(partial.reshape(heads * query_copies, rows, LANES), QUERY_...  14.5 us
    pallas_call x1, Pallas kernels, attend(): pl.pallas_call(body, out_shape=jax.ShapeDtypeStruct(queries.shape, querie...  3.07 us
    pallas_call x1, Pallas kernels, project(): pl.pallas_call(body, grid=(tp_size,), in_specs=[pl.BlockSpec(parts.shape,...  2.4 us

profile of v3, /device:TPU:1, one launch (start us, length us, event | category | flops | bytes accessed | tf_op | source)
XLA Modules:
  0.0 90.0 jit_solution(2454270665158476528)
XLA Ops:
  0.0 0.0 copy-start
  0.0 1.1 %pad_maximum_fusion.held = bf16[192,448]{1,0:T(8,128)(2,1)S(1)} fusion(bf16[64,448]{1,0:T(8,128)(2,1)} %param.4, bf16[64,448]{1,0:T(8,128)(2,1)} %param.6, bf16[64,448]{1,0:T(8,128)(2,1)} %param.5), kind=kLoop, calls=%fused_computation | loop fusion | flops 516096 | bytes 344064 | tf_op jit(solution)/shard_map/concatenate | solution.py:52
  1.1 0.2 shard_map.46
  1.2 28.6 %all_to_all.20 = bf16[16,64,256]{2,1,0:T(8,128)(2,1)S(1)} all-to-all(bf16[16,64,256]{2,1,0:T(8,128)(2,1)S(1)} %bitcast.11), channel_id=1, replica_groups=mesh['x'=4,'yl'=2,'zh'=4,'zl'=2,'core'=2,'tp'=4] {'x','zh'}, dimensions={0} | all-to-all | bytes 1048576 | tf_op jit(solution)/shard_map/all_to_all | solution.py:166
  29.8 19.4 %all_to_all.21 = bf16[32,64,128]{2,1,0:T(8,128)(2,1)S(1)} all-to-all(bf16[32,64,128]{2,1,0:T(8,128)(2,1)S(1)} %bitcast.10), channel_id=1, replica_groups=mesh['x'=4,'yl'=2,'zh'=4,'zl'=2,'core'=2,'tp'=4] {'x','yl','zl','core'}, dimensions={0} | all-to-all | bytes 1048576 | tf_op jit(solution)/shard_map/all_to_all | solution.py:163
  49.2 3.1 %shard_map.47 = bf16[2048,128]{1,0:T(8,128)(2,1)S(1)} custom-call(bf16[2048,128]{1,0:T(8,128)(2,1)S(1)} %bitcast.7, bf16[1024,256]{1,0:T(8,128)(2,1)S(1)} %bitcast.6), custom_call_target="tpu_custom_call" | custom-call | tf_op jit(solution)/shard_map/pallas_call | solution.py:97
  52.2 14.5 %all_to_all.22 = bf16[32,64,128]{2,1,0:T(8,128)(2,1)S(1)} all-to-all(bf16[32,64,128]{2,1,0:T(8,128)(2,1)S(1)} %bitcast.8), channel_id=1, replica_groups=mesh['x'=4,'yl'=2,'zh'=4,'zl'=2,'core'=2,'tp'=4] {'x','yl','zl','core'}, dimensions={0} | all-to-all | bytes 1048576 | tf_op jit(solution)/shard_map/all_to_all | solution.py:172
  66.7 0.0 copy-done
  66.7 2.4 %shard_map.48 = bf16[4,64,896]{2,1,0:T(8,128)(2,1)S(1)} custom-call(bf16[2048,128]{1,0:T(8,128)(2,1)S(1)} %bitcast.9, bf16[448,3584]{1,0:T(8,128)(2,1)S(1)} %copy-done), custom_call_target="tpu_custom_call" | custom-call | tf_op jit(solution)/shard_map/pallas_call | solution.py:140
  69.1 20.2 %all_to_all.23 = bf16[4,64,896]{2,1,0:T(8,128)(2,1)S(1)} all-to-all(bf16[4,64,896]{2,1,0:T(8,128)(2,1)S(1)} %shard_map.48), channel_id=1, replica_groups=mesh['x'=4,'yl'=2,'zh'=4,'zl'=2,'core'=2,'tp'=4] {'tp'}, dimensions={0} | all-to-all | bytes 917504 | tf_op jit(solution)/shard_map/all_to_all | solution.py:178
  89.3 0.7 reduce_sum.12
Async XLA Ops:
  0.0 66.7 %copy-start = (bf16[448,3584]{1,0:T(8,128)(2,1)S(1)}, bf16[448,3584]{1,0:T(8,128)(2,1)}, u32[]{:S(2)}) copy-start(bf16[448,3584]{1,0:T(8,128)(2,1)} %weight_ref.1) | copy-start | bytes 9633796

commit v4 on v3

--- a/solution.py
+++ b/solution.py
@@ -101,54 +101,87 @@
     )(queries, keys_values)
 
 
-def project_kernel(heads, groups, rows, parts_ref, weight_ref, out_ref, attention_ref):
-    @pl.when(pl.program_id(0) == 0)
-    def _():
-        for head in range(heads):
-            parts = [
-                parts_ref[
-                    (head * groups + group) * rows : (head * groups + group + 1) * rows, :
-                ].astype(jnp.float32)
-                for group in range(groups)
-            ]
-            shifts = [part[:, SHIFT : SHIFT + 1] for part in parts]
-            top = shifts[0]
-            for shift in shifts[1:]:
-                top = jnp.maximum(top, shift)
-            mixed = jnp.zeros_like(parts[0])
-            for shift, part in zip(shifts, parts):
-                mixed = mixed + jnp.exp2(shift - top) * part
-            row_total = (
-                mixed[:, TOTAL : TOTAL + 1] + mixed[:, TOTAL_LOW : TOTAL_LOW + 1]
-            )
-            attention_ref[:, head * HEAD_DIM : (head + 1) * HEAD_DIM] = (
-                mixed[:, :HEAD_DIM] / row_total
-            ).astype(attention_ref.dtype)
-
-    out_ref[0] = jnp.dot(
-        attention_ref[...], weight_ref[...], preferred_element_type=jnp.float32
-    ).astype(out_ref.dtype)
-
-
-def project(parts, out_weight, heads, groups, rows, tp_size):
+def combine(parts_ref, attention_ref, heads, groups, rows):
+    for head in range(heads):
+        parts = [
+            parts_ref[
+                (head * groups + group) * rows : (head * groups + group + 1) * rows, :
+            ].astype(jnp.float32)
+            for group in range(groups)
+        ]
+        shifts = [part[:, SHIFT : SHIFT + 1] for part in parts]
+        top = shifts[0]
+        for shift in shifts[1:]:
+            top = jnp.maximum(top, shift)
+        mixed = jnp.zeros_like(parts[0])
+        for shift, part in zip(shifts, parts):
+            mixed = mixed + jnp.exp2(shift - top) * part
+        row_total = mixed[:, TOTAL : TOTAL + 1] + mixed[:, TOTAL_LOW : TOTAL_LOW + 1]
+        attention_ref[:, head * HEAD_DIM : (head + 1) * HEAD_DIM] = (
+            mixed[:, :HEAD_DIM] / row_total
+        ).astype(attention_ref.dtype)
+
+
+def share_of(attention_ref, weight_ref, step, tp_size):
+    width = weight_ref.shape[1] // tp_size
+    member = lax.rem(lax.axis_index("tp") + step, tp_size)
+    columns = pl.ds(pl.multiple_of(member * width, LANES), width)
+    return jnp.dot(
+        attention_ref[...], weight_ref[:, columns], preferred_element_type=jnp.float32
+    )
+
+
+def project_far(parts, out_weight, heads, groups, rows, step, tp_size):
     features, columns = out_weight.shape
-    width = columns // tp_size
-
-    def body(parts_ref, weight_ref, out_ref, attention_ref):
-        project_kernel(heads, groups, rows, parts_ref, weight_ref, out_ref, attention_ref)
-
-    return pl.pallas_call(
-        body,
-        grid=(tp_size,),
-        in_specs=[
-            pl.BlockSpec(parts.shape, lambda i: (0, 0)),
-            pl.BlockSpec((features, width), lambda i: (0, i)),
+
+    def body(parts_ref, weight_ref, attention_ref, far_ref):
+        combine(parts_ref, attention_ref, heads, groups, rows)
+        far_ref[...] = share_of(attention_ref, weight_ref, step, tp_size).astype(far_ref.dtype)
+
+    return pl.pallas_call(
+        body,
+        out_shape=(
+            jax.ShapeDtypeStruct((rows, features), jnp.bfloat16),
+            jax.ShapeDtypeStruct((rows, columns // tp_size), jnp.bfloat16),
+        ),
+        cost_estimate=pl.CostEstimate(
+            flops=2 * rows * features * columns // tp_size,
+            bytes_accessed=2 * features * columns,
+            transcendentals=0,
+        ),
+        compiler_params=pltpu.CompilerParams(vmem_limit_bytes=VMEM_LIMIT),
+    )(parts, out_weight)
+
+
+def project_near(attention, out_weight, steps, tp_size):
+    rows, features = attention.shape
+    columns = out_weight.shape[1]
+
+    def body(attention_ref, weight_ref, *out_refs):
+        for step, out_ref in zip(steps, out_refs):
+            out_ref[...] = share_of(attention_ref, weight_ref, step, tp_size).astype(
+                out_ref.dtype
+            )
+
+    return pl.pallas_call(
+        body,
+        out_shape=[
+            jax.ShapeDtypeStruct(
+                (rows, columns // tp_size), jnp.bfloat16 if step else jnp.float32
+            )
+            for step in steps
         ],
-        out_specs=pl.BlockSpec((1, rows, width), lambda i: (i, 0, 0)),
-        out_shape=jax.ShapeDtypeStruct((tp_size, rows, width), jnp.bfloat16),
-        scratch_shapes=[pltpu.VMEM((rows, features), jnp.bfloat16)],
-        compiler_params=pltpu.CompilerParams(vmem_limit_bytes=VMEM_LIMIT),
-    )(parts, out_weight)
+        cost_estimate=pl.CostEstimate(
+            flops=2 * rows * features * len(steps) * (columns // tp_size),
+            bytes_accessed=2 * features * columns,
+            transcendentals=0,
+        ),
+        compiler_params=pltpu.CompilerParams(vmem_limit_bytes=VMEM_LIMIT),
+    )(attention, out_weight)
+
+
+def to_member(share, step, tp_size):
+    return lax.ppermute(share, "tp", [(i, (i + step) % tp_size) for i in range(tp_size)])
 
 
 def shards(queries, keys, values, out_weight):
@@ -172,11 +205,18 @@
     returned = lax.all_to_all(
         partial.reshape(heads * query_copies, rows, LANES), QUERY_AXES, 0, 0, tiled=True
     )
-    shares = project(
-        returned.reshape(-1, LANES), out_weight, heads, query_copies, rows, tp_size
-    )
-    arrived = lax.all_to_all(shares, "tp", 0, 0, tiled=True)
-    return jnp.sum(arrived.astype(jnp.float32), axis=0).astype(jnp.bfloat16)
+    far = tp_size // 2
+    near = [step for step in range(1, tp_size) if step != far]
+    attention, far_share = project_far(
+        returned.reshape(-1, LANES), out_weight, heads, query_copies, rows, far, tp_size
+    )
+    arrived = [to_member(far_share, far, tp_size)]
+    *near_shares, own_share = project_near(attention, out_weight, near + [0], tp_size)
+    arrived += [to_member(share, step, tp_size) for share, step in zip(near_shares, near)]
+    total = own_share
+    for share in arrived:
+        total = total + share.astype(jnp.float32)
+    return total.astype(jnp.bfloat16)
 
 
 def solution(mesh):

time: 90.2 us -> 88 us (0.976)
  the two profiles are of different devices: /device:TPU:1 before, /device:TPU:56 now
where the time goes in v4:
time: 88 us; the launch traced here: 86.9 us
  blocking collectives  60 us (68%)
  starting transfers between devices  11.5 us (13%)
  waiting for transfers between devices  9.01 us (10%)
  Pallas kernels  4.58 us (5%)
  other arithmetic  1.77 us (2%)
    all_to_all x1, blocking collectives, shards(): lax.all_to_all(sent_kv.reshape(heads * key_copies, rows, 2 * LANES), KEY_...  29.5 us
    all_to_all x1, blocking collectives, shards(): lax.all_to_all(sent_q.reshape(heads * query_copies, rows, LANES), QUERY_A...  16.1 us
    all_to_all x1, blocking collectives, shards(): lax.all_to_all(partial.reshape(heads * query_copies, rows, LANES), QUERY_...  14.5 us
    ppermute x3, starting transfers between devices, to_member(): lax.ppermute(share, 'tp', [(i, (i + step) % tp_size) for i in range(tp_si...  11.5 us
    ppermute x3, waiting for transfers between devices, to_member(): lax.ppermute(share, 'tp', [(i, (i + step) % tp_size) for i in range(tp_si...  9.01 us
    pallas_call x1, Pallas kernels, attend(): pl.pallas_call(body, out_shape=jax.ShapeDtypeStruct(queries.shape, querie...  3.06 us
  transfers between devices with their start and end apart: 3, of which 3 were waited for; matrix products, arithmetic and copies ran while one was open for 0% of the time, Pallas kernels for 1%

profile of v4, /device:TPU:56, one launch (start us, length us, event | category | flops | bytes accessed | tf_op | source)
XLA Modules:
  0.0 86.9 jit_solution(9394230519819222744)
XLA Ops:
  0.0 0.0 copy-start
  0.0 1.1 %pad_maximum_fusion.held = bf16[192,448]{1,0:T(8,128)(2,1)S(1)} fusion(bf16[64,448]{1,0:T(8,128)(2,1)} %param.4, bf16[64,448]{1,0:T(8,128)(2,1)} %param.6, bf16[64,448]{1,0:T(8,128)(2,1)} %param.5), kind=kLoop, calls=%fused_computation.1 | loop fusion | flops 516096 | bytes 344064 | tf_op jit(solution)/shard_map/concatenate | solution.py:52
  1.1 0.2 shard_map.46
  1.2 29.5 %all_to_all.15 = bf16[16,64,256]{2,1,0:T(8,128)(2,1)S(1)} all-to-all(bf16[16,64,256]{2,1,0:T(8,128)(2,1)S(1)} %bitcast.11), channel_id=1, replica_groups=mesh['x'=4,'yl'=2,'zh'=4,'zl'=2,'core'=2,'tp'=4] {'x','zh'}, dimensions={0} | all-to-all | bytes 1048576 | tf_op jit(solution)/shard_map/all_to_all | solution.py:199
  30.8 16.1 %all_to_all.16 = bf16[32,64,128]{2,1,0:T(8,128)(2,1)S(1)} all-to-all(bf16[32,64,128]{2,1,0:T(8,128)(2,1)S(1)} %bitcast.10), channel_id=1, replica_groups=mesh['x'=4,'yl'=2,'zh'=4,'zl'=2,'core'=2,'tp'=4] {'x','yl','zl','core'}, dimensions={0} | all-to-all | bytes 1048576 | tf_op jit(solution)/shard_map/all_to_all | solution.py:196
  46.8 3.1 %shard_map.47 = bf16[2048,128]{1,0:T(8,128)(2,1)S(1)} custom-call(bf16[2048,128]{1,0:T(8,128)(2,1)S(1)} %bitcast.8, bf16[1024,256]{1,0:T(8,128)(2,1)S(1)} %bitcast.6), custom_call_target="tpu_custom_call" | custom-call | tf_op jit(solution)/shard_map/pallas_call | solution.py:97
  49.9 14.5 %all_to_all.17 = bf16[32,64,128]{2,1,0:T(8,128)(2,1)S(1)} all-to-all(bf16[32,64,128]{2,1,0:T(8,128)(2,1)S(1)} %bitcast.9), channel_id=1, replica_groups=mesh['x'=4,'yl'=2,'zh'=4,'zl'=2,'core'=2,'tp'=4] {'x','yl','zl','core'}, dimensions={0} | all-to-all | bytes 1048576 | tf_op jit(solution)/shard_map/all_to_all | solution.py:205
  64.3 0.0 copy-done
  64.3 0.8 shard_map.48
  65.2 4.7 %collective-permute-start = (bf16[64,896]{1,0:T(8,128)(2,1)S(1)}, bf16[64,896]{1,0:T(8,128)(2,1)S(1)}, u32[]{:S(2)}, u32[]{:S(2)}) collective-permute-start(bf16[64,896]{1,0:T(8,128)(2,1)S(1)} %get-tuple-element.16), channel_id=1, source_target_pairs={{0,2},{1,3},{2,0},{3,1},{4,6},{5,7},{6,4},{7,5},{8,10},{9,11},{10,... | collective-permute-start | bytes 344072 | tf_op jit(solution)/shard_map/ppermute | solution.py:184
  69.9 0.5 shard_map.49
  70.5 4.8 %collective-permute-start.1 = (bf16[64,896]{1,0:T(8,128)(2,1)S(1)}, bf16[64,896]{1,0:T(8,128)(2,1)S(1)}, u32[]{:S(2)}, u32[]{:S(2)}) collective-permute-start(bf16[64,896]{1,0:T(8,128)(2,1)S(1)} %get-tuple-element.17), channel_id=1, source_target_pairs={{0,1},{1,2},{2,3},{3,0},{4,5},{5,6},{6,7},{7,4},{8,9},{9,10},{10,1... | collective-permute-start | bytes 344072 | tf_op jit(solution)/shard_map/ppermute | solution.py:184
  75.3 1.9 %collective-permute-start.2 = (bf16[64,896]{1,0:T(8,128)(2,1)S(1)}, bf16[64,896]{1,0:T(8,128)(2,1)S(1)}, u32[]{:S(2)}, u32[]{:S(2)}) collective-permute-start(bf16[64,896]{1,0:T(8,128)(2,1)S(1)} %get-tuple-element.18), channel_id=1, source_target_pairs={{0,3},{1,0},{2,1},{3,2},{4,7},{5,4},{6,5},{7,6},{8,11},{9,8},{10,9... | collective-permute-start | bytes 344072 | tf_op jit(solution)/shard_map/ppermute | solution.py:184
  77.2 1.0 %collective-permute-done = bf16[64,896]{1,0:T(8,128)(2,1)S(1)} collective-permute-done((bf16[64,896]{1,0:T(8,128)(2,1)S(1)}, bf16[64,896]{1,0:T(8,128)(2,1)S(1)}, u32[]{:S(2)}, u32[]{:S(2)}) %collective-permute-start) | collective-permute-done | bytes 114720 | tf_op jit(solution)/shard_map/ppermute | solution.py:184
  78.2 4.0 %collective-permute-done.1 = bf16[64,896]{1,0:T(8,128)(2,1)S(1)} collective-permute-done((bf16[64,896]{1,0:T(8,128)(2,1)S(1)}, bf16[64,896]{1,0:T(8,128)(2,1)S(1)}, u32[]{:S(2)}, u32[]{:S(2)}) %collective-permute-start.1) | collective-permute-done | bytes 114720 | tf_op jit(solution)/shard_map/ppermute | solution.py:184
  82.2 4.0 %collective-permute-done.2 = bf16[64,896]{1,0:T(8,128)(2,1)S(1)} collective-permute-done((bf16[64,896]{1,0:T(8,128)(2,1)S(1)}, bf16[64,896]{1,0:T(8,128)(2,1)S(1)}, u32[]{:S(2)}, u32[]{:S(2)}) %collective-permute-start.2) | collective-permute-done | bytes 114720 | tf_op jit(solution)/shard_map/ppermute | solution.py:184
  86.2 0.7 add_convert_fusion
Async XLA Ops:
  0.0 64.3 %copy-start = (bf16[448,3584]{1,0:T(8,128)(2,1)S(1)}, bf16[448,3584]{1,0:T(8,128)(2,1)}, u32[]{:S(2)}) copy-start(bf16[448,3584]{1,0:T(8,128)(2,1)} %weight_ref.3) | copy-start | bytes 9633796
  65.2 13.0 %collective-permute-start = (bf16[64,896]{1,0:T(8,128)(2,1)S(1)}, bf16[64,896]{1,0:T(8,128)(2,1)S(1)}, u32[]{:S(2)}, u32[]{:S(2)}) collective-permute-start(bf16[64,896]{1,0:T(8,128)(2,1)S(1)} %get-tuple-element.16), channel_id=1, source_target_pairs={{0,2},{1,3},{2,0},{3,1},{4,6},{5,7},{6,4},{7,5},{8,10},{9,11},{10,... | collective-permute-start | bytes 344072 | tf_op jit(solution)/shard_map/ppermute | solution.py:184
  70.5 11.7 %collective-permute-start.1 = (bf16[64,896]{1,0:T(8,128)(2,1)S(1)}, bf16[64,896]{1,0:T(8,128)(2,1)S(1)}, u32[]{:S(2)}, u32[]{:S(2)}) collective-permute-start(bf16[64,896]{1,0:T(8,128)(2,1)S(1)} %get-tuple-element.17), channel_id=1, source_target_pairs={{0,1},{1,2},{2,3},{3,0},{4,5},{5,6},{6,7},{7,4},{8,9},{9,10},{10,1... | collective-permute-start | bytes 344072 | tf_op jit(solution)/shard_map/ppermute | solution.py:184
  75.3 11.0 %collective-permute-start.2 = (bf16[64,896]{1,0:T(8,128)(2,1)S(1)}, bf16[64,896]{1,0:T(8,128)(2,1)S(1)}, u32[]{:S(2)}, u32[]{:S(2)}) collective-permute-start(bf16[64,896]{1,0:T(8,128)(2,1)S(1)} %get-tuple-element.18), channel_id=1, source_target_pairs={{0,3},{1,0},{2,1},{3,2},{4,7},{5,4},{6,5},{7,6},{8,11},{9,8},{10,9... | collective-permute-start | bytes 344072 | tf_op jit(solution)/shard_map/ppermute | solution.py:184

commit v5 on v4

v5 whole, which is shorter than its diff:
```python
import math

import jax
import jax.numpy as jnp
from jax import lax
from jax.experimental import pallas as pl
from jax.experimental.pallas import tpu as pltpu
from jax.sharding import Mesh, PartitionSpec as P

HEAD_DIM = 112
LANES = 128
TOTAL, TOTAL_LOW, SHIFT = HEAD_DIM, HEAD_DIM + 1, HEAD_DIM + 2
NEG_FILL = -1e30
AXES = ("x", "yl", "zh", "zl", "core", "tp")
CTX = AXES[:5]
HEAD_AXES = ("zl", "core")
QUERY_AXES = ("x", "yl")
RETURN_AXES = ("x", "yl", "zl", "core")
VMEM_LIMIT = 48 * 1024 * 1024
EXP2_SCALE = math.log2(math.e) / HEAD_DIM**0.5


def pack(queries, keys, values, heads):
    rows = queries.shape[0]
    kind = queries.dtype

    def body(held, out_ref):
        for head in range(heads):
            columns = slice(head * HEAD_DIM, (head + 1) * HEAD_DIM)
            key, value, query = (
                held[part * rows : (part + 1) * rows, columns] for part in range(3)
            )
            gap = jnp.zeros((rows, LANES - HEAD_DIM), kind)
            out_ref[head] = jnp.concatenate(
                [key, gap, value, jnp.ones_like(gap), query, gap], axis=1
            )

    return pl.pallas_call(
        body,
        out_shape=jax.ShapeDtypeStruct((heads, rows, 3 * LANES), kind),
        compiler_params=pltpu.CompilerParams(vmem_limit_bytes=VMEM_LIMIT),
    )(jnp.concatenate([keys, values, queries], axis=0))


def spread(one_head, copies):
    rows = one_head.shape[0]
    kind = one_head.dtype

    def body(one_ref, kv_out, q_out):
        kv_out[...] = one_ref[:, : 2 * LANES]
        query = one_ref[:, 2 * LANES :]
        for copy in range(copies):
            q_out[copy] = query

    return pl.pallas_call(
        body,
        out_shape=(
            jax.ShapeDtypeStruct((rows, 2 * LANES), kind),
            jax.ShapeDtypeStruct((copies, rows, LANES), kind),
        ),
        compiler_params=pltpu.CompilerParams(vmem_limit_bytes=VMEM_LIMIT),
    )(one_head)


def attend_kernel(coarse_size, steps, block, q_ref, kv_refs, out_ref):
    zh_size = lax.axis_size("zh")
    zh = lax.axis_index("zh")
    own_coarse = lax.axis_index("x") * lax.axis_size("yl") + lax.axis_index("yl")
    lane = lax.broadcasted_iota(jnp.int32, (block, LANES), 1)

    def tile(at, masked):
        start = pl.multiple_of(at * block, block)
        queries = q_ref[pl.ds(start, block), :]
        scores = []
        for step, kv_ref in zip(steps, kv_refs):
            part = lax.dot_general(
                queries,
                kv_ref[:, :LANES],
                (((1,), (1,)), ((), ())),
                preferred_element_type=jnp.float32,
            )
            if masked:
                source = lax.rem(zh + zh_size - step, zh_size)
                query_at = lax.broadcasted_iota(jnp.int32, (block, block), 0)
                key_at = lax.broadcasted_iota(jnp.int32, (block, block), 1)
                part = jnp.where(
                    query_at - key_at + (zh - source) * block >= 0, part, NEG_FILL
                )
            scores.append(part)
        scores = jnp.concatenate(scores, axis=1)
        top = jnp.max(scores, axis=1, keepdims=True) * EXP2_SCALE
        shift = top.astype(jnp.bfloat16).astype(jnp.float32)
        weights = jnp.exp2(scores * EXP2_SCALE - shift).astype(jnp.bfloat16)
        weighted = jnp.zeros((block, LANES), jnp.float32)
        for part, kv_ref in enumerate(kv_refs):
            weighted = weighted + jnp.dot(
                weights[:, part * block : (part + 1) * block],
                kv_ref[:, LANES:],
                preferred_element_type=jnp.float32,
            )
        rounded = weighted.astype(jnp.bfloat16).astype(jnp.float32)
        weighted = jnp.where(lane == TOTAL_LOW, weighted - rounded, weighted)
        weighted = jnp.where(lane == SHIFT, shift, weighted)
        out_ref[pl.ds(start, block), :] = weighted.astype(out_ref.dtype)

    for at in range(coarse_size):

        @pl.when(at > own_coarse)
        def _(at=at):
            tile(at, False)

        @pl.when(at == own_coarse)
        def _(at=at):
            tile(at, True)

        @pl.when(at < own_coarse)
        def _(at=at):
            out_ref[at * block : (at + 1) * block, :] = jnp.where(
                lane == SHIFT, NEG_FILL, 0.0
            ).astype(out_ref.dtype)


def attend(queries, keys_values, steps, coarse_size):
    block = queries.shape[0] // coarse_size

    def body(q_ref, *refs):
        attend_kernel(coarse_size, steps, block, q_ref, refs[:-1], refs[-1])

    return pl.pallas_call(
        body,
        out_shape=jax.ShapeDtypeStruct(queries.shape, queries.dtype),
        compiler_params=pltpu.CompilerParams(vmem_limit_bytes=VMEM_LIMIT),
    )(queries, *keys_values)


def combine(parts_ref, attention_ref, heads, groups, rows):
    for head in range(heads):
        parts = [
            parts_ref[
                (group * heads + head) * rows : (group * heads + head + 1) * rows, :
            ].astype(jnp.float32)
            for group in range(groups)
        ]
        shifts = [part[:, SHIFT : SHIFT + 1] for part in parts]
        top = shifts[0]
        for shift in shifts[1:]:
            top = jnp.maximum(top, shift)
        mixed = jnp.zeros_like(parts[0])
        for shift, part in zip(shifts, parts):
            mixed = mixed + jnp.exp2(shift - top) * part
        row_total = mixed[:, TOTAL : TOTAL + 1] + mixed[:, TOTAL_LOW : TOTAL_LOW + 1]
        attention_ref[:, head * HEAD_DIM : (head + 1) * HEAD_DIM] = (
            mixed[:, :HEAD_DIM] / row_total
        ).astype(attention_ref.dtype)


def share_of(attention_ref, weight_ref, step, tp_size):
    width = weight_ref.shape[1] // tp_size
    member = lax.rem(lax.axis_index("tp") + step, tp_size)
    columns = pl.ds(pl.multiple_of(member * width, LANES), width)
    return jnp.dot(
        attention_ref[...], weight_ref[:, columns], preferred_element_type=jnp.float32
    )


def project_far(parts, out_weight, heads, groups, rows, step, tp_size):
    features, columns = out_weight.shape

    def body(parts_ref, weight_ref, attention_ref, far_ref):
        combine(parts_ref, attention_ref, heads, groups, rows)
        far_ref[...] = share_of(attention_ref, weight_ref, step, tp_size).astype(far_ref.dtype)

    return pl.pallas_call(
        body,
        out_shape=(
            jax.ShapeDtypeStruct((rows, features), jnp.bfloat16),
            jax.ShapeDtypeStruct((rows, columns // tp_size), jnp.bfloat16),
        ),
        cost_estimate=pl.CostEstimate(
            flops=2 * rows * features * columns // tp_size,
            bytes_accessed=2 * features * columns,
            transcendentals=0,
        ),
        compiler_params=pltpu.CompilerParams(vmem_limit_bytes=VMEM_LIMIT),
    )(parts, out_weight)


def project_near(attention, out_weight, steps, tp_size):
    rows, features = attention.shape
    columns = out_weight.shape[1]

    def body(attention_ref, weight_ref, *out_refs):
        for step, out_ref in zip(steps, out_refs):
            out_ref[...] = share_of(attention_ref, weight_ref, step, tp_size).astype(
                out_ref.dtype
            )

    return pl.pallas_call(
        body,
        out_shape=[
            jax.ShapeDtypeStruct(
                (rows, columns // tp_size), jnp.bfloat16 if step else jnp.float32
            )
            for step in steps
        ],
        cost_estimate=pl.CostEstimate(
            flops=2 * rows * features * len(steps) * (columns // tp_size),
            bytes_accessed=2 * features * columns,
            transcendentals=0,
        ),
        compiler_params=pltpu.CompilerParams(vmem_limit_bytes=VMEM_LIMIT),
    )(attention, out_weight)


def to_member(share, step, tp_size):
    return lax.ppermute(share, "tp", [(i, (i + step) % tp_size) for i in range(tp_size)])


def shards(queries, keys, values, out_weight):
    rows, features = queries.shape
    heads = features // HEAD_DIM
    coarse_size = lax.axis_size("x") * lax.axis_size("yl")
    zh_size = lax.axis_size("zh")
    tp_size = lax.axis_size("tp")

    one_head = lax.all_to_all(
        pack(queries, keys, values, heads), HEAD_AXES, 0, 0, tiled=True
    ).reshape(heads * rows, 3 * LANES)
    own_kv, sent_q = spread(one_head, coarse_size)
    steps = [0, zh_size // 2] + [step for step in range(1, zh_size) if step != zh_size // 2]
    got_kv = [own_kv] + [
        lax.ppermute(own_kv, "zh", [(i, (i + step) % zh_size) for i in range(zh_size)])
        for step in steps[1:]
    ]
    got_q = lax.all_to_all(sent_q, QUERY_AXES, 0, 0, tiled=True)
    partial = attend(got_q.reshape(-1, LANES), got_kv, steps, coarse_size)
    returned = lax.all_to_all(
        partial.reshape(coarse_size * heads, rows, LANES), RETURN_AXES, 0, 0, tiled=True
    )
    far = tp_size // 2
    near = [step for step in range(1, tp_size) if step != far]
    attention, far_share = project_far(
        returned.reshape(-1, LANES), out_weight, heads, coarse_size, rows, far, tp_size
    )
    arrived = [to_member(far_share, far, tp_size)]
    *near_shares, own_share = project_near(attention, out_weight, near + [0], tp_size)
    arrived += [to_member(share, step, tp_size) for share, step in zip(near_shares, near)]
    total = own_share
    for share in arrived:
        total = total + share.astype(jnp.float32)
    return total.astype(jnp.bfloat16)


def solution(mesh):
    split = Mesh(mesh.devices.reshape(4, 2, 4, 2, 2, 4), AXES)
    placed = (P(CTX, "tp"), P(CTX, "tp"), P(CTX, "tp"), P("tp", None))
    return jax.shard_map(
        shards, mesh=split, in_specs=placed, out_specs=P(CTX, "tp"), check_vma=False
    )
```

time: 88 us -> 88.7 us (level)
  blocking collectives: 60 us -> 25.1 us
  starting transfers between devices: 11.5 us -> 34 us
  waiting for transfers between devices: 9.01 us -> 15.5 us
  local copies, waits for them, and re-layouts: 0.01 us -> 3.93 us
  Pallas kernels: 4.58 us -> 7.05 us
    all_to_all x3 -> x2, blocking collectives: 60 us -> 25.1 us  [the longest x1 16.3 us: shards(): lax.all_to_all(partial.reshape(coarse_size * heads, rows, LANES), RETURN_...]
    ppermute x0 -> x3, starting transfers between devices: none -> 16.7 us  [shards(): lax.ppermute(own_kv, 'zh', [(i, (i + step) % zh_size) for i in range(zh_s...]
    ppermute x0 -> x3, waiting for transfers between devices: none -> 6.51 us  [shards(): lax.ppermute(own_kv, 'zh', [(i, (i + step) % zh_size) for i in range(zh_s...]
    all_to_all x0 -> x1, starting transfers between devices: none -> 5.76 us  [shards(): got_q = lax.all_to_all(sent_q, QUERY_AXES, 0, 0, tiled=True)]
    unnamed x2 -> x12, local copies, waits for them, and re-layouts: 0.01 us -> 3.93 us
    pallas_call x1, Pallas kernels: 3.06 us -> 5.47 us  [attend(): pl.pallas_call(body, out_shape=jax.ShapeDtypeStruct(queries.shape, querie...]
  transfers between devices with their start and end apart: 3 -> 7, of which waited for: 3 -> 4; matrix products, arithmetic and copies ran while one was open for 0% -> 0% of each run, Pallas kernels for 1% -> 1%
where the time goes in v5:
time: 88.7 us; the launch traced here: 87.4 us
  starting transfers between devices  34 us (38%)
  blocking collectives  25.1 us (28%)
  waiting for transfers between devices  15.5 us (17%)
  Pallas kernels  7.05 us (8%)
  local copies, waits for them, and re-layouts  3.93 us (4%)
  other arithmetic  1.77 us (2%)
    ppermute x3, starting transfers between devices, shards(): lax.ppermute(own_kv, 'zh', [(i, (i + step) % zh_size) for i in range(zh_s...  16.7 us
    all_to_all x1, blocking collectives, shards(): lax.all_to_all(partial.reshape(coarse_size * heads, rows, LANES), RETURN_...  16.3 us
    ppermute x3, starting transfers between devices, to_member(): lax.ppermute(share, 'tp', [(i, (i + step) % tp_size) for i in range(tp_si...  11.5 us
    ppermute x3, waiting for transfers between devices, to_member(): lax.ppermute(share, 'tp', [(i, (i + step) % tp_size) for i in range(tp_si...  9.01 us
    all_to_all x1, blocking collectives, shards(): lax.all_to_all(pack(queries, keys, values, heads), HEAD_AXES, 0, 0, tiled...  8.78 us
    ppermute x3, waiting for transfers between devices, shards(): lax.ppermute(own_kv, 'zh', [(i, (i + step) % zh_size) for i in range(zh_s...  6.51 us
    all_to_all x1, starting transfers between devices, shards(): got_q = lax.all_to_all(sent_q, QUERY_AXES, 0, 0, tiled=True)  5.76 us
    pallas_call x1, Pallas kernels, attend(): pl.pallas_call(body, out_shape=jax.ShapeDtypeStruct(queries.shape, querie...  5.47 us
  transfers between devices with their start and end apart: 7, of which 4 were waited for; matrix products, arithmetic and copies ran while one was open for 0% of the time, Pallas kernels for 1%

profile of v5, /device:TPU:56, one launch (start us, length us, event | category | flops | bytes accessed | tf_op | source)
XLA Modules:
  0.0 87.4 jit_solution(5234402866788480639)
XLA Ops:
  0.0 1.1 %pad_maximum_fusion.held = bf16[192,448]{1,0:T(8,128)(2,1)S(1)} fusion(bf16[64,448]{1,0:T(8,128)(2,1)} %param.4, bf16[64,448]{1,0:T(8,128)(2,1)} %param.6, bf16[64,448]{1,0:T(8,128)(2,1)} %param.5), kind=kLoop, calls=%fused_computation.1 | loop fusion | flops 516096 | bytes 344064 | tf_op jit(solution)/shard_map/concatenate | solution.py:42
  1.1 0.1 shard_map.46
  1.2 8.8 %all_to_all.15 = bf16[4,64,384]{2,1,0:T(8,128)(2,1)S(1)} all-to-all(bf16[4,64,384]{2,1,0:T(8,128)(2,1)S(1)} %shard_map.46), channel_id=1, replica_groups=mesh['x'=4,'yl'=2,'zh'=4,'zl'=2,'core'=2,'tp'=4] {'zl','core'}, dimensions={0} | all-to-all | bytes 393216 | tf_op jit(solution)/shard_map/all_to_all | solution.py:226
  10.1 0.8 copy-done.1
  10.9 5.8 %all-to-all-start.1 = ((bf16[8,256,128]{2,1,0:T(8,128)(2,1)}), bf16[8,256,128]{2,1,0:T(8,128)(2,1)}, u32[]{:S(2)}, u32[]{:S(2)}) async-start(bf16[8,256,128]{2,1,0:T(8,128)(2,1)} %copy-done.1), calls=%async_computation.1 | async-start | bytes 1048576 | tf_op jit(solution)/shard_map/all_to_all | solution.py:235
  16.6 10.0 %collective-permute-start.2 = (bf16[256,256]{1,0:T(8,128)(2,1)S(1)}, bf16[256,256]{1,0:T(8,128)(2,1)S(1)}, u32[]{:S(2)}, u32[]{:S(2)}) collective-permute-start(bf16[256,256]{1,0:T(8,128)(2,1)S(1)} %get-tuple-element.13.refs_0_), channel_id=1, source_target_pairs={{0,48},{16,0},{32,16},{48,32},{1,49},{17,1},{33,17},{49,33},{2,50}... | collective-permute-start | bytes 393224 | tf_op jit(solution)/shard_map/ppermute | solution.py:232
  26.7 1.9 %collective-permute-start.1 = (bf16[256,256]{1,0:T(8,128)(2,1)S(1)}, bf16[256,256]{1,0:T(8,128)(2,1)S(1)}, u32[]{:S(2)}, u32[]{:S(2)}) collective-permute-start(bf16[256,256]{1,0:T(8,128)(2,1)S(1)} %get-tuple-element.13.refs_0_), channel_id=1, source_target_pairs={{0,16},{16,32},{32,48},{48,0},{1,17},{17,33},{33,49},{49,1},{2,18}... | collective-permute-start | bytes 393224 | tf_op jit(solution)/shard_map/ppermute | solution.py:232
  28.6 4.8 %collective-permute-start = (bf16[256,256]{1,0:T(8,128)(2,1)S(1)}, bf16[256,256]{1,0:T(8,128)(2,1)S(1)}, u32[]{:S(2)}, u32[]{:S(2)}) collective-permute-start(bf16[256,256]{1,0:T(8,128)(2,1)S(1)} %get-tuple-element.13.refs_0_), channel_id=1, source_target_pairs={{0,32},{16,48},{32,0},{48,16},{1,33},{17,49},{33,1},{49,17},{2,34}... | collective-permute-start | bytes 393224 | tf_op jit(solution)/shard_map/ppermute | solution.py:232
  33.4 6.5 %collective-permute-done.1.refs_2_ = bf16[256,256]{1,0:T(8,128)(2,1)S(1)} collective-permute-done((bf16[256,256]{1,0:T(8,128)(2,1)S(1)}, bf16[256,256]{1,0:T(8,128)(2,1)S(1)}, u32[]{:S(2)}, u32[]{:S(2)}) %collective-permute-start.1) | collective-permute-done | bytes 131104 | tf_op jit(solution)/shard_map/ppermute | solution.py:232
  39.9 0.7 copy-done.2
  40.6 0.7 copy-done.4
  41.3 0.9 %copy-done.3 = bf16[256,256]{1,0:T(8,128)(2,1)S(1)} copy-done((bf16[256,256]{1,0:T(8,128)(2,1)S(1)}, bf16[256,256]{1,0:T(8,128)(2,1)}, u32[]{:S(2)}) %copy-start.3) | copy-done | bytes 131096
  42.2 0.9 %copy-done.5 = bf16[256,256]{1,0:T(8,128)(2,1)S(1)} copy-done((bf16[256,256]{1,0:T(8,128)(2,1)S(1)}, bf16[256,256]{1,0:T(8,128)(2,1)}, u32[]{:S(2)}) %copy-start.5) | copy-done | bytes 131096
  43.1 5.5 %shard_map.48 = bf16[2048,128]{1,0:T(8,128)(2,1)S(1)} custom-call(bf16[2048,128]{1,0:T(8,128)(2,1)} %bitcast.1.q_ref, bf16[256,256]{1,0:T(8,128)(2,1)S(1)} %get-tuple-element.13.refs_0_, bf16[256,256]{1,0:T(8,128)(2,1)S(1)} %copy-done.5, bf16[256,256]{1,0:T(8,128)(2,1)S(1)} %copy-done.3, bf16[256,256]{1,0:T(8,128)(2,1)S(1)} %collective-permute-done.2.refs_3_), custom_call_target="tpu_custom_call" | custom-call | tf_op jit(solution)/shard_map/pallas_call | solution.py:129
  48.6 16.3 %all_to_all.16 = bf16[32,64,128]{2,1,0:T(8,128)(2,1)S(1)} all-to-all(bf16[32,64,128]{2,1,0:T(8,128)(2,1)S(1)} %bitcast.4), channel_id=1, replica_groups=mesh['x'=4,'yl'=2,'zh'=4,'zl'=2,'core'=2,'tp'=4] {'x','yl','zl','core'}, dimensions={0} | all-to-all | bytes 1048576 | tf_op jit(solution)/shard_map/all_to_all | solution.py:237
  64.9 0.8 shard_map.49
  65.7 4.7 %collective-permute-start.3 = (bf16[64,896]{1,0:T(8,128)(2,1)S(1)}, bf16[64,896]{1,0:T(8,128)(2,1)S(1)}, u32[]{:S(2)}, u32[]{:S(2)}) collective-permute-start(bf16[64,896]{1,0:T(8,128)(2,1)S(1)} %get-tuple-element.16), channel_id=1, source_target_pairs={{0,2},{1,3},{2,0},{3,1},{4,6},{5,7},{6,4},{7,5},{8,10},{9,11},{10,... | collective-permute-start | bytes 344072 | tf_op jit(solution)/shard_map/ppermute | solution.py:216
  70.4 0.5 shard_map.50
  70.9 4.8 %collective-permute-start.4 = (bf16[64,896]{1,0:T(8,128)(2,1)S(1)}, bf16[64,896]{1,0:T(8,128)(2,1)S(1)}, u32[]{:S(2)}, u32[]{:S(2)}) collective-permute-start(bf16[64,896]{1,0:T(8,128)(2,1)S(1)} %get-tuple-element.17), channel_id=1, source_target_pairs={{0,1},{1,2},{2,3},{3,0},{4,5},{5,6},{6,7},{7,4},{8,9},{9,10},{10,1... | collective-permute-start | bytes 344072 | tf_op jit(solution)/shard_map/ppermute | solution.py:216
  75.8 1.9 %collective-permute-start.5 = (bf16[64,896]{1,0:T(8,128)(2,1)S(1)}, bf16[64,896]{1,0:T(8,128)(2,1)S(1)}, u32[]{:S(2)}, u32[]{:S(2)}) collective-permute-start(bf16[64,896]{1,0:T(8,128)(2,1)S(1)} %get-tuple-element.18), channel_id=1, source_target_pairs={{0,3},{1,0},{2,1},{3,2},{4,7},{5,4},{6,5},{7,6},{8,11},{9,8},{10,9... | collective-permute-start | bytes 344072 | tf_op jit(solution)/shard_map/ppermute | solution.py:216
  77.7 1.0 %collective-permute-done.3 = bf16[64,896]{1,0:T(8,128)(2,1)S(1)} collective-permute-done((bf16[64,896]{1,0:T(8,128)(2,1)S(1)}, bf16[64,896]{1,0:T(8,128)(2,1)S(1)}, u32[]{:S(2)}, u32[]{:S(2)}) %collective-permute-start.3) | collective-permute-done | bytes 114720 | tf_op jit(solution)/shard_map/ppermute | solution.py:216
  78.7 4.0 %collective-permute-done.4 = bf16[64,896]{1,0:T(8,128)(2,1)S(1)} collective-permute-done((bf16[64,896]{1,0:T(8,128)(2,1)S(1)}, bf16[64,896]{1,0:T(8,128)(2,1)S(1)}, u32[]{:S(2)}, u32[]{:S(2)}) %collective-permute-start.4) | collective-permute-done | bytes 114720 | tf_op jit(solution)/shard_map/ppermute | solution.py:216
  82.7 4.0 %collective-permute-done.5 = bf16[64,896]{1,0:T(8,128)(2,1)S(1)} collective-permute-done((bf16[64,896]{1,0:T(8,128)(2,1)S(1)}, bf16[64,896]{1,0:T(8,128)(2,1)S(1)}, u32[]{:S(2)}, u32[]{:S(2)}) %collective-permute-start.5) | collective-permute-done | bytes 114720 | tf_op jit(solution)/shard_map/ppermute | solution.py:216
  86.7 0.7 add_convert_fusion
  (11 shorter events, 0.1 us)
Async XLA Ops:
  0.0 64.8 %copy-start = (bf16[448,3584]{1,0:T(8,128)(2,1)S(1)}, bf16[448,3584]{1,0:T(8,128)(2,1)}, u32[]{:S(2)}) copy-start(bf16[448,3584]{1,0:T(8,128)(2,1)} %weight_ref.3) | copy-start | bytes 9633796
  10.1 0.8 copy-start.1
  10.9 30.4 %all-to-all-start.1 = ((bf16[8,256,128]{2,1,0:T(8,128)(2,1)}), bf16[8,256,128]{2,1,0:T(8,128)(2,1)}, u32[]{:S(2)}, u32[]{:S(2)}) async-start(bf16[8,256,128]{2,1,0:T(8,128)(2,1)} %copy-done.1), calls=%async_computation.1 | async-start | bytes 1048576 | tf_op jit(solution)/shard_map/all_to_all | solution.py:235
  16.6 16.8 %collective-permute-start.2 = (bf16[256,256]{1,0:T(8,128)(2,1)S(1)}, bf16[256,256]{1,0:T(8,128)(2,1)S(1)}, u32[]{:S(2)}, u32[]{:S(2)}) collective-permute-start(bf16[256,256]{1,0:T(8,128)(2,1)S(1)} %get-tuple-element.13.refs_0_), channel_id=1, source_target_pairs={{0,48},{16,0},{32,16},{48,32},{1,49},{17,1},{33,17},{49,33},{2,50}... | collective-permute-start | bytes 393224 | tf_op jit(solution)/shard_map/ppermute | solution.py:232
  26.7 13.3 %collective-permute-start.1 = (bf16[256,256]{1,0:T(8,128)(2,1)S(1)}, bf16[256,256]{1,0:T(8,128)(2,1)S(1)}, u32[]{:S(2)}, u32[]{:S(2)}) collective-permute-start(bf16[256,256]{1,0:T(8,128)(2,1)S(1)} %get-tuple-element.13.refs_0_), channel_id=1, source_target_pairs={{0,16},{16,32},{32,48},{48,0},{1,17},{17,33},{33,49},{49,1},{2,18}... | collective-permute-start | bytes 393224 | tf_op jit(solution)/shard_map/ppermute | solution.py:232
  28.6 12.0 %collective-permute-start = (bf16[256,256]{1,0:T(8,128)(2,1)S(1)}, bf16[256,256]{1,0:T(8,128)(2,1)S(1)}, u32[]{:S(2)}, u32[]{:S(2)}) collective-permute-start(bf16[256,256]{1,0:T(8,128)(2,1)S(1)} %get-tuple-element.13.refs_0_), channel_id=1, source_target_pairs={{0,32},{16,48},{32,0},{48,16},{1,33},{17,49},{33,1},{49,17},{2,34}... | collective-permute-start | bytes 393224 | tf_op jit(solution)/shard_map/ppermute | solution.py:232
  39.9 0.7 copy-start.2
  40.6 0.7 copy-start.4
  41.3 0.9 %copy-start.3 = (bf16[256,256]{1,0:T(8,128)(2,1)S(1)}, bf16[256,256]{1,0:T(8,128)(2,1)}, u32[]{:S(2)}) copy-start(bf16[256,256]{1,0:T(8,128)(2,1)} %copy-done.2) | copy-start | bytes 393220
  42.2 0.9 %copy-start.5 = (bf16[256,256]{1,0:T(8,128)(2,1)S(1)}, bf16[256,256]{1,0:T(8,128)(2,1)}, u32[]{:S(2)}) copy-start(bf16[256,256]{1,0:T(8,128)(2,1)} %copy-done.4) | copy-start | bytes 393220
  65.7 13.0 %collective-permute-start.3 = (bf16[64,896]{1,0:T(8,128)(2,1)S(1)}, bf16[64,896]{1,0:T(8,128)(2,1)S(1)}, u32[]{:S(2)}, u32[]{:S(2)}) collective-permute-start(bf16[64,896]{1,0:T(8,128)(2,1)S(1)} %get-tuple-element.16), channel_id=1, source_target_pairs={{0,2},{1,3},{2,0},{3,1},{4,6},{5,7},{6,4},{7,5},{8,10},{9,11},{10,... | collective-permute-start | bytes 344072 | tf_op jit(solution)/shard_map/ppermute | solution.py:216
  70.9 11.7 %collective-permute-start.4 = (bf16[64,896]{1,0:T(8,128)(2,1)S(1)}, bf16[64,896]{1,0:T(8,128)(2,1)S(1)}, u32[]{:S(2)}, u32[]{:S(2)}) collective-permute-start(bf16[64,896]{1,0:T(8,128)(2,1)S(1)} %get-tuple-element.17), channel_id=1, source_target_pairs={{0,1},{1,2},{2,3},{3,0},{4,5},{5,6},{6,7},{7,4},{8,9},{9,10},{10,1... | collective-permute-start | bytes 344072 | tf_op jit(solution)/shard_map/ppermute | solution.py:216
  75.8 11.0 %collective-permute-start.5 = (bf16[64,896]{1,0:T(8,128)(2,1)S(1)}, bf16[64,896]{1,0:T(8,128)(2,1)S(1)}, u32[]{:S(2)}, u32[]{:S(2)}) collective-permute-start(bf16[64,896]{1,0:T(8,128)(2,1)S(1)} %get-tuple-element.18), channel_id=1, source_target_pairs={{0,3},{1,0},{2,1},{3,2},{4,7},{5,4},{6,5},{7,6},{8,11},{9,8},{10,9... | collective-permute-start | bytes 344072 | tf_op jit(solution)/shard_map/ppermute | solution.py:216

commit v6 on v5

--- a/solution.py
+++ b/solution.py
@@ -17,6 +17,8 @@
 QUERY_AXES = ("x", "yl")
 RETURN_AXES = ("x", "yl", "zl", "core")
 VMEM_LIMIT = 48 * 1024 * 1024
+VMEM_MOST = 58 * 1024 * 1024
+VMEM_WHOLE = 63 * 1024 * 1024
 EXP2_SCALE = math.log2(math.e) / HEAD_DIM**0.5
 
 
@@ -58,7 +60,7 @@
             jax.ShapeDtypeStruct((rows, 2 * LANES), kind),
             jax.ShapeDtypeStruct((copies, rows, LANES), kind),
         ),
-        compiler_params=pltpu.CompilerParams(vmem_limit_bytes=VMEM_LIMIT),
+        compiler_params=pltpu.CompilerParams(vmem_limit_bytes=VMEM_WHOLE),
     )(one_head)
 
 
@@ -103,21 +105,32 @@
         weighted = jnp.where(lane == SHIFT, shift, weighted)
         out_ref[pl.ds(start, block), :] = weighted.astype(out_ref.dtype)
 
-    for at in range(coarse_size):
-
-        @pl.when(at > own_coarse)
-        def _(at=at):
-            tile(at, False)
-
-        @pl.when(at == own_coarse)
-        def _(at=at):
-            tile(at, True)
-
-        @pl.when(at < own_coarse)
-        def _(at=at):
-            out_ref[at * block : (at + 1) * block, :] = jnp.where(
-                lane == SHIFT, NEG_FILL, 0.0
-            ).astype(out_ref.dtype)
+    def empty(at, _):
+        start = pl.multiple_of(at * block, block)
+        out_ref[pl.ds(start, block), :] = jnp.where(lane == SHIFT, NEG_FILL, 0.0).astype(
+            out_ref.dtype
+        )
+        return 0
+
+    def pair(count, first):
+        tile(first + 2 * count, False)
+        tile(first + 2 * count + 1, False)
+        return first
+
+    lax.fori_loop(0, own_coarse, empty, 0)
+    later = coarse_size - 1 - own_coarse
+    odd = lax.rem(later, 2)
+
+    @pl.when(odd == 1)
+    def _():
+        tile(own_coarse, True)
+        tile(own_coarse + 1, False)
+
+    @pl.when(odd == 0)
+    def _():
+        tile(own_coarse, True)
+
+    lax.fori_loop(0, later // 2, pair, own_coarse + 1 + odd)
 
 
 def attend(queries, keys_values, steps, coarse_size):
@@ -129,7 +142,7 @@
     return pl.pallas_call(
         body,
         out_shape=jax.ShapeDtypeStruct(queries.shape, queries.dtype),
-        compiler_params=pltpu.CompilerParams(vmem_limit_bytes=VMEM_LIMIT),
+        compiler_params=pltpu.CompilerParams(vmem_limit_bytes=VMEM_MOST),
     )(queries, *keys_values)
 
 

time: 88.7 us -> 89 us (level)
  local copies, waits for them, and re-layouts: 3.93 us -> 0.63 us
  Pallas kernels: 7.05 us -> 9.18 us
    unnamed x12 -> x6, local copies, waits for them, and re-layouts: 3.93 us -> 0.63 us
    pallas_call x1, Pallas kernels: 0.08 us -> 1.79 us  [spread(): pl.pallas_call(body, out_shape=(jax.ShapeDtypeStruct((rows, 2 * LANES), k...]
where the time goes in v6:
time: 89 us; the launch traced here: 87.6 us
  starting transfers between devices  34.6 us (39%)
  blocking collectives  25.7 us (29%)
  waiting for transfers between devices  15.7 us (18%)
  Pallas kernels  9.18 us (10%)
  other arithmetic  1.62 us (2%)
    ppermute x3, starting transfers between devices, shards(): lax.ppermute(own_kv, 'zh', [(i, (i + step) % zh_size) for i in range(zh_s...  17.2 us
    all_to_all x1, blocking collectives, shards(): lax.all_to_all(partial.reshape(coarse_size * heads, rows, LANES), RETURN_...  16.8 us
    ppermute x3, starting transfers between devices, to_member(): lax.ppermute(share, 'tp', [(i, (i + step) % tp_size) for i in range(tp_si...  11.5 us
    ppermute x3, waiting for transfers between devices, to_member(): lax.ppermute(share, 'tp', [(i, (i + step) % tp_size) for i in range(tp_si...  9.01 us
    all_to_all x1, blocking collectives, shards(): lax.all_to_all(pack(queries, keys, values, heads), HEAD_AXES, 0, 0, tiled...  8.88 us
    ppermute x3, waiting for transfers between devices, shards(): lax.ppermute(own_kv, 'zh', [(i, (i + step) % zh_size) for i in range(zh_s...  6.71 us
    all_to_all x1, starting transfers between devices, shards(): got_q = lax.all_to_all(sent_q, QUERY_AXES, 0, 0, tiled=True)  6.02 us
    pallas_call x1, Pallas kernels, attend(): pl.pallas_call(body, out_shape=jax.ShapeDtypeStruct(queries.shape, querie...  5.89 us
  transfers between devices with their start and end apart: 7, of which 4 were waited for; matrix products, arithmetic and copies ran while one was open for 0% of the time, Pallas kernels for 1%

profile of v6, /device:TPU:56, one launch (start us, length us, event | category | flops | bytes accessed | tf_op | source)
XLA Modules:
  0.0 87.6 jit_solution(15476193343539341312)
XLA Ops:
  0.0 0.9 %pad_maximum_fusion.held = bf16[192,448]{1,0:T(8,128)(2,1)S(1)} fusion(bf16[64,448]{1,0:T(8,128)(2,1)} %param.4, bf16[64,448]{1,0:T(8,128)(2,1)} %param.6, bf16[64,448]{1,0:T(8,128)(2,1)} %param.5), kind=kLoop, calls=%fused_computation.1 | loop fusion | flops 516096 | bytes 344064 | tf_op jit(solution)/shard_map/concatenate | solution.py:44
  0.9 0.1 shard_map.46
  1.1 8.9 %all_to_all.15 = bf16[4,64,384]{2,1,0:T(8,128)(2,1)} all-to-all(bf16[4,64,384]{2,1,0:T(8,128)(2,1)S(1)} %shard_map.46), channel_id=1, replica_groups=mesh['x'=4,'yl'=2,'zh'=4,'zl'=2,'core'=2,'tp'=4] {'zl','core'}, dimensions={0} | all-to-all | bytes 393216 | tf_op jit(solution)/shard_map/all_to_all | solution.py:239
  10.0 1.8 %shard_map.47 = (bf16[256,256]{1,0:T(8,128)(2,1)}, bf16[8,256,128]{2,1,0:T(8,128)(2,1)}) custom-call(bf16[256,384]{1,0:T(8,128)(2,1)} %bitcast.6), custom_call_target="tpu_custom_call" | custom-call | tf_op jit(solution)/shard_map/pallas_call | solution.py:57
  11.8 6.0 %all-to-all-start.1 = ((bf16[8,256,128]{2,1,0:T(8,128)(2,1)}), bf16[8,256,128]{2,1,0:T(8,128)(2,1)}, u32[]{:S(2)}, u32[]{:S(2)}) async-start(bf16[8,256,128]{2,1,0:T(8,128)(2,1)} %get-tuple-element.12), calls=%async_computation.1 | async-start | bytes 1048576 | tf_op jit(solution)/shard_map/all_to_all | solution.py:248
  17.8 10.4 %collective-permute-start.2 = (bf16[256,256]{1,0:T(8,128)(2,1)}, bf16[256,256]{1,0:T(8,128)(2,1)S(1)}, u32[]{:S(2)}, u32[]{:S(2)}) collective-permute-start(bf16[256,256]{1,0:T(8,128)(2,1)} %get-tuple-element.13.refs_0_), channel_id=1, source_target_pairs={{0,48},{16,0},{32,16},{48,32},{1,49},{17,1},{33,17},{49,33},{2,50}... | collective-permute-start | bytes 393224 | tf_op jit(solution)/shard_map/ppermute | solution.py:245
  28.2 1.9 %collective-permute-start.1 = (bf16[256,256]{1,0:T(8,128)(2,1)}, bf16[256,256]{1,0:T(8,128)(2,1)S(1)}, u32[]{:S(2)}, u32[]{:S(2)}) collective-permute-start(bf16[256,256]{1,0:T(8,128)(2,1)} %get-tuple-element.13.refs_0_), channel_id=1, source_target_pairs={{0,16},{16,32},{32,48},{48,0},{1,17},{17,33},{33,49},{49,1},{2,18}... | collective-permute-start | bytes 393224 | tf_op jit(solution)/shard_map/ppermute | solution.py:245
  30.2 4.8 %collective-permute-start = (bf16[256,256]{1,0:T(8,128)(2,1)}, bf16[256,256]{1,0:T(8,128)(2,1)}, u32[]{:S(2)}, u32[]{:S(2)}) collective-permute-start(bf16[256,256]{1,0:T(8,128)(2,1)} %get-tuple-element.13.refs_0_), channel_id=1, source_target_pairs={{0,32},{16,48},{32,0},{48,16},{1,33},{17,49},{33,1},{49,17},{2,34}... | collective-permute-start | bytes 393224 | tf_op jit(solution)/shard_map/ppermute | solution.py:245
  35.0 0.0 collective-permute-done.2.refs_3_
  35.0 6.7 %collective-permute-done.1.refs_2_ = bf16[256,256]{1,0:T(8,128)(2,1)S(1)} collective-permute-done((bf16[256,256]{1,0:T(8,128)(2,1)}, bf16[256,256]{1,0:T(8,128)(2,1)S(1)}, u32[]{:S(2)}, u32[]{:S(2)}) %collective-permute-start.1) | collective-permute-done | bytes 131104 | tf_op jit(solution)/shard_map/ppermute | solution.py:245
  41.7 0.0 collective-permute-done.refs_1_
  41.7 0.0 all-to-all-done.1
  41.7 0.6 copy-done.2
  42.3 5.9 %shard_map.48 = bf16[2048,128]{1,0:T(8,128)(2,1)} custom-call(bf16[2048,128]{1,0:T(8,128)(2,1)} %bitcast.1.q_ref, bf16[256,256]{1,0:T(8,128)(2,1)} %get-tuple-element.13.refs_0_, bf16[256,256]{1,0:T(8,128)(2,1)} %collective-permute-done.refs_1_, bf16[256,256]{1,0:T(8,128)(2,1)} %copy-done.2, bf16[256,256]{1,0:T(8,128)(2,1)} %copy-done.1), custom_call_target="tpu_custom_call" | custom-call | tf_op jit(solution)/shard_map/pallas_call | solution.py:142
  48.2 16.8 %all_to_all.16 = bf16[32,64,128]{2,1,0:T(8,128)(2,1)S(1)} all-to-all(bf16[32,64,128]{2,1,0:T(8,128)(2,1)} %bitcast.5), channel_id=1, replica_groups=mesh['x'=4,'yl'=2,'zh'=4,'zl'=2,'core'=2,'tp'=4] {'x','yl','zl','core'}, dimensions={0} | all-to-all | bytes 1048576 | tf_op jit(solution)/shard_map/all_to_all | solution.py:250
  65.0 0.8 shard_map.49
  65.9 4.7 %collective-permute-start.3 = (bf16[64,896]{1,0:T(8,128)(2,1)S(1)}, bf16[64,896]{1,0:T(8,128)(2,1)S(1)}, u32[]{:S(2)}, u32[]{:S(2)}) collective-permute-start(bf16[64,896]{1,0:T(8,128)(2,1)S(1)} %get-tuple-element.16), channel_id=1, source_target_pairs={{0,2},{1,3},{2,0},{3,1},{4,6},{5,7},{6,4},{7,5},{8,10},{9,11},{10,... | collective-permute-start | bytes 344072 | tf_op jit(solution)/shard_map/ppermute | solution.py:229
  70.6 0.5 shard_map.50
  71.1 4.8 %collective-permute-start.4 = (bf16[64,896]{1,0:T(8,128)(2,1)S(1)}, bf16[64,896]{1,0:T(8,128)(2,1)S(1)}, u32[]{:S(2)}, u32[]{:S(2)}) collective-permute-start(bf16[64,896]{1,0:T(8,128)(2,1)S(1)} %get-tuple-element.17), channel_id=1, source_target_pairs={{0,1},{1,2},{2,3},{3,0},{4,5},{5,6},{6,7},{7,4},{8,9},{9,10},{10,1... | collective-permute-start | bytes 344072 | tf_op jit(solution)/shard_map/ppermute | solution.py:229
  75.9 1.9 %collective-permute-start.5 = (bf16[64,896]{1,0:T(8,128)(2,1)S(1)}, bf16[64,896]{1,0:T(8,128)(2,1)S(1)}, u32[]{:S(2)}, u32[]{:S(2)}) collective-permute-start(bf16[64,896]{1,0:T(8,128)(2,1)S(1)} %get-tuple-element.18), channel_id=1, source_target_pairs={{0,3},{1,0},{2,1},{3,2},{4,7},{5,4},{6,5},{7,6},{8,11},{9,8},{10,9... | collective-permute-start | bytes 344072 | tf_op jit(solution)/shard_map/ppermute | solution.py:229
  77.9 1.0 %collective-permute-done.3 = bf16[64,896]{1,0:T(8,128)(2,1)S(1)} collective-permute-done((bf16[64,896]{1,0:T(8,128)(2,1)S(1)}, bf16[64,896]{1,0:T(8,128)(2,1)S(1)}, u32[]{:S(2)}, u32[]{:S(2)}) %collective-permute-start.3) | collective-permute-done | bytes 114720 | tf_op jit(solution)/shard_map/ppermute | solution.py:229
  78.9 4.0 %collective-permute-done.4 = bf16[64,896]{1,0:T(8,128)(2,1)S(1)} collective-permute-done((bf16[64,896]{1,0:T(8,128)(2,1)S(1)}, bf16[64,896]{1,0:T(8,128)(2,1)S(1)}, u32[]{:S(2)}, u32[]{:S(2)}) %collective-permute-start.4) | collective-permute-done | bytes 114720 | tf_op jit(solution)/shard_map/ppermute | solution.py:229
  82.9 4.0 %collective-permute-done.5 = bf16[64,896]{1,0:T(8,128)(2,1)S(1)} collective-permute-done((bf16[64,896]{1,0:T(8,128)(2,1)S(1)}, bf16[64,896]{1,0:T(8,128)(2,1)S(1)}, u32[]{:S(2)}, u32[]{:S(2)}) %collective-permute-start.5) | collective-permute-done | bytes 114720 | tf_op jit(solution)/shard_map/ppermute | solution.py:229
  86.9 0.7 add_convert_fusion
  (5 shorter events, 0.0 us)
Async XLA Ops:
  11.8 53.3 %copy-start = (bf16[448,3584]{1,0:T(8,128)(2,1)S(1)}, bf16[448,3584]{1,0:T(8,128)(2,1)}, u32[]{:S(2)}) copy-start(bf16[448,3584]{1,0:T(8,128)(2,1)} %weight_ref.3) | copy-start | bytes 9633796
  11.8 29.9 %all-to-all-start.1 = ((bf16[8,256,128]{2,1,0:T(8,128)(2,1)}), bf16[8,256,128]{2,1,0:T(8,128)(2,1)}, u32[]{:S(2)}, u32[]{:S(2)}) async-start(bf16[8,256,128]{2,1,0:T(8,128)(2,1)} %get-tuple-element.12), calls=%async_computation.1 | async-start | bytes 1048576 | tf_op jit(solution)/shard_map/all_to_all | solution.py:248
  17.8 17.2 %collective-permute-start.2 = (bf16[256,256]{1,0:T(8,128)(2,1)}, bf16[256,256]{1,0:T(8,128)(2,1)S(1)}, u32[]{:S(2)}, u32[]{:S(2)}) collective-permute-start(bf16[256,256]{1,0:T(8,128)(2,1)} %get-tuple-element.13.refs_0_), channel_id=1, source_target_pairs={{0,48},{16,0},{32,16},{48,32},{1,49},{17,1},{33,17},{49,33},{2,50}... | collective-permute-start | bytes 393224 | tf_op jit(solution)/shard_map/ppermute | solution.py:245
  28.2 13.5 %collective-permute-start.1 = (bf16[256,256]{1,0:T(8,128)(2,1)}, bf16[256,256]{1,0:T(8,128)(2,1)S(1)}, u32[]{:S(2)}, u32[]{:S(2)}) collective-permute-start(bf16[256,256]{1,0:T(8,128)(2,1)} %get-tuple-element.13.refs_0_), channel_id=1, source_target_pairs={{0,16},{16,32},{32,48},{48,0},{1,17},{17,33},{33,49},{49,1},{2,18}... | collective-permute-start | bytes 393224 | tf_op jit(solution)/shard_map/ppermute | solution.py:245
  30.2 11.5 %collective-permute-start = (bf16[256,256]{1,0:T(8,128)(2,1)}, bf16[256,256]{1,0:T(8,128)(2,1)}, u32[]{:S(2)}, u32[]{:S(2)}) collective-permute-start(bf16[256,256]{1,0:T(8,128)(2,1)} %get-tuple-element.13.refs_0_), channel_id=1, source_target_pairs={{0,32},{16,48},{32,0},{48,16},{1,33},{17,49},{33,1},{49,17},{2,34}... | collective-permute-start | bytes 393224 | tf_op jit(solution)/shard_map/ppermute | solution.py:245
  35.0 6.7 %copy-start.1 = (bf16[256,256]{1,0:T(8,128)(2,1)}, bf16[256,256]{1,0:T(8,128)(2,1)S(1)}, u32[]{:S(2)}) copy-start(bf16[256,256]{1,0:T(8,128)(2,1)S(1)} %collective-permute-done.2.refs_3_) | copy-start | bytes 393220
  41.7 0.6 copy-start.2
  65.9 13.0 %collective-permute-start.3 = (bf16[64,896]{1,0:T(8,128)(2,1)S(1)}, bf16[64,896]{1,0:T(8,128)(2,1)S(1)}, u32[]{:S(2)}, u32[]{:S(2)}) collective-permute-start(bf16[64,896]{1,0:T(8,128)(2,1)S(1)} %get-tuple-element.16), channel_id=1, source_target_pairs={{0,2},{1,3},{2,0},{3,1},{4,6},{5,7},{6,4},{7,5},{8,10},{9,11},{10,... | collective-permute-start | bytes 344072 | tf_op jit(solution)/shard_map/ppermute | solution.py:229
  71.1 11.7 %collective-permute-start.4 = (bf16[64,896]{1,0:T(8,128)(2,1)S(1)}, bf16[64,896]{1,0:T(8,128)(2,1)S(1)}, u32[]{:S(2)}, u32[]{:S(2)}) collective-permute-start(bf16[64,896]{1,0:T(8,128)(2,1)S(1)} %get-tuple-element.17), channel_id=1, source_target_pairs={{0,1},{1,2},{2,3},{3,0},{4,5},{5,6},{6,7},{7,4},{8,9},{9,10},{10,1... | collective-permute-start | bytes 344072 | tf_op jit(solution)/shard_map/ppermute | solution.py:229
  75.9 11.0 %collective-permute-start.5 = (bf16[64,896]{1,0:T(8,128)(2,1)S(1)}, bf16[64,896]{1,0:T(8,128)(2,1)S(1)}, u32[]{:S(2)}, u32[]{:S(2)}) collective-permute-start(bf16[64,896]{1,0:T(8,128)(2,1)S(1)} %get-tuple-element.18), channel_id=1, source_target_pairs={{0,3},{1,0},{2,1},{3,2},{4,7},{5,4},{6,5},{7,6},{8,11},{9,8},{10,9... | collective-permute-start | bytes 344072 | tf_op jit(solution)/shard_map/ppermute | solution.py:229

commit v7 on v4

--- a/solution.py
+++ b/solution.py
@@ -133,19 +133,24 @@
 
 def project_far(parts, out_weight, heads, groups, rows, step, tp_size):
     features, columns = out_weight.shape
-
-    def body(parts_ref, weight_ref, attention_ref, far_ref):
+    width = columns // tp_size
+    half = rows // 2
+
+    def body(parts_ref, weight_ref, attention_ref, upper_ref, lower_ref):
         combine(parts_ref, attention_ref, heads, groups, rows)
-        far_ref[...] = share_of(attention_ref, weight_ref, step, tp_size).astype(far_ref.dtype)
+        share = share_of(attention_ref, weight_ref, step, tp_size).astype(upper_ref.dtype)
+        upper_ref[...] = share[:half]
+        lower_ref[...] = share[half:]
 
     return pl.pallas_call(
         body,
         out_shape=(
             jax.ShapeDtypeStruct((rows, features), jnp.bfloat16),
-            jax.ShapeDtypeStruct((rows, columns // tp_size), jnp.bfloat16),
+            jax.ShapeDtypeStruct((half, width), jnp.bfloat16),
+            jax.ShapeDtypeStruct((half, width), jnp.bfloat16),
         ),
         cost_estimate=pl.CostEstimate(
-            flops=2 * rows * features * columns // tp_size,
+            flops=2 * rows * features * width,
             bytes_accessed=2 * features * columns,
             transcendentals=0,
         ),
@@ -159,17 +164,12 @@
 
     def body(attention_ref, weight_ref, *out_refs):
         for step, out_ref in zip(steps, out_refs):
-            out_ref[...] = share_of(attention_ref, weight_ref, step, tp_size).astype(
-                out_ref.dtype
-            )
+            out_ref[...] = share_of(attention_ref, weight_ref, step, tp_size)
 
     return pl.pallas_call(
         body,
         out_shape=[
-            jax.ShapeDtypeStruct(
-                (rows, columns // tp_size), jnp.bfloat16 if step else jnp.float32
-            )
-            for step in steps
+            jax.ShapeDtypeStruct((rows, columns // tp_size), jnp.float32) for _ in steps
         ],
         cost_estimate=pl.CostEstimate(
             flops=2 * rows * features * len(steps) * (columns // tp_size),
@@ -178,6 +178,24 @@
         ),
         compiler_params=pltpu.CompilerParams(vmem_limit_bytes=VMEM_LIMIT),
     )(attention, out_weight)
+
+
+def add_passing(up, down, upper, lower):
+    half = upper.shape[0]
+
+    def body(up_ref, down_ref, upper_ref, lower_ref, up_out, down_out):
+        up_out[:half] = (up_ref[:half] + upper_ref[...].astype(jnp.float32)).astype(up_out.dtype)
+        up_out[half:] = up_ref[half:].astype(up_out.dtype)
+        down_out[:half] = down_ref[:half].astype(down_out.dtype)
+        down_out[half:] = (down_ref[half:] + lower_ref[...].astype(jnp.float32)).astype(
+            down_out.dtype
+        )
+
+    return pl.pallas_call(
+        body,
+        out_shape=[jax.ShapeDtypeStruct(up.shape, jnp.bfloat16)] * 2,
+        compiler_params=pltpu.CompilerParams(vmem_limit_bytes=VMEM_LIMIT),
+    )(up, down, upper, lower)
 
 
 def to_member(share, step, tp_size):
@@ -205,17 +223,16 @@
     returned = lax.all_to_all(
         partial.reshape(heads * query_copies, rows, LANES), QUERY_AXES, 0, 0, tiled=True
     )
-    far = tp_size // 2
-    near = [step for step in range(1, tp_size) if step != far]
-    attention, far_share = project_far(
-        returned.reshape(-1, LANES), out_weight, heads, query_copies, rows, far, tp_size
-    )
-    arrived = [to_member(far_share, far, tp_size)]
-    *near_shares, own_share = project_near(attention, out_weight, near + [0], tp_size)
-    arrived += [to_member(share, step, tp_size) for share, step in zip(near_shares, near)]
-    total = own_share
-    for share in arrived:
-        total = total + share.astype(jnp.float32)
+    attention, upper, lower = project_far(
+        returned.reshape(-1, LANES), out_weight, heads, query_copies, rows, 2, tp_size
+    )
+    upper = to_member(upper, 1, tp_size)
+    lower = to_member(lower, 3, tp_size)
+    up, down, own_share = project_near(attention, out_weight, (1, 3, 0), tp_size)
+    up, down = add_passing(up, down, upper, lower)
+    up = to_member(up, 1, tp_size)
+    down = to_member(down, 3, tp_size)
+    total = own_share + up.astype(jnp.float32) + down.astype(jnp.float32)
     return total.astype(jnp.bfloat16)
 
 

time: 88 us -> 94.7 us (1.076)
  the two profiles are of different devices: /device:TPU:56 before, /device:TPU:1 now
where the time goes in v7:
time: 94.7 us; the launch traced here: 94.4 us
  blocking collectives  62.4 us (66%)
  starting transfers between devices  15 us (16%)
  waiting for transfers between devices  10.6 us (11%)
  Pallas kernels  4.62 us (5%)
  other arithmetic  1.76 us (2%)
    all_to_all x1, blocking collectives, shards(): lax.all_to_all(sent_kv.reshape(heads * key_copies, rows, 2 * LANES), KEY_...  28.6 us
    all_to_all x1, blocking collectives, shards(): lax.all_to_all(sent_q.reshape(heads * query_copies, rows, LANES), QUERY_A...  19.4 us
    ppermute x4, starting transfers between devices, to_member(): lax.ppermute(share, 'tp', [(i, (i + step) % tp_size) for i in range(tp_si...  15 us
    all_to_all x1, blocking collectives, shards(): lax.all_to_all(partial.reshape(heads * query_copies, rows, LANES), QUERY_...  14.5 us
    ppermute x4, waiting for transfers between devices, to_member(): lax.ppermute(share, 'tp', [(i, (i + step) % tp_size) for i in range(tp_si...  10.6 us
    pallas_call x1, Pallas kernels, attend(): pl.pallas_call(body, out_shape=jax.ShapeDtypeStruct(queries.shape, querie...  3.07 us
  transfers between devices with their start and end apart: 4, of which 4 were waited for; matrix products, arithmetic and copies ran while one was open for 0% of the time, Pallas kernels for 1%

profile of v7, /device:TPU:1, one launch (start us, length us, event | category | flops | bytes accessed | tf_op | source)
XLA Modules:
  0.0 94.4 jit_solution(7481660456300749665)
XLA Ops:
  0.0 0.0 copy-start
  0.0 1.1 %pad_maximum_fusion.held = bf16[192,448]{1,0:T(8,128)(2,1)S(1)} fusion(bf16[64,448]{1,0:T(8,128)(2,1)} %param.4, bf16[64,448]{1,0:T(8,128)(2,1)} %param.6, bf16[64,448]{1,0:T(8,128)(2,1)} %param.5), kind=kLoop, calls=%fused_computation.1 | loop fusion | flops 516096 | bytes 344064 | tf_op jit(solution)/shard_map/concatenate | solution.py:52
  1.1 0.2 shard_map.46
  1.2 28.6 %all_to_all.15 = bf16[16,64,256]{2,1,0:T(8,128)(2,1)S(1)} all-to-all(bf16[16,64,256]{2,1,0:T(8,128)(2,1)S(1)} %bitcast.11), channel_id=1, replica_groups=mesh['x'=4,'yl'=2,'zh'=4,'zl'=2,'core'=2,'tp'=4] {'x','zh'}, dimensions={0} | all-to-all | bytes 1048576 | tf_op jit(solution)/shard_map/all_to_all | solution.py:217
  29.8 19.4 %all_to_all.16 = bf16[32,64,128]{2,1,0:T(8,128)(2,1)S(1)} all-to-all(bf16[32,64,128]{2,1,0:T(8,128)(2,1)S(1)} %bitcast.10), channel_id=1, replica_groups=mesh['x'=4,'yl'=2,'zh'=4,'zl'=2,'core'=2,'tp'=4] {'x','yl','zl','core'}, dimensions={0} | all-to-all | bytes 1048576 | tf_op jit(solution)/shard_map/all_to_all | solution.py:214
  49.2 3.1 %shard_map.47 = bf16[2048,128]{1,0:T(8,128)(2,1)S(1)} custom-call(bf16[2048,128]{1,0:T(8,128)(2,1)S(1)} %bitcast.8, bf16[1024,256]{1,0:T(8,128)(2,1)S(1)} %bitcast.6), custom_call_target="tpu_custom_call" | custom-call | tf_op jit(solution)/shard_map/pallas_call | solution.py:97
  52.2 14.5 %all_to_all.17 = bf16[32,64,128]{2,1,0:T(8,128)(2,1)S(1)} all-to-all(bf16[32,64,128]{2,1,0:T(8,128)(2,1)S(1)} %bitcast.9), channel_id=1, replica_groups=mesh['x'=4,'yl'=2,'zh'=4,'zl'=2,'core'=2,'tp'=4] {'x','yl','zl','core'}, dimensions={0} | all-to-all | bytes 1048576 | tf_op jit(solution)/shard_map/all_to_all | solution.py:223
  66.7 0.0 copy-done
  66.7 0.8 shard_map.48
  67.5 4.2 %collective-permute-start = (bf16[32,896]{1,0:T(8,128)(2,1)S(1)}, bf16[32,896]{1,0:T(8,128)(2,1)S(1)}, u32[]{:S(2)}, u32[]{:S(2)}) collective-permute-start(bf16[32,896]{1,0:T(8,128)(2,1)S(1)} %get-tuple-element.21), channel_id=1, source_target_pairs={{0,1},{1,2},{2,3},{3,0},{4,5},{5,6},{6,7},{7,4},{8,9},{9,10},{10,1... | collective-permute-start | bytes 172040 | tf_op jit(solution)/shard_map/ppermute | solution.py:202
  71.8 3.2 %collective-permute-start.1 = (bf16[32,896]{1,0:T(8,128)(2,1)S(1)}, bf16[32,896]{1,0:T(8,128)(2,1)S(1)}, u32[]{:S(2)}, u32[]{:S(2)}) collective-permute-start(bf16[32,896]{1,0:T(8,128)(2,1)S(1)} %get-tuple-element.22), channel_id=1, source_target_pairs={{0,3},{1,0},{2,1},{3,2},{4,7},{5,4},{6,5},{7,6},{8,11},{9,8},{10,9... | collective-permute-start | bytes 172040 | tf_op jit(solution)/shard_map/ppermute | solution.py:202
  74.9 0.5 shard_map.49
  75.5 1.0 %collective-permute-done.upper_ref = bf16[32,896]{1,0:T(8,128)(2,1)S(1)} collective-permute-done((bf16[32,896]{1,0:T(8,128)(2,1)S(1)}, bf16[32,896]{1,0:T(8,128)(2,1)S(1)}, u32[]{:S(2)}, u32[]{:S(2)}) %collective-permute-start) | collective-permute-done | bytes 57376 | tf_op jit(solution)/shard_map/ppermute | solution.py:202
  76.5 3.2 %collective-permute-done.1.lower_ref = bf16[32,896]{1,0:T(8,128)(2,1)S(1)} collective-permute-done((bf16[32,896]{1,0:T(8,128)(2,1)S(1)}, bf16[32,896]{1,0:T(8,128)(2,1)S(1)}, u32[]{:S(2)}, u32[]{:S(2)}) %collective-permute-start.1) | collective-permute-done | bytes 57376 | tf_op jit(solution)/shard_map/ppermute | solution.py:202
  79.6 5.7 %collective-permute-start.2 = (bf16[64,896]{1,0:T(8,128)(2,1)S(1)}, bf16[64,896]{1,0:T(8,128)(2,1)S(1)}, u32[]{:S(2)}, u32[]{:S(2)}) collective-permute-start(bf16[64,896]{1,0:T(8,128)(2,1)S(1)} %get-tuple-element.23), channel_id=1, source_target_pairs={{0,1},{1,2},{2,3},{3,0},{4,5},{5,6},{6,7},{7,4},{8,9},{9,10},{10,1... | collective-permute-start | bytes 344072 | tf_op jit(solution)/shard_map/ppermute | solution.py:202
  85.3 1.9 %collective-permute-start.3 = (bf16[64,896]{1,0:T(8,128)(2,1)S(1)}, bf16[64,896]{1,0:T(8,128)(2,1)S(1)}, u32[]{:S(2)}, u32[]{:S(2)}) collective-permute-start(bf16[64,896]{1,0:T(8,128)(2,1)S(1)} %get-tuple-element.24), channel_id=1, source_target_pairs={{0,3},{1,0},{2,1},{3,2},{4,7},{5,4},{6,5},{7,6},{8,11},{9,8},{10,9... | collective-permute-start | bytes 344072 | tf_op jit(solution)/shard_map/ppermute | solution.py:202
  87.3 2.2 %collective-permute-done.2 = bf16[64,896]{1,0:T(8,128)(2,1)S(1)} collective-permute-done((bf16[64,896]{1,0:T(8,128)(2,1)S(1)}, bf16[64,896]{1,0:T(8,128)(2,1)S(1)}, u32[]{:S(2)}, u32[]{:S(2)}) %collective-permute-start.2) | collective-permute-done | bytes 114720 | tf_op jit(solution)/shard_map/ppermute | solution.py:202
  89.4 4.3 %collective-permute-done.3 = bf16[64,896]{1,0:T(8,128)(2,1)S(1)} collective-permute-done((bf16[64,896]{1,0:T(8,128)(2,1)S(1)}, bf16[64,896]{1,0:T(8,128)(2,1)S(1)}, u32[]{:S(2)}, u32[]{:S(2)}) %collective-permute-start.3) | collective-permute-done | bytes 114720 | tf_op jit(solution)/shard_map/ppermute | solution.py:202
  93.7 0.7 add_convert_fusion
  (1 shorter events, 0.0 us)
Async XLA Ops:
  0.0 66.7 %copy-start = (bf16[448,3584]{1,0:T(8,128)(2,1)S(1)}, bf16[448,3584]{1,0:T(8,128)(2,1)}, u32[]{:S(2)}) copy-start(bf16[448,3584]{1,0:T(8,128)(2,1)} %weight_ref.3) | copy-start | bytes 9633796
  67.5 8.9 %collective-permute-start = (bf16[32,896]{1,0:T(8,128)(2,1)S(1)}, bf16[32,896]{1,0:T(8,128)(2,1)S(1)}, u32[]{:S(2)}, u32[]{:S(2)}) collective-permute-start(bf16[32,896]{1,0:T(8,128)(2,1)S(1)} %get-tuple-element.21), channel_id=1, source_target_pairs={{0,1},{1,2},{2,3},{3,0},{4,5},{5,6},{6,7},{7,4},{8,9},{9,10},{10,1... | collective-permute-start | bytes 172040 | tf_op jit(solution)/shard_map/ppermute | solution.py:202
  71.8 7.8 %collective-permute-start.1 = (bf16[32,896]{1,0:T(8,128)(2,1)S(1)}, bf16[32,896]{1,0:T(8,128)(2,1)S(1)}, u32[]{:S(2)}, u32[]{:S(2)}) collective-permute-start(bf16[32,896]{1,0:T(8,128)(2,1)S(1)} %get-tuple-element.22), channel_id=1, source_target_pairs={{0,3},{1,0},{2,1},{3,2},{4,7},{5,4},{6,5},{7,6},{8,11},{9,8},{10,9... | collective-permute-start | bytes 172040 | tf_op jit(solution)/shard_map/ppermute | solution.py:202
  79.6 9.8 %collective-permute-start.2 = (bf16[64,896]{1,0:T(8,128)(2,1)S(1)}, bf16[64,896]{1,0:T(8,128)(2,1)S(1)}, u32[]{:S(2)}, u32[]{:S(2)}) collective-permute-start(bf16[64,896]{1,0:T(8,128)(2,1)S(1)} %get-tuple-element.23), channel_id=1, source_target_pairs={{0,1},{1,2},{2,3},{3,0},{4,5},{5,6},{6,7},{7,4},{8,9},{9,10},{10,1... | collective-permute-start | bytes 344072 | tf_op jit(solution)/shard_map/ppermute | solution.py:202
  85.3 8.4 %collective-permute-start.3 = (bf16[64,896]{1,0:T(8,128)(2,1)S(1)}, bf16[64,896]{1,0:T(8,128)(2,1)S(1)}, u32[]{:S(2)}, u32[]{:S(2)}) collective-permute-start(bf16[64,896]{1,0:T(8,128)(2,1)S(1)} %get-tuple-element.24), channel_id=1, source_target_pairs={{0,3},{1,0},{2,1},{3,2},{4,7},{5,4},{6,5},{7,6},{8,11},{9,8},{10,9... | collective-permute-start | bytes 344072 | tf_op jit(solution)/shard_map/ppermute | solution.py:202

commit v8 on v5

--- a/solution.py
+++ b/solution.py
@@ -11,11 +11,12 @@
 LANES = 128
 TOTAL, TOTAL_LOW, SHIFT = HEAD_DIM, HEAD_DIM + 1, HEAD_DIM + 2
 NEG_FILL = -1e30
-AXES = ("x", "yl", "zh", "zl", "core", "tp")
-CTX = AXES[:5]
-HEAD_AXES = ("zl", "core")
-QUERY_AXES = ("x", "yl")
-RETURN_AXES = ("x", "yl", "zl", "core")
+NEG_CLAMP = -1e29
+AXES = ("xa", "xb", "yl", "zh", "zl", "core", "tp")
+CTX = AXES[:6]
+HEAD_AXES = ("xa", "zl")
+QUERY_AXES = ("xb", "yl", "core")
+RETURN_AXES = QUERY_AXES + HEAD_AXES
 VMEM_LIMIT = 48 * 1024 * 1024
 EXP2_SCALE = math.log2(math.e) / HEAD_DIM**0.5
 
@@ -62,75 +63,77 @@
     )(one_head)
 
 
-def attend_kernel(coarse_size, steps, block, q_ref, kv_refs, out_ref):
-    zh_size = lax.axis_size("zh")
-    zh = lax.axis_index("zh")
-    own_coarse = lax.axis_index("x") * lax.axis_size("yl") + lax.axis_index("yl")
+def attend_kernel(rows, q_ref, kv_ref, out_ref, key_ref, value_ref):
+    xb, yl, zh, core = (lax.axis_index(name) for name in ("xb", "yl", "zh", "core"))
+    pair = 2 * rows
+    block = 2 * pair
+    zh_size = kv_ref.shape[0] // block
+    half = zh_size * pair
+    coarse = 4 * block
+    for xa_at in range(2):
+        for zh_at in range(zh_size):
+            start = zh_at * block + xa_at * pair
+            to_rows = slice(xa_at * half + zh_at * pair, xa_at * half + (zh_at + 1) * pair)
+            key_ref[to_rows, :] = kv_ref[start : start + pair, :LANES]
+            value_ref[to_rows, :] = kv_ref[start : start + pair, LANES:]
+    query_at = lax.broadcasted_iota(jnp.int32, (block, half), 0)
+    query_at = query_at % pair + (query_at // rows % 2) * rows + (query_at // pair) * rows
+    key_at = lax.broadcasted_iota(jnp.int32, (block, half), 1)
+    key_at = (key_at // pair) * block + key_at % pair + (key_at // rows % 2) * rows
+    distance = query_at - key_at + zh * block - core * rows
     lane = lax.broadcasted_iota(jnp.int32, (block, LANES), 1)
-
-    def tile(at, masked):
-        start = pl.multiple_of(at * block, block)
-        queries = q_ref[pl.ds(start, block), :]
-        scores = []
-        for step, kv_ref in zip(steps, kv_refs):
-            part = lax.dot_general(
-                queries,
-                kv_ref[:, :LANES],
-                (((1,), (1,)), ((), ())),
-                preferred_element_type=jnp.float32,
-            )
-            if masked:
-                source = lax.rem(zh + zh_size - step, zh_size)
-                query_at = lax.broadcasted_iota(jnp.int32, (block, block), 0)
-                key_at = lax.broadcasted_iota(jnp.int32, (block, block), 1)
-                part = jnp.where(
-                    query_at - key_at + (zh - source) * block >= 0, part, NEG_FILL
+    for xb_at in range(2):
+        for yl_at in range(2):
+            ahead = (xb_at - xb) * 2 * coarse + (yl_at - yl) * coarse
+            kept = distance + ahead >= 0
+            for xa_at in range(2):
+                total = (xa_at + 1) * half
+                known = total - half
+                starts = [
+                    ((xb_at * 2 + yl_at) * 2 + core_at) * block + xa_at * pair
+                    for core_at in range(2)
+                ]
+                queries = jnp.concatenate(
+                    [q_ref[start : start + pair, :] for start in starts], axis=0
                 )
-            scores.append(part)
-        scores = jnp.concatenate(scores, axis=1)
-        top = jnp.max(scores, axis=1, keepdims=True) * EXP2_SCALE
-        shift = top.astype(jnp.bfloat16).astype(jnp.float32)
-        weights = jnp.exp2(scores * EXP2_SCALE - shift).astype(jnp.bfloat16)
-        weighted = jnp.zeros((block, LANES), jnp.float32)
-        for part, kv_ref in enumerate(kv_refs):
-            weighted = weighted + jnp.dot(
-                weights[:, part * block : (part + 1) * block],
-                kv_ref[:, LANES:],
-                preferred_element_type=jnp.float32,
-            )
-        rounded = weighted.astype(jnp.bfloat16).astype(jnp.float32)
-        weighted = jnp.where(lane == TOTAL_LOW, weighted - rounded, weighted)
-        weighted = jnp.where(lane == SHIFT, shift, weighted)
-        out_ref[pl.ds(start, block), :] = weighted.astype(out_ref.dtype)
-
-    for at in range(coarse_size):
-
-        @pl.when(at > own_coarse)
-        def _(at=at):
-            tile(at, False)
-
-        @pl.when(at == own_coarse)
-        def _(at=at):
-            tile(at, True)
-
-        @pl.when(at < own_coarse)
-        def _(at=at):
-            out_ref[at * block : (at + 1) * block, :] = jnp.where(
-                lane == SHIFT, NEG_FILL, 0.0
-            ).astype(out_ref.dtype)
-
-
-def attend(queries, keys_values, steps, coarse_size):
-    block = queries.shape[0] // coarse_size
-
-    def body(q_ref, *refs):
-        attend_kernel(coarse_size, steps, block, q_ref, refs[:-1], refs[-1])
+                scores = lax.dot_general(
+                    queries,
+                    key_ref[:total, :],
+                    (((1,), (1,)), ((), ())),
+                    preferred_element_type=jnp.float32,
+                )
+                last = jnp.where(kept, scores[:, known:], NEG_FILL)
+                if known:
+                    scores = jnp.concatenate([scores[:, :known], last], axis=1)
+                else:
+                    scores = last
+                top = jnp.maximum(jnp.max(scores, axis=1, keepdims=True), NEG_CLAMP)
+                shift = (top * EXP2_SCALE).astype(jnp.bfloat16).astype(jnp.float32)
+                weights = jnp.exp2(scores * EXP2_SCALE - shift)
+                weighted = jnp.dot(
+                    weights.astype(jnp.bfloat16),
+                    value_ref[:total, :],
+                    preferred_element_type=jnp.float32,
+                )
+                rounded = weighted.astype(jnp.bfloat16).astype(jnp.float32)
+                weighted = jnp.where(lane == TOTAL_LOW, weighted - rounded, weighted)
+                weighted = jnp.where(lane == SHIFT, shift, weighted).astype(out_ref.dtype)
+                for core_at, start in enumerate(starts):
+                    out_ref[start : start + pair, :] = weighted[
+                        core_at * pair : (core_at + 1) * pair
+                    ]
+
+
+def attend(queries, keys_values, rows):
+    def body(*refs):
+        attend_kernel(rows, *refs)
 
     return pl.pallas_call(
         body,
         out_shape=jax.ShapeDtypeStruct(queries.shape, queries.dtype),
-        compiler_params=pltpu.CompilerParams(vmem_limit_bytes=VMEM_LIMIT),
-    )(queries, *keys_values)
+        scratch_shapes=[pltpu.VMEM((keys_values.shape[0], LANES), queries.dtype)] * 2,
+        compiler_params=pltpu.CompilerParams(vmem_limit_bytes=VMEM_LIMIT),
+    )(queries, keys_values)
 
 
 def combine(parts_ref, attention_ref, heads, groups, rows):
@@ -219,28 +222,23 @@
 def shards(queries, keys, values, out_weight):
     rows, features = queries.shape
     heads = features // HEAD_DIM
-    coarse_size = lax.axis_size("x") * lax.axis_size("yl")
-    zh_size = lax.axis_size("zh")
+    groups = lax.axis_size("xb") * lax.axis_size("yl") * lax.axis_size("core")
     tp_size = lax.axis_size("tp")
 
     one_head = lax.all_to_all(
         pack(queries, keys, values, heads), HEAD_AXES, 0, 0, tiled=True
     ).reshape(heads * rows, 3 * LANES)
-    own_kv, sent_q = spread(one_head, coarse_size)
-    steps = [0, zh_size // 2] + [step for step in range(1, zh_size) if step != zh_size // 2]
-    got_kv = [own_kv] + [
-        lax.ppermute(own_kv, "zh", [(i, (i + step) % zh_size) for i in range(zh_size)])
-        for step in steps[1:]
-    ]
+    own_kv, sent_q = spread(one_head, groups)
     got_q = lax.all_to_all(sent_q, QUERY_AXES, 0, 0, tiled=True)
-    partial = attend(got_q.reshape(-1, LANES), got_kv, steps, coarse_size)
+    got_kv = lax.all_gather(own_kv, "zh", axis=0, tiled=True)
+    partial = attend(got_q.reshape(-1, LANES), got_kv, rows)
     returned = lax.all_to_all(
-        partial.reshape(coarse_size * heads, rows, LANES), RETURN_AXES, 0, 0, tiled=True
+        partial.reshape(groups * heads, rows, LANES), RETURN_AXES, 0, 0, tiled=True
     )
     far = tp_size // 2
     near = [step for step in range(1, tp_size) if step != far]
     attention, far_share = project_far(
-        returned.reshape(-1, LANES), out_weight, heads, coarse_size, rows, far, tp_size
+        returned.reshape(-1, LANES), out_weight, heads, groups, rows, far, tp_size
     )
     arrived = [to_member(far_share, far, tp_size)]
     *near_shares, own_share = project_near(attention, out_weight, near + [0], tp_size)
@@ -252,7 +250,7 @@
 
 
 def solution(mesh):
-    split = Mesh(mesh.devices.reshape(4, 2, 4, 2, 2, 4), AXES)
+    split = Mesh(mesh.devices.reshape(2, 2, 2, 4, 2, 2, 4), AXES)
     placed = (P(CTX, "tp"), P(CTX, "tp"), P(CTX, "tp"), P("tp", None))
     return jax.shard_map(
         shards, mesh=split, in_specs=placed, out_specs=P(CTX, "tp"), check_vma=False

time: 88.7 us -> 84.9 us (0.957)
  blocking collectives: 25.1 us -> 49.4 us
  starting transfers between devices: 34 us -> 16.8 us
  waiting for transfers between devices: 15.5 us -> 8.03 us
  local copies, waits for them, and re-layouts: 3.93 us -> 1.82 us
  Pallas kernels: 7.05 us -> 5.86 us
    all_gather x0 -> x1, blocking collectives: none -> 22 us  [shards(): got_kv = lax.all_gather(own_kv, 'zh', axis=0, tiled=True)]
    ppermute x3 -> x0, starting transfers between devices: 16.7 us -> none  [shards(): lax.ppermute(own_kv, 'zh', [(i, (i + step) % zh_size) for i in range(zh_s...]
    ppermute x3 -> x0, waiting for transfers between devices: 6.51 us -> none  [shards(): lax.ppermute(own_kv, 'zh', [(i, (i + step) % zh_size) for i in range(zh_s...]
    all_to_all x1, blocking collectives: 8.78 us -> 13 us  [shards(): lax.all_to_all(pack(queries, keys, values, heads), HEAD_AXES, 0, 0, tiled...]
    unnamed x12 -> x6, local copies, waits for them, and re-layouts: 3.93 us -> 1.82 us
    all_to_all x1, blocking collectives: 16.3 us -> 14.5 us  [shards(): lax.all_to_all(partial.reshape(groups * heads, rows, LANES), RETURN_AXES,...]
    pallas_call x1, Pallas kernels: 5.47 us -> 4.28 us  [attend(): pl.pallas_call(body, out_shape=jax.ShapeDtypeStruct(queries.shape, querie...]
    ppermute x3, waiting for transfers between devices: 9.01 us -> 8.03 us  [to_member(): lax.ppermute(share, 'tp', [(i, (i + step) % tp_size) for i in range(tp_si...]
  transfers between devices with their start and end apart: 7 -> 4, of which waited for: 4 -> 2; matrix products, arithmetic and copies ran while one was open for 0% -> 0% of each run, Pallas kernels for 1% -> 1%
where the time goes in v8:
time: 84.9 us; the launch traced here: 83.8 us
  blocking collectives  49.4 us (58%)
  starting transfers between devices  16.8 us (20%)
  waiting for transfers between devices  8.03 us (9%)
  Pallas kernels  5.86 us (7%)
  local copies, waits for them, and re-layouts  1.82 us (2%)
  other arithmetic  1.77 us (2%)
    all_gather x1, blocking collectives, shards(): got_kv = lax.all_gather(own_kv, 'zh', axis=0, tiled=True)  22 us
    all_to_all x1, blocking collectives, shards(): lax.all_to_all(partial.reshape(groups * heads, rows, LANES), RETURN_AXES,...  14.5 us
    all_to_all x1, blocking collectives, shards(): lax.all_to_all(pack(queries, keys, values, heads), HEAD_AXES, 0, 0, tiled...  13 us
    ppermute x3, starting transfers between devices, to_member(): lax.ppermute(share, 'tp', [(i, (i + step) % tp_size) for i in range(tp_si...  11.4 us
    ppermute x3, waiting for transfers between devices, to_member(): lax.ppermute(share, 'tp', [(i, (i + step) % tp_size) for i in range(tp_si...  8.03 us
    all_to_all x1, starting transfers between devices, shards(): got_q = lax.all_to_all(sent_q, QUERY_AXES, 0, 0, tiled=True)  5.38 us
    pallas_call x1, Pallas kernels, attend(): pl.pallas_call(body, out_shape=jax.ShapeDtypeStruct(queries.shape, querie...  4.28 us
    unnamed x6, local copies, waits for them, and re-layouts  1.82 us
  transfers between devices with their start and end apart: 4, of which 2 were waited for; matrix products, arithmetic and copies ran while one was open for 0% of the time, Pallas kernels for 1%

profile of v8, /device:TPU:56, one launch (start us, length us, event | category | flops | bytes accessed | tf_op | source)
XLA Modules:
  0.0 83.8 jit_solution(9679186156683725935)
XLA Ops:
  0.0 0.0 copy-start
  0.0 1.1 %pad_maximum_fusion.held = bf16[192,448]{1,0:T(8,128)(2,1)S(1)} fusion(bf16[64,448]{1,0:T(8,128)(2,1)} %param.4, bf16[64,448]{1,0:T(8,128)(2,1)} %param.6, bf16[64,448]{1,0:T(8,128)(2,1)} %param.5), kind=kLoop, calls=%fused_computation.1 | loop fusion | flops 516096 | bytes 344064 | tf_op jit(solution)/shard_map/concatenate | solution.py:43
  1.1 0.1 shard_map.46
  1.2 13.0 %all_to_all.15 = bf16[4,64,384]{2,1,0:T(8,128)(2,1)S(1)} all-to-all(bf16[4,64,384]{2,1,0:T(8,128)(2,1)S(1)} %shard_map.46), channel_id=1, replica_groups=mesh['xa'=2,'xb'=2,'yl'=2,'zh'=4,'zl'=2,'core'=2,'tp'=4] {'xa','zl'}, dimensions={0} | all-to-all | bytes 393216 | tf_op jit(solution)/shard_map/all_to_all | solution.py:228
  14.2 0.1 shard_map.47
  14.3 0.0 copy-start.2
  14.3 0.8 copy-done.2
  15.0 5.4 %all-to-all-start.1 = ((bf16[8,256,128]{2,1,0:T(8,128)(2,1)}), bf16[8,256,128]{2,1,0:T(8,128)(2,1)}, u32[]{:S(2)}, u32[]{:S(2)}) async-start(bf16[8,256,128]{2,1,0:T(8,128)(2,1)} %copy-done.2), calls=%async_computation.1 | async-start | bytes 1048576 | tf_op jit(solution)/shard_map/all_to_all | solution.py:232
  20.4 22.0 %all_gather.3.refs_1_ = bf16[1024,256]{1,0:T(8,128)(2,1)} all-gather(bf16[256,256]{1,0:T(8,128)(2,1)S(1)} %get-tuple-element.13), channel_id=1, replica_groups=mesh['xa'=2,'xb'=2,'yl'=2,'zh'=4,'zl'=2,'core'=2,'tp'=4] {'zh'}, dimensions={0}, use_global_device_ids=true | all-gather | bytes 655360 | tf_op jit(solution)/shard_map/all_gather | solution.py:233
  42.4 0.0 all-to-all-done.1
  42.4 0.0 copy-start.1
  42.4 1.0 %copy-done.1 = bf16[1024,256]{1,0:T(8,128)(2,1)S(1)} copy-done((bf16[1024,256]{1,0:T(8,128)(2,1)S(1)}, bf16[1024,256]{1,0:T(8,128)(2,1)}, u32[]{:S(2)}) %copy-start.1) | copy-done | bytes 524312
  43.4 4.3 %shard_map.48 = bf16[2048,128]{1,0:T(8,128)(2,1)S(1)} custom-call(bf16[2048,128]{1,0:T(8,128)(2,1)} %bitcast.1.refs_0_, bf16[1024,256]{1,0:T(8,128)(2,1)S(1)} %copy-done.1), custom_call_target="tpu_custom_call" | custom-call | tf_op jit(solution)/shard_map/pallas_call | solution.py:131
  47.7 14.5 %all_to_all.16 = bf16[32,64,128]{2,1,0:T(8,128)(2,1)S(1)} all-to-all(bf16[32,64,128]{2,1,0:T(8,128)(2,1)S(1)} %bitcast.5), channel_id=1, replica_groups=mesh['xa'=2,'xb'=2,'yl'=2,'zh'=4,'zl'=2,'core'=2,'tp'=4] {'xb','yl','cor..., dimensions={0} | all-to-all | bytes 1048576 | tf_op jit(solution)/shard_map/all_to_all | solution.py:235
  62.2 0.0 copy-done
  62.2 0.8 shard_map.49
  63.1 3.8 %collective-permute-start = (bf16[64,896]{1,0:T(8,128)(2,1)S(1)}, bf16[64,896]{1,0:T(8,128)(2,1)S(1)}, u32[]{:S(2)}, u32[]{:S(2)}) collective-permute-start(bf16[64,896]{1,0:T(8,128)(2,1)S(1)} %get-tuple-element.16), channel_id=1, source_target_pairs={{0,2},{1,3},{2,0},{3,1},{4,6},{5,7},{6,4},{7,5},{8,10},{9,11},{10,... | collective-permute-start | bytes 344072 | tf_op jit(solution)/shard_map/ppermute | solution.py:219
  66.9 0.5 shard_map.50
  67.4 5.7 %collective-permute-start.1 = (bf16[64,896]{1,0:T(8,128)(2,1)S(1)}, bf16[64,896]{1,0:T(8,128)(2,1)S(1)}, u32[]{:S(2)}, u32[]{:S(2)}) collective-permute-start(bf16[64,896]{1,0:T(8,128)(2,1)S(1)} %get-tuple-element.17), channel_id=1, source_target_pairs={{0,1},{1,2},{2,3},{3,0},{4,5},{5,6},{6,7},{7,4},{8,9},{9,10},{10,1... | collective-permute-start | bytes 344072 | tf_op jit(solution)/shard_map/ppermute | solution.py:219
  73.1 1.9 %collective-permute-start.2 = (bf16[64,896]{1,0:T(8,128)(2,1)S(1)}, bf16[64,896]{1,0:T(8,128)(2,1)S(1)}, u32[]{:S(2)}, u32[]{:S(2)}) collective-permute-start(bf16[64,896]{1,0:T(8,128)(2,1)S(1)} %get-tuple-element.18), channel_id=1, source_target_pairs={{0,3},{1,0},{2,1},{3,2},{4,7},{5,4},{6,5},{7,6},{8,11},{9,8},{10,9... | collective-permute-start | bytes 344072 | tf_op jit(solution)/shard_map/ppermute | solution.py:219
  75.1 0.0 collective-permute-done
  75.1 3.9 %collective-permute-done.1 = bf16[64,896]{1,0:T(8,128)(2,1)S(1)} collective-permute-done((bf16[64,896]{1,0:T(8,128)(2,1)S(1)}, bf16[64,896]{1,0:T(8,128)(2,1)S(1)}, u32[]{:S(2)}, u32[]{:S(2)}) %collective-permute-start.1) | collective-permute-done | bytes 114720 | tf_op jit(solution)/shard_map/ppermute | solution.py:219
  79.0 4.1 %collective-permute-done.2 = bf16[64,896]{1,0:T(8,128)(2,1)S(1)} collective-permute-done((bf16[64,896]{1,0:T(8,128)(2,1)S(1)}, bf16[64,896]{1,0:T(8,128)(2,1)S(1)}, u32[]{:S(2)}, u32[]{:S(2)}) %collective-permute-start.2) | collective-permute-done | bytes 114720 | tf_op jit(solution)/shard_map/ppermute | solution.py:219
  83.1 0.7 add_convert_fusion
Async XLA Ops:
  0.0 62.2 %copy-start = (bf16[448,3584]{1,0:T(8,128)(2,1)S(1)}, bf16[448,3584]{1,0:T(8,128)(2,1)}, u32[]{:S(2)}) copy-start(bf16[448,3584]{1,0:T(8,128)(2,1)} %weight_ref.3) | copy-start | bytes 9633796
  14.3 0.8 copy-start.2
  15.0 27.3 %all-to-all-start.1 = ((bf16[8,256,128]{2,1,0:T(8,128)(2,1)}), bf16[8,256,128]{2,1,0:T(8,128)(2,1)}, u32[]{:S(2)}, u32[]{:S(2)}) async-start(bf16[8,256,128]{2,1,0:T(8,128)(2,1)} %copy-done.2), calls=%async_computation.1 | async-start | bytes 1048576 | tf_op jit(solution)/shard_map/all_to_all | solution.py:232
  42.4 1.0 %copy-start.1 = (bf16[1024,256]{1,0:T(8,128)(2,1)S(1)}, bf16[1024,256]{1,0:T(8,128)(2,1)}, u32[]{:S(2)}) copy-start(bf16[1024,256]{1,0:T(8,128)(2,1)} %all_gather.3.refs_1_) | copy-start | bytes 1572868
  63.1 12.0 %collective-permute-start = (bf16[64,896]{1,0:T(8,128)(2,1)S(1)}, bf16[64,896]{1,0:T(8,128)(2,1)S(1)}, u32[]{:S(2)}, u32[]{:S(2)}) collective-permute-start(bf16[64,896]{1,0:T(8,128)(2,1)S(1)} %get-tuple-element.16), channel_id=1, source_target_pairs={{0,2},{1,3},{2,0},{3,1},{4,6},{5,7},{6,4},{7,5},{8,10},{9,11},{10,... | collective-permute-start | bytes 344072 | tf_op jit(solution)/shard_map/ppermute | solution.py:219
  67.4 11.6 %collective-permute-start.1 = (bf16[64,896]{1,0:T(8,128)(2,1)S(1)}, bf16[64,896]{1,0:T(8,128)(2,1)S(1)}, u32[]{:S(2)}, u32[]{:S(2)}) collective-permute-start(bf16[64,896]{1,0:T(8,128)(2,1)S(1)} %get-tuple-element.17), channel_id=1, source_target_pairs={{0,1},{1,2},{2,3},{3,0},{4,5},{5,6},{6,7},{7,4},{8,9},{9,10},{10,1... | collective-permute-start | bytes 344072 | tf_op jit(solution)/shard_map/ppermute | solution.py:219
  73.1 10.0 %collective-permute-start.2 = (bf16[64,896]{1,0:T(8,128)(2,1)S(1)}, bf16[64,896]{1,0:T(8,128)(2,1)S(1)}, u32[]{:S(2)}, u32[]{:S(2)}) collective-permute-start(bf16[64,896]{1,0:T(8,128)(2,1)S(1)} %get-tuple-element.18), channel_id=1, source_target_pairs={{0,3},{1,0},{2,1},{3,2},{4,7},{5,4},{6,5},{7,6},{8,11},{9,8},{10,9... | collective-permute-start | bytes 344072 | tf_op jit(solution)/shard_map/ppermute | solution.py:219

commit v9 on v8

--- a/solution.py
+++ b/solution.py
@@ -15,8 +15,8 @@
 AXES = ("xa", "xb", "yl", "zh", "zl", "core", "tp")
 CTX = AXES[:6]
 HEAD_AXES = ("xa", "zl")
-QUERY_AXES = ("xb", "yl", "core")
-RETURN_AXES = QUERY_AXES + HEAD_AXES
+KEY_AXES = ("xb", "yl", "core")
+RETURN_AXES = ("zh",) + HEAD_AXES
 VMEM_LIMIT = 48 * 1024 * 1024
 EXP2_SCALE = math.log2(math.e) / HEAD_DIM**0.5
 
@@ -47,17 +47,17 @@
     rows = one_head.shape[0]
     kind = one_head.dtype
 
-    def body(one_ref, kv_out, q_out):
-        kv_out[...] = one_ref[:, : 2 * LANES]
-        query = one_ref[:, 2 * LANES :]
+    def body(one_ref, q_out, kv_out):
+        q_out[...] = one_ref[:, 2 * LANES :]
+        pair = one_ref[:, : 2 * LANES]
         for copy in range(copies):
-            q_out[copy] = query
+            kv_out[copy] = pair
 
     return pl.pallas_call(
         body,
         out_shape=(
-            jax.ShapeDtypeStruct((rows, 2 * LANES), kind),
-            jax.ShapeDtypeStruct((copies, rows, LANES), kind),
+            jax.ShapeDtypeStruct((rows, LANES), kind),
+            jax.ShapeDtypeStruct((copies, rows, 2 * LANES), kind),
         ),
         compiler_params=pltpu.CompilerParams(vmem_limit_bytes=VMEM_LIMIT),
     )(one_head)
@@ -67,61 +67,60 @@
     xb, yl, zh, core = (lax.axis_index(name) for name in ("xb", "yl", "zh", "core"))
     pair = 2 * rows
     block = 2 * pair
-    zh_size = kv_ref.shape[0] // block
-    half = zh_size * pair
     coarse = 4 * block
+    sources = kv_ref.shape[0] // block
+    half = sources * pair
     for xa_at in range(2):
-        for zh_at in range(zh_size):
-            start = zh_at * block + xa_at * pair
-            to_rows = slice(xa_at * half + zh_at * pair, xa_at * half + (zh_at + 1) * pair)
+        for source in range(sources):
+            start = source * block + xa_at * pair
+            to_rows = slice(xa_at * half + source * pair, xa_at * half + (source + 1) * pair)
             key_ref[to_rows, :] = kv_ref[start : start + pair, :LANES]
             value_ref[to_rows, :] = kv_ref[start : start + pair, LANES:]
     query_at = lax.broadcasted_iota(jnp.int32, (block, half), 0)
-    query_at = query_at % pair + (query_at // rows % 2) * rows + (query_at // pair) * rows
+    query_at = (query_at // pair) * block + query_at % pair + (query_at // rows % 2) * rows
     key_at = lax.broadcasted_iota(jnp.int32, (block, half), 1)
-    key_at = (key_at // pair) * block + key_at % pair + (key_at // rows % 2) * rows
-    distance = query_at - key_at + zh * block - core * rows
+    source_at = key_at // pair
+    key_at = (
+        (source_at // 2) * coarse
+        + (source_at % 2) * rows
+        + key_at % pair
+        + (key_at // rows % 2) * rows
+    )
+    distance = query_at - key_at + (xb * 2 + yl) * coarse + core * rows - zh * block
     lane = lax.broadcasted_iota(jnp.int32, (block, LANES), 1)
-    for xb_at in range(2):
-        for yl_at in range(2):
-            ahead = (xb_at - xb) * 2 * coarse + (yl_at - yl) * coarse
-            kept = distance + ahead >= 0
-            for xa_at in range(2):
-                total = (xa_at + 1) * half
-                known = total - half
-                starts = [
-                    ((xb_at * 2 + yl_at) * 2 + core_at) * block + xa_at * pair
-                    for core_at in range(2)
-                ]
-                queries = jnp.concatenate(
-                    [q_ref[start : start + pair, :] for start in starts], axis=0
-                )
-                scores = lax.dot_general(
-                    queries,
-                    key_ref[:total, :],
-                    (((1,), (1,)), ((), ())),
-                    preferred_element_type=jnp.float32,
-                )
-                last = jnp.where(kept, scores[:, known:], NEG_FILL)
-                if known:
-                    scores = jnp.concatenate([scores[:, :known], last], axis=1)
-                else:
-                    scores = last
-                top = jnp.maximum(jnp.max(scores, axis=1, keepdims=True), NEG_CLAMP)
-                shift = (top * EXP2_SCALE).astype(jnp.bfloat16).astype(jnp.float32)
-                weights = jnp.exp2(scores * EXP2_SCALE - shift)
-                weighted = jnp.dot(
-                    weights.astype(jnp.bfloat16),
-                    value_ref[:total, :],
-                    preferred_element_type=jnp.float32,
-                )
-                rounded = weighted.astype(jnp.bfloat16).astype(jnp.float32)
-                weighted = jnp.where(lane == TOTAL_LOW, weighted - rounded, weighted)
-                weighted = jnp.where(lane == SHIFT, shift, weighted).astype(out_ref.dtype)
-                for core_at, start in enumerate(starts):
-                    out_ref[start : start + pair, :] = weighted[
-                        core_at * pair : (core_at + 1) * pair
-                    ]
+    for zh_at in range(0, q_ref.shape[0] // block, 2):
+        kept = distance + zh_at * block >= 0
+        for xa_at in range(2):
+            total = (xa_at + 1) * half
+            known = total - half
+            starts = [(zh_at + after) * block + xa_at * pair for after in range(2)]
+            queries = jnp.concatenate(
+                [q_ref[start : start + pair, :] for start in starts], axis=0
+            )
+            scores = lax.dot_general(
+                queries,
+                key_ref[:total, :],
+                (((1,), (1,)), ((), ())),
+                preferred_element_type=jnp.float32,
+            )
+            last = jnp.where(kept, scores[:, known:], NEG_FILL)
+            if known:
+                scores = jnp.concatenate([scores[:, :known], last], axis=1)
+            else:
+                scores = last
+            top = jnp.maximum(jnp.max(scores, axis=1, keepdims=True), NEG_CLAMP)
+            shift = (top * EXP2_SCALE).astype(jnp.bfloat16).astype(jnp.float32)
+            weights = jnp.exp2(scores * EXP2_SCALE - shift)
+            weighted = jnp.dot(
+                weights.astype(jnp.bfloat16),
+                value_ref[:total, :],
+                preferred_element_type=jnp.float32,
+            )
+            rounded = weighted.astype(jnp.bfloat16).astype(jnp.float32)
+            weighted = jnp.where(lane == TOTAL_LOW, weighted - rounded, weighted)
+            weighted = jnp.where(lane == SHIFT, shift, weighted).astype(out_ref.dtype)
+            for after, start in enumerate(starts):
+                out_ref[start : start + pair, :] = weighted[after * pair : (after + 1) * pair]
 
 
 def attend(queries, keys_values, rows):
@@ -222,16 +221,17 @@
 def shards(queries, keys, values, out_weight):
     rows, features = queries.shape
     heads = features // HEAD_DIM
-    groups = lax.axis_size("xb") * lax.axis_size("yl") * lax.axis_size("core")
+    groups = lax.axis_size("zh")
+    key_copies = lax.axis_size("xb") * lax.axis_size("yl") * lax.axis_size("core")
     tp_size = lax.axis_size("tp")
 
     one_head = lax.all_to_all(
         pack(queries, keys, values, heads), HEAD_AXES, 0, 0, tiled=True
     ).reshape(heads * rows, 3 * LANES)
-    own_kv, sent_q = spread(one_head, groups)
-    got_q = lax.all_to_all(sent_q, QUERY_AXES, 0, 0, tiled=True)
-    got_kv = lax.all_gather(own_kv, "zh", axis=0, tiled=True)
-    partial = attend(got_q.reshape(-1, LANES), got_kv, rows)
+    own_q, sent_kv = spread(one_head, key_copies)
+    got_kv = lax.all_to_all(sent_kv, KEY_AXES, 0, 0, tiled=True)
+    got_q = lax.all_gather(own_q, "zh", axis=0, tiled=True)
+    partial = attend(got_q, got_kv.reshape(-1, 2 * LANES), rows)
     returned = lax.all_to_all(
         partial.reshape(groups * heads, rows, LANES), RETURN_AXES, 0, 0, tiled=True
     )

time: 84.9 us -> 80.7 us (0.951)
  waiting for transfers between devices: 8.03 us -> 6.87 us
  blocking collectives: 49.4 us -> 48.3 us
    all_gather x1, blocking collectives: 22 us -> 19 us  [shards(): got_q = lax.all_gather(own_q, 'zh', axis=0, tiled=True)]
    all_to_all x1, blocking collectives: 14.5 us -> 16.3 us  [shards(): lax.all_to_all(partial.reshape(groups * heads, rows, LANES), RETURN_AXES,...]
    ppermute x3, waiting for transfers between devices: 8.03 us -> 6.87 us  [to_member(): lax.ppermute(share, 'tp', [(i, (i + step) % tp_size) for i in range(tp_si...]
    unnamed x6 -> x4, local copies, waits for them, and re-layouts: 1.82 us -> 1.02 us
  transfers between devices with their start and end apart: 4 -> 4, of which waited for: 2 -> 3; matrix products, arithmetic and copies ran while one was open for 0% -> 0% of each run, Pallas kernels for 1% -> 1%
where the time goes in v9:
time: 80.7 us; the launch traced here: 80.4 us
  blocking collectives  48.3 us (60%)
  starting transfers between devices  16.9 us (21%)
  waiting for transfers between devices  6.87 us (9%)
  Pallas kernels  5.43 us (7%)
  other arithmetic  1.77 us (2%)
  local copies, waits for them, and re-layouts  1.02 us (1%)
    all_gather x1, blocking collectives, shards(): got_q = lax.all_gather(own_q, 'zh', axis=0, tiled=True)  19 us
    all_to_all x1, blocking collectives, shards(): lax.all_to_all(partial.reshape(groups * heads, rows, LANES), RETURN_AXES,...  16.3 us
    all_to_all x1, blocking collectives, shards(): lax.all_to_all(pack(queries, keys, values, heads), HEAD_AXES, 0, 0, tiled...  13 us
    ppermute x3, starting transfers between devices, to_member(): lax.ppermute(share, 'tp', [(i, (i + step) % tp_size) for i in range(tp_si...  11.4 us
    ppermute x3, waiting for transfers between devices, to_member(): lax.ppermute(share, 'tp', [(i, (i + step) % tp_size) for i in range(tp_si...  6.87 us
    all_to_all x1, starting transfers between devices, shards(): got_kv = lax.all_to_all(sent_kv, KEY_AXES, 0, 0, tiled=True)  5.47 us
    pallas_call x1, Pallas kernels, attend(): pl.pallas_call(body, out_shape=jax.ShapeDtypeStruct(queries.shape, querie...  4.06 us
  transfers between devices with their start and end apart: 4, of which 3 were waited for; matrix products, arithmetic and copies ran while one was open for 0% of the time, Pallas kernels for 1%

profile of v9, /device:TPU:56, one launch (start us, length us, event | category | flops | bytes accessed | tf_op | source)
XLA Modules:
  0.0 80.4 jit_solution(8380299285591567280)
XLA Ops:
  0.0 0.0 copy-start
  0.0 1.1 %pad_maximum_fusion.held = bf16[192,448]{1,0:T(8,128)(2,1)S(1)} fusion(bf16[64,448]{1,0:T(8,128)(2,1)} %param.4, bf16[64,448]{1,0:T(8,128)(2,1)} %param.6, bf16[64,448]{1,0:T(8,128)(2,1)} %param.5), kind=kLoop, calls=%fused_computation.1 | loop fusion | flops 516096 | bytes 344064 | tf_op jit(solution)/shard_map/concatenate | solution.py:43
  1.1 0.1 shard_map.46
  1.2 13.0 %all_to_all.15 = bf16[4,64,384]{2,1,0:T(8,128)(2,1)S(1)} all-to-all(bf16[4,64,384]{2,1,0:T(8,128)(2,1)S(1)} %shard_map.46), channel_id=1, replica_groups=mesh['xa'=2,'xb'=2,'yl'=2,'zh'=4,'zl'=2,'core'=2,'tp'=4] {'xa','zl'}, dimensions={0} | all-to-all | bytes 393216 | tf_op jit(solution)/shard_map/all_to_all | solution.py:228
  14.2 0.1 shard_map.47
  14.3 0.0 copy-start.1
  14.3 1.0 %copy-done.1 = bf16[8,256,256]{2,1,0:T(8,128)(2,1)} copy-done((bf16[8,256,256]{2,1,0:T(8,128)(2,1)}, bf16[8,256,256]{2,1,0:T(8,128)(2,1)S(1)}, u32[]{:S(2)}) %copy-start.1) | copy-done | bytes 1048600
  15.3 5.5 %all-to-all-start.1 = ((bf16[8,256,256]{2,1,0:T(8,128)(2,1)}), bf16[8,256,256]{2,1,0:T(8,128)(2,1)}, u32[]{:S(2)}, u32[]{:S(2)}) async-start(bf16[8,256,256]{2,1,0:T(8,128)(2,1)} %copy-done.1), calls=%async_computation.1 | async-start | bytes 2097152 | tf_op jit(solution)/shard_map/all_to_all | solution.py:232
  20.8 19.0 %all_gather.3.refs_0_ = bf16[1024,128]{1,0:T(8,128)(2,1)S(1)} all-gather(bf16[256,128]{1,0:T(8,128)(2,1)S(1)} %get-tuple-element.12), channel_id=1, replica_groups=mesh['xa'=2,'xb'=2,'yl'=2,'zh'=4,'zl'=2,'core'=2,'tp'=4] {'zh'}, dimensions={0}, use_global_device_ids=true | all-gather | bytes 327680 | tf_op jit(solution)/shard_map/all_gather | solution.py:233
  39.8 0.0 all-to-all-done.1
  39.8 4.1 %shard_map.48 = bf16[1024,128]{1,0:T(8,128)(2,1)S(1)} custom-call(bf16[1024,128]{1,0:T(8,128)(2,1)S(1)} %all_gather.3.refs_0_, bf16[2048,256]{1,0:T(8,128)(2,1)} %bitcast.1.refs_1_), custom_call_target="tpu_custom_call" | custom-call | tf_op jit(solution)/shard_map/pallas_call | solution.py:130
  43.9 16.3 %all_to_all.16 = bf16[16,64,128]{2,1,0:T(8,128)(2,1)S(1)} all-to-all(bf16[16,64,128]{2,1,0:T(8,128)(2,1)S(1)} %bitcast.4), channel_id=1, replica_groups=mesh['xa'=2,'xb'=2,'yl'=2,'zh'=4,'zl'=2,'core'=2,'tp'=4] {'zh','xa','zl'}, dimensions={0} | all-to-all | bytes 524288 | tf_op jit(solution)/shard_map/all_to_all | solution.py:235
  60.2 0.0 copy-done
  60.2 0.6 shard_map.49
  60.8 3.8 %collective-permute-start = (bf16[64,896]{1,0:T(8,128)(2,1)S(1)}, bf16[64,896]{1,0:T(8,128)(2,1)S(1)}, u32[]{:S(2)}, u32[]{:S(2)}) collective-permute-start(bf16[64,896]{1,0:T(8,128)(2,1)S(1)} %get-tuple-element.16), channel_id=1, source_target_pairs={{0,2},{1,3},{2,0},{3,1},{4,6},{5,7},{6,4},{7,5},{8,10},{9,11},{10,... | collective-permute-start | bytes 344072 | tf_op jit(solution)/shard_map/ppermute | solution.py:218
  64.7 0.5 shard_map.50
  65.2 5.7 %collective-permute-start.1 = (bf16[64,896]{1,0:T(8,128)(2,1)S(1)}, bf16[64,896]{1,0:T(8,128)(2,1)S(1)}, u32[]{:S(2)}, u32[]{:S(2)}) collective-permute-start(bf16[64,896]{1,0:T(8,128)(2,1)S(1)} %get-tuple-element.17), channel_id=1, source_target_pairs={{0,1},{1,2},{2,3},{3,0},{4,5},{5,6},{6,7},{7,4},{8,9},{9,10},{10,1... | collective-permute-start | bytes 344072 | tf_op jit(solution)/shard_map/ppermute | solution.py:218
  70.9 1.9 %collective-permute-start.2 = (bf16[64,896]{1,0:T(8,128)(2,1)S(1)}, bf16[64,896]{1,0:T(8,128)(2,1)S(1)}, u32[]{:S(2)}, u32[]{:S(2)}) collective-permute-start(bf16[64,896]{1,0:T(8,128)(2,1)S(1)} %get-tuple-element.18), channel_id=1, source_target_pairs={{0,3},{1,0},{2,1},{3,2},{4,7},{5,4},{6,5},{7,6},{8,11},{9,8},{10,9... | collective-permute-start | bytes 344072 | tf_op jit(solution)/shard_map/ppermute | solution.py:218
  72.8 0.2 collective-permute-done
  73.1 1.0 %collective-permute-done.1 = bf16[64,896]{1,0:T(8,128)(2,1)S(1)} collective-permute-done((bf16[64,896]{1,0:T(8,128)(2,1)S(1)}, bf16[64,896]{1,0:T(8,128)(2,1)S(1)}, u32[]{:S(2)}, u32[]{:S(2)}) %collective-permute-start.1) | collective-permute-done | bytes 114720 | tf_op jit(solution)/shard_map/ppermute | solution.py:218
  74.1 5.6 %collective-permute-done.2 = bf16[64,896]{1,0:T(8,128)(2,1)S(1)} collective-permute-done((bf16[64,896]{1,0:T(8,128)(2,1)S(1)}, bf16[64,896]{1,0:T(8,128)(2,1)S(1)}, u32[]{:S(2)}, u32[]{:S(2)}) %collective-permute-start.2) | collective-permute-done | bytes 114720 | tf_op jit(solution)/shard_map/ppermute | solution.py:218
  79.7 0.7 add_convert_fusion
Async XLA Ops:
  0.0 60.2 %copy-start = (bf16[448,3584]{1,0:T(8,128)(2,1)S(1)}, bf16[448,3584]{1,0:T(8,128)(2,1)}, u32[]{:S(2)}) copy-start(bf16[448,3584]{1,0:T(8,128)(2,1)} %weight_ref.3) | copy-start | bytes 9633796
  14.3 1.0 %copy-start.1 = (bf16[8,256,256]{2,1,0:T(8,128)(2,1)}, bf16[8,256,256]{2,1,0:T(8,128)(2,1)S(1)}, u32[]{:S(2)}) copy-start(bf16[8,256,256]{2,1,0:T(8,128)(2,1)S(1)} %get-tuple-element.13) | copy-start | bytes 3145732
  15.3 24.5 %all-to-all-start.1 = ((bf16[8,256,256]{2,1,0:T(8,128)(2,1)}), bf16[8,256,256]{2,1,0:T(8,128)(2,1)}, u32[]{:S(2)}, u32[]{:S(2)}) async-start(bf16[8,256,256]{2,1,0:T(8,128)(2,1)} %copy-done.1), calls=%async_computation.1 | async-start | bytes 2097152 | tf_op jit(solution)/shard_map/all_to_all | solution.py:232
  60.8 12.2 %collective-permute-start = (bf16[64,896]{1,0:T(8,128)(2,1)S(1)}, bf16[64,896]{1,0:T(8,128)(2,1)S(1)}, u32[]{:S(2)}, u32[]{:S(2)}) collective-permute-start(bf16[64,896]{1,0:T(8,128)(2,1)S(1)} %get-tuple-element.16), channel_id=1, source_target_pairs={{0,2},{1,3},{2,0},{3,1},{4,6},{5,7},{6,4},{7,5},{8,10},{9,11},{10,... | collective-permute-start | bytes 344072 | tf_op jit(solution)/shard_map/ppermute | solution.py:218
  65.2 8.9 %collective-permute-start.1 = (bf16[64,896]{1,0:T(8,128)(2,1)S(1)}, bf16[64,896]{1,0:T(8,128)(2,1)S(1)}, u32[]{:S(2)}, u32[]{:S(2)}) collective-permute-start(bf16[64,896]{1,0:T(8,128)(2,1)S(1)} %get-tuple-element.17), channel_id=1, source_target_pairs={{0,1},{1,2},{2,3},{3,0},{4,5},{5,6},{6,7},{7,4},{8,9},{9,10},{10,1... | collective-permute-start | bytes 344072 | tf_op jit(solution)/shard_map/ppermute | solution.py:218
  70.9 8.8 %collective-permute-start.2 = (bf16[64,896]{1,0:T(8,128)(2,1)S(1)}, bf16[64,896]{1,0:T(8,128)(2,1)S(1)}, u32[]{:S(2)}, u32[]{:S(2)}) collective-permute-start(bf16[64,896]{1,0:T(8,128)(2,1)S(1)} %get-tuple-element.18), channel_id=1, source_target_pairs={{0,3},{1,0},{2,1},{3,2},{4,7},{5,4},{6,5},{7,6},{8,11},{9,8},{10,9... | collective-permute-start | bytes 344072 | tf_op jit(solution)/shard_map/ppermute | solution.py:218

commit v10 on v9

--- a/solution.py
+++ b/solution.py
@@ -165,21 +165,23 @@
     )
 
 
-def project_far(parts, out_weight, heads, groups, rows, step, tp_size):
+def project_first(parts, out_weight, heads, groups, rows, steps, tp_size):
     features, columns = out_weight.shape
-
-    def body(parts_ref, weight_ref, attention_ref, far_ref):
+    width = columns // tp_size
+
+    def body(parts_ref, weight_ref, attention_ref, *out_refs):
         combine(parts_ref, attention_ref, heads, groups, rows)
-        far_ref[...] = share_of(attention_ref, weight_ref, step, tp_size).astype(far_ref.dtype)
-
-    return pl.pallas_call(
-        body,
-        out_shape=(
-            jax.ShapeDtypeStruct((rows, features), jnp.bfloat16),
-            jax.ShapeDtypeStruct((rows, columns // tp_size), jnp.bfloat16),
-        ),
+        for step, out_ref in zip(steps, out_refs):
+            out_ref[...] = share_of(attention_ref, weight_ref, step, tp_size).astype(
+                out_ref.dtype
+            )
+
+    return pl.pallas_call(
+        body,
+        out_shape=[jax.ShapeDtypeStruct((rows, features), jnp.bfloat16)]
+        + [jax.ShapeDtypeStruct((rows, width), jnp.bfloat16) for _ in steps],
         cost_estimate=pl.CostEstimate(
-            flops=2 * rows * features * columns // tp_size,
+            flops=2 * rows * features * width * len(steps),
             bytes_accessed=2 * features * columns,
             transcendentals=0,
         ),
@@ -187,7 +189,7 @@
     )(parts, out_weight)
 
 
-def project_near(attention, out_weight, steps, tp_size):
+def project_rest(attention, out_weight, steps, tp_size):
     rows, features = attention.shape
     columns = out_weight.shape[1]
 
@@ -237,12 +239,12 @@
     )
     far = tp_size // 2
     near = [step for step in range(1, tp_size) if step != far]
-    attention, far_share = project_far(
-        returned.reshape(-1, LANES), out_weight, heads, groups, rows, far, tp_size
-    )
-    arrived = [to_member(far_share, far, tp_size)]
-    *near_shares, own_share = project_near(attention, out_weight, near + [0], tp_size)
-    arrived += [to_member(share, step, tp_size) for share, step in zip(near_shares, near)]
+    attention, *near_shares = project_first(
+        returned.reshape(-1, LANES), out_weight, heads, groups, rows, near, tp_size
+    )
+    arrived = [to_member(share, step, tp_size) for share, step in zip(near_shares, near)]
+    far_share, own_share = project_rest(attention, out_weight, [far, 0], tp_size)
+    arrived.append(to_member(far_share, far, tp_size))
     total = own_share
     for share in arrived:
         total = total + share.astype(jnp.float32)

time: 80.7 us -> 81.8 us (1.014)
  waiting for transfers between devices: 6.87 us -> 7.99 us
    ppermute x3, waiting for transfers between devices: 6.87 us -> 7.99 us  [to_member(): lax.ppermute(share, 'tp', [(i, (i + step) % tp_size) for i in range(tp_si...]
  transfers between devices with their start and end apart: 4 -> 4, of which waited for: 3 -> 2; matrix products, arithmetic and copies ran while one was open for 0% -> 0% of each run, Pallas kernels for 1% -> 0%
where the time goes in v10:
time: 81.8 us; the launch traced here: 81.5 us
  blocking collectives  48.3 us (59%)
  starting transfers between devices  16.9 us (21%)
  waiting for transfers between devices  7.99 us (10%)
  Pallas kernels  5.41 us (7%)
  other arithmetic  1.77 us (2%)
  local copies, waits for them, and re-layouts  1.02 us (1%)
    all_gather x1, blocking collectives, shards(): got_q = lax.all_gather(own_q, 'zh', axis=0, tiled=True)  19 us
    all_to_all x1, blocking collectives, shards(): lax.all_to_all(partial.reshape(groups * heads, rows, LANES), RETURN_AXES,...  16.3 us
    all_to_all x1, blocking collectives, shards(): lax.all_to_all(pack(queries, keys, values, heads), HEAD_AXES, 0, 0, tiled...  13 us
    ppermute x3, starting transfers between devices, to_member(): lax.ppermute(share, 'tp', [(i, (i + step) % tp_size) for i in range(tp_si...  11.4 us
    ppermute x3, waiting for transfers between devices, to_member(): lax.ppermute(share, 'tp', [(i, (i + step) % tp_size) for i in range(tp_si...  7.99 us
    all_to_all x1, starting transfers between devices, shards(): got_kv = lax.all_to_all(sent_kv, KEY_AXES, 0, 0, tiled=True)  5.47 us
    pallas_call x1, Pallas kernels, attend(): pl.pallas_call(body, out_shape=jax.ShapeDtypeStruct(queries.shape, querie...  4.06 us
  transfers between devices with their start and end apart: 4, of which 2 were waited for; matrix products, arithmetic and copies ran while one was open for 0% of the time, Pallas kernels for 0%

profile of v10, /device:TPU:56, one launch (start us, length us, event | category | flops | bytes accessed | tf_op | source)
XLA Modules:
  0.0 81.5 jit_solution(10089894475937967601)
XLA Ops:
  0.0 0.0 copy-start
  0.0 1.1 %pad_maximum_fusion.held = bf16[192,448]{1,0:T(8,128)(2,1)S(1)} fusion(bf16[64,448]{1,0:T(8,128)(2,1)} %param.4, bf16[64,448]{1,0:T(8,128)(2,1)} %param.6, bf16[64,448]{1,0:T(8,128)(2,1)} %param.5), kind=kLoop, calls=%fused_computation.1 | loop fusion | flops 516096 | bytes 344064 | tf_op jit(solution)/shard_map/concatenate | solution.py:43
  1.1 0.1 shard_map.46
  1.2 13.0 %all_to_all.15 = bf16[4,64,384]{2,1,0:T(8,128)(2,1)S(1)} all-to-all(bf16[4,64,384]{2,1,0:T(8,128)(2,1)S(1)} %shard_map.46), channel_id=1, replica_groups=mesh['xa'=2,'xb'=2,'yl'=2,'zh'=4,'zl'=2,'core'=2,'tp'=4] {'xa','zl'}, dimensions={0} | all-to-all | bytes 393216 | tf_op jit(solution)/shard_map/all_to_all | solution.py:230
  14.2 0.1 shard_map.47
  14.3 0.0 copy-start.1
  14.3 1.0 %copy-done.1 = bf16[8,256,256]{2,1,0:T(8,128)(2,1)} copy-done((bf16[8,256,256]{2,1,0:T(8,128)(2,1)}, bf16[8,256,256]{2,1,0:T(8,128)(2,1)S(1)}, u32[]{:S(2)}) %copy-start.1) | copy-done | bytes 1048600
  15.3 5.5 %all-to-all-start.1 = ((bf16[8,256,256]{2,1,0:T(8,128)(2,1)}), bf16[8,256,256]{2,1,0:T(8,128)(2,1)}, u32[]{:S(2)}, u32[]{:S(2)}) async-start(bf16[8,256,256]{2,1,0:T(8,128)(2,1)} %copy-done.1), calls=%async_computation.1 | async-start | bytes 2097152 | tf_op jit(solution)/shard_map/all_to_all | solution.py:234
  20.8 19.0 %all_gather.3.refs_0_ = bf16[1024,128]{1,0:T(8,128)(2,1)S(1)} all-gather(bf16[256,128]{1,0:T(8,128)(2,1)S(1)} %get-tuple-element.12), channel_id=1, replica_groups=mesh['xa'=2,'xb'=2,'yl'=2,'zh'=4,'zl'=2,'core'=2,'tp'=4] {'zh'}, dimensions={0}, use_global_device_ids=true | all-gather | bytes 327680 | tf_op jit(solution)/shard_map/all_gather | solution.py:235
  39.8 0.0 all-to-all-done.1
  39.8 4.1 %shard_map.48 = bf16[1024,128]{1,0:T(8,128)(2,1)S(1)} custom-call(bf16[1024,128]{1,0:T(8,128)(2,1)S(1)} %all_gather.3.refs_0_, bf16[2048,256]{1,0:T(8,128)(2,1)} %bitcast.1.refs_1_), custom_call_target="tpu_custom_call" | custom-call | tf_op jit(solution)/shard_map/pallas_call | solution.py:130
  43.9 16.3 %all_to_all.16 = bf16[16,64,128]{2,1,0:T(8,128)(2,1)S(1)} all-to-all(bf16[16,64,128]{2,1,0:T(8,128)(2,1)S(1)} %bitcast.4), channel_id=1, replica_groups=mesh['xa'=2,'xb'=2,'yl'=2,'zh'=4,'zl'=2,'core'=2,'tp'=4] {'zh','xa','zl'}, dimensions={0} | all-to-all | bytes 524288 | tf_op jit(solution)/shard_map/all_to_all | solution.py:237
  60.2 0.0 copy-done
  60.2 0.7 shard_map.49
  61.0 1.9 %collective-permute-start = (bf16[64,896]{1,0:T(8,128)(2,1)S(1)}, bf16[64,896]{1,0:T(8,128)(2,1)S(1)}, u32[]{:S(2)}, u32[]{:S(2)}) collective-permute-start(bf16[64,896]{1,0:T(8,128)(2,1)S(1)} %get-tuple-element.16), channel_id=1, source_target_pairs={{0,1},{1,2},{2,3},{3,0},{4,5},{5,6},{6,7},{7,4},{8,9},{9,10},{10,1... | collective-permute-start | bytes 344072 | tf_op jit(solution)/shard_map/ppermute | solution.py:220
  62.9 4.8 %collective-permute-start.1 = (bf16[64,896]{1,0:T(8,128)(2,1)S(1)}, bf16[64,896]{1,0:T(8,128)(2,1)S(1)}, u32[]{:S(2)}, u32[]{:S(2)}) collective-permute-start(bf16[64,896]{1,0:T(8,128)(2,1)S(1)} %get-tuple-element.17), channel_id=1, source_target_pairs={{0,3},{1,0},{2,1},{3,2},{4,7},{5,4},{6,5},{7,6},{8,11},{9,8},{10,9... | collective-permute-start | bytes 344072 | tf_op jit(solution)/shard_map/ppermute | solution.py:220
  67.7 0.4 shard_map.50
  68.1 4.7 %collective-permute-start.2 = (bf16[64,896]{1,0:T(8,128)(2,1)S(1)}, bf16[64,896]{1,0:T(8,128)(2,1)S(1)}, u32[]{:S(2)}, u32[]{:S(2)}) collective-permute-start(bf16[64,896]{1,0:T(8,128)(2,1)S(1)} %get-tuple-element.18), channel_id=1, source_target_pairs={{0,2},{1,3},{2,0},{3,1},{4,6},{5,7},{6,4},{7,5},{8,10},{9,11},{10,... | collective-permute-start | bytes 344072 | tf_op jit(solution)/shard_map/ppermute | solution.py:220
  72.8 0.0 collective-permute-done
  72.8 0.1 collective-permute-done.1
  72.9 7.9 %collective-permute-done.2 = bf16[64,896]{1,0:T(8,128)(2,1)S(1)} collective-permute-done((bf16[64,896]{1,0:T(8,128)(2,1)S(1)}, bf16[64,896]{1,0:T(8,128)(2,1)S(1)}, u32[]{:S(2)}, u32[]{:S(2)}) %collective-permute-start.2) | collective-permute-done | bytes 114720 | tf_op jit(solution)/shard_map/ppermute | solution.py:220
  80.8 0.7 add_convert_fusion
Async XLA Ops:
  0.0 60.2 %copy-start = (bf16[448,3584]{1,0:T(8,128)(2,1)S(1)}, bf16[448,3584]{1,0:T(8,128)(2,1)}, u32[]{:S(2)}) copy-start(bf16[448,3584]{1,0:T(8,128)(2,1)} %weight_ref.3) | copy-start | bytes 9633796
  14.3 1.0 %copy-start.1 = (bf16[8,256,256]{2,1,0:T(8,128)(2,1)}, bf16[8,256,256]{2,1,0:T(8,128)(2,1)S(1)}, u32[]{:S(2)}) copy-start(bf16[8,256,256]{2,1,0:T(8,128)(2,1)S(1)} %get-tuple-element.13) | copy-start | bytes 3145732
  15.3 24.5 %all-to-all-start.1 = ((bf16[8,256,256]{2,1,0:T(8,128)(2,1)}), bf16[8,256,256]{2,1,0:T(8,128)(2,1)}, u32[]{:S(2)}, u32[]{:S(2)}) async-start(bf16[8,256,256]{2,1,0:T(8,128)(2,1)} %copy-done.1), calls=%async_computation.1 | async-start | bytes 2097152 | tf_op jit(solution)/shard_map/all_to_all | solution.py:234
  61.0 11.9 %collective-permute-start = (bf16[64,896]{1,0:T(8,128)(2,1)S(1)}, bf16[64,896]{1,0:T(8,128)(2,1)S(1)}, u32[]{:S(2)}, u32[]{:S(2)}) collective-permute-start(bf16[64,896]{1,0:T(8,128)(2,1)S(1)} %get-tuple-element.16), channel_id=1, source_target_pairs={{0,1},{1,2},{2,3},{3,0},{4,5},{5,6},{6,7},{7,4},{8,9},{9,10},{10,1... | collective-permute-start | bytes 344072 | tf_op jit(solution)/shard_map/ppermute | solution.py:220
  62.9 10.0 %collective-permute-start.1 = (bf16[64,896]{1,0:T(8,128)(2,1)S(1)}, bf16[64,896]{1,0:T(8,128)(2,1)S(1)}, u32[]{:S(2)}, u32[]{:S(2)}) collective-permute-start(bf16[64,896]{1,0:T(8,128)(2,1)S(1)} %get-tuple-element.17), channel_id=1, source_target_pairs={{0,3},{1,0},{2,1},{3,2},{4,7},{5,4},{6,5},{7,6},{8,11},{9,8},{10,9... | collective-permute-start | bytes 344072 | tf_op jit(solution)/shard_map/ppermute | solution.py:220
  68.1 12.7 %collective-permute-start.2 = (bf16[64,896]{1,0:T(8,128)(2,1)S(1)}, bf16[64,896]{1,0:T(8,128)(2,1)S(1)}, u32[]{:S(2)}, u32[]{:S(2)}) collective-permute-start(bf16[64,896]{1,0:T(8,128)(2,1)S(1)} %get-tuple-element.18), channel_id=1, source_target_pairs={{0,2},{1,3},{2,0},{3,1},{4,6},{5,7},{6,4},{7,5},{8,10},{9,11},{10,... | collective-permute-start | bytes 344072 | tf_op jit(solution)/shard_map/ppermute | solution.py:220

commit v11 on v9

--- a/solution.py
+++ b/solution.py
@@ -9,6 +9,7 @@
 
 HEAD_DIM = 112
 LANES = 128
+ZH_STEP = 2
 TOTAL, TOTAL_LOW, SHIFT = HEAD_DIM, HEAD_DIM + 1, HEAD_DIM + 2
 NEG_FILL = -1e30
 NEG_CLAMP = -1e29
@@ -63,22 +64,28 @@
     )(one_head)
 
 
-def attend_kernel(rows, q_ref, kv_ref, out_ref, key_ref, value_ref):
+def attend_kernel(rows, zh_step, q_ref, kv_hbm, out_ref, kv_ref, arrived):
     xb, yl, zh, core = (lax.axis_index(name) for name in ("xb", "yl", "zh", "core"))
     pair = 2 * rows
     block = 2 * pair
     coarse = 4 * block
-    sources = kv_ref.shape[0] // block
+    zh_size = q_ref.shape[0]
+    sources = kv_hbm.shape[0]
     half = sources * pair
-    for xa_at in range(2):
-        for source in range(sources):
-            start = source * block + xa_at * pair
-            to_rows = slice(xa_at * half + source * pair, xa_at * half + (source + 1) * pair)
-            key_ref[to_rows, :] = kv_ref[start : start + pair, :LANES]
-            value_ref[to_rows, :] = kv_ref[start : start + pair, LANES:]
-    query_at = lax.broadcasted_iota(jnp.int32, (block, half), 0)
+    loads = [
+        pltpu.make_async_copy(
+            kv_hbm.at[:, xa_at * pair : (xa_at + 1) * pair, :],
+            kv_ref.at[xa_at],
+            arrived.at[xa_at],
+        )
+        for xa_at in range(2)
+    ]
+    for load in loads:
+        load.start()
+    tile = zh_step * pair
+    query_at = lax.broadcasted_iota(jnp.int32, (tile, half), 0)
     query_at = (query_at // pair) * block + query_at % pair + (query_at // rows % 2) * rows
-    key_at = lax.broadcasted_iota(jnp.int32, (block, half), 1)
+    key_at = lax.broadcasted_iota(jnp.int32, (tile, half), 1)
     source_at = key_at // pair
     key_at = (
         (source_at // 2) * coarse
@@ -87,50 +94,52 @@
         + (key_at // rows % 2) * rows
     )
     distance = query_at - key_at + (xb * 2 + yl) * coarse + core * rows - zh * block
-    lane = lax.broadcasted_iota(jnp.int32, (block, LANES), 1)
-    for zh_at in range(0, q_ref.shape[0] // block, 2):
-        kept = distance + zh_at * block >= 0
-        for xa_at in range(2):
-            total = (xa_at + 1) * half
-            known = total - half
-            starts = [(zh_at + after) * block + xa_at * pair for after in range(2)]
-            queries = jnp.concatenate(
-                [q_ref[start : start + pair, :] for start in starts], axis=0
-            )
-            scores = lax.dot_general(
-                queries,
-                key_ref[:total, :],
-                (((1,), (1,)), ((), ())),
-                preferred_element_type=jnp.float32,
-            )
-            last = jnp.where(kept, scores[:, known:], NEG_FILL)
-            if known:
-                scores = jnp.concatenate([scores[:, :known], last], axis=1)
-            else:
-                scores = last
-            top = jnp.maximum(jnp.max(scores, axis=1, keepdims=True), NEG_CLAMP)
+    lane = lax.broadcasted_iota(jnp.int32, (tile, LANES), 1)
+    for xa_at in range(2):
+        loads[xa_at].wait()
+        keys = [kv_ref[at, :, :, :LANES].reshape(half, LANES) for at in range(xa_at + 1)]
+        values = [kv_ref[at, :, :, LANES:].reshape(half, LANES) for at in range(xa_at + 1)]
+        for zh_at in range(0, zh_size, zh_step):
+            own = (slice(zh_at, zh_at + zh_step), slice(xa_at * pair, (xa_at + 1) * pair))
+            queries = q_ref[own].reshape(tile, LANES)
+            scores = [
+                lax.dot_general(
+                    queries, key, (((1,), (1,)), ((), ())), preferred_element_type=jnp.float32
+                )
+                for key in keys
+            ]
+            scores[-1] = jnp.where(distance + zh_at * block >= 0, scores[-1], NEG_FILL)
+            top = jnp.max(scores[0], axis=1, keepdims=True)
+            for score in scores[1:]:
+                top = jnp.maximum(top, jnp.max(score, axis=1, keepdims=True))
+            top = jnp.maximum(top, NEG_CLAMP)
             shift = (top * EXP2_SCALE).astype(jnp.bfloat16).astype(jnp.float32)
-            weights = jnp.exp2(scores * EXP2_SCALE - shift)
-            weighted = jnp.dot(
-                weights.astype(jnp.bfloat16),
-                value_ref[:total, :],
-                preferred_element_type=jnp.float32,
-            )
+            weighted = jnp.zeros((tile, LANES), jnp.float32)
+            for score, value in zip(scores, values):
+                weights = jnp.exp2(score * EXP2_SCALE - shift).astype(jnp.bfloat16)
+                weighted = weighted + jnp.dot(
+                    weights, value, preferred_element_type=jnp.float32
+                )
             rounded = weighted.astype(jnp.bfloat16).astype(jnp.float32)
             weighted = jnp.where(lane == TOTAL_LOW, weighted - rounded, weighted)
             weighted = jnp.where(lane == SHIFT, shift, weighted).astype(out_ref.dtype)
-            for after, start in enumerate(starts):
-                out_ref[start : start + pair, :] = weighted[after * pair : (after + 1) * pair]
-
-
-def attend(queries, keys_values, rows):
+            out_ref[own] = weighted.reshape(zh_step, pair, LANES)
+
+
+def attend(queries, keys_values, rows, zh_step):
+    sources, block, width = keys_values.shape
+
     def body(*refs):
-        attend_kernel(rows, *refs)
-
-    return pl.pallas_call(
-        body,
+        attend_kernel(rows, zh_step, *refs)
+
+    return pl.pallas_call(
+        body,
+        in_specs=[pl.BlockSpec(memory_space=pltpu.VMEM), pl.BlockSpec(memory_space=pl.ANY)],
         out_shape=jax.ShapeDtypeStruct(queries.shape, queries.dtype),
-        scratch_shapes=[pltpu.VMEM((keys_values.shape[0], LANES), queries.dtype)] * 2,
+        scratch_shapes=[
+            pltpu.VMEM((2, sources, block // 2, width), queries.dtype),
+            pltpu.SemaphoreType.DMA((2,)),
+        ],
         compiler_params=pltpu.CompilerParams(vmem_limit_bytes=VMEM_LIMIT),
     )(queries, keys_values)
 
@@ -231,7 +240,8 @@
     own_q, sent_kv = spread(one_head, key_copies)
     got_kv = lax.all_to_all(sent_kv, KEY_AXES, 0, 0, tiled=True)
     got_q = lax.all_gather(own_q, "zh", axis=0, tiled=True)
-    partial = attend(got_q, got_kv.reshape(-1, 2 * LANES), rows)
+    got_q = got_q.reshape(groups, heads * rows, LANES)
+    partial = attend(got_q, got_kv, rows, ZH_STEP)
     returned = lax.all_to_all(
         partial.reshape(groups * heads, rows, LANES), RETURN_AXES, 0, 0, tiled=True
     )

time: 80.7 us -> 80.7 us (level)
  no operation moved by 1% of the time
where the time goes in v11:
time: 80.7 us; the launch traced here: 80.4 us
  blocking collectives  48.3 us (60%)
  starting transfers between devices  16.9 us (21%)
  waiting for transfers between devices  6.87 us (9%)
  Pallas kernels  5.4 us (7%)
  other arithmetic  1.77 us (2%)
  local copies, waits for them, and re-layouts  1.02 us (1%)
    all_gather x1, blocking collectives, shards(): got_q = lax.all_gather(own_q, 'zh', axis=0, tiled=True)  19 us
    all_to_all x1, blocking collectives, shards(): lax.all_to_all(partial.reshape(groups * heads, rows, LANES), RETURN_AXES,...  16.3 us
    all_to_all x1, blocking collectives, shards(): lax.all_to_all(pack(queries, keys, values, heads), HEAD_AXES, 0, 0, tiled...  13 us
    ppermute x3, starting transfers between devices, to_member(): lax.ppermute(share, 'tp', [(i, (i + step) % tp_size) for i in range(tp_si...  11.4 us
    ppermute x3, waiting for transfers between devices, to_member(): lax.ppermute(share, 'tp', [(i, (i + step) % tp_size) for i in range(tp_si...  6.87 us
    all_to_all x1, starting transfers between devices, shards(): got_kv = lax.all_to_all(sent_kv, KEY_AXES, 0, 0, tiled=True)  5.47 us
    pallas_call x1, Pallas kernels, attend(): pl.pallas_call(body, in_specs=[pl.BlockSpec(memory_space=pltpu.VMEM), pl....  4.03 us
  transfers between devices with their start and end apart: 4, of which 3 were waited for; matrix products, arithmetic and copies ran while one was open for 0% of the time, Pallas kernels for 1%

profile of v11, /device:TPU:56, one launch (start us, length us, event | category | flops | bytes accessed | tf_op | source)
XLA Modules:
  0.0 80.4 jit_solution(3979406958674430759)
XLA Ops:
  0.0 0.0 copy-start
  0.0 1.1 %pad_maximum_fusion.held = bf16[192,448]{1,0:T(8,128)(2,1)S(1)} fusion(bf16[64,448]{1,0:T(8,128)(2,1)} %param.4, bf16[64,448]{1,0:T(8,128)(2,1)} %param.6, bf16[64,448]{1,0:T(8,128)(2,1)} %param.5), kind=kLoop, calls=%fused_computation.1 | loop fusion | flops 516096 | bytes 344064 | tf_op jit(solution)/shard_map/concatenate | solution.py:44
  1.1 0.1 shard_map.46
  1.2 13.0 %all_to_all.15 = bf16[4,64,384]{2,1,0:T(8,128)(2,1)S(1)} all-to-all(bf16[4,64,384]{2,1,0:T(8,128)(2,1)S(1)} %shard_map.46), channel_id=1, replica_groups=mesh['xa'=2,'xb'=2,'yl'=2,'zh'=4,'zl'=2,'core'=2,'tp'=4] {'xa','zl'}, dimensions={0} | all-to-all | bytes 393216 | tf_op jit(solution)/shard_map/all_to_all | solution.py:237
  14.2 0.1 shard_map.47
  14.3 0.0 copy-start.1
  14.3 1.0 %copy-done.1 = bf16[8,256,256]{2,1,0:T(8,128)(2,1)} copy-done((bf16[8,256,256]{2,1,0:T(8,128)(2,1)}, bf16[8,256,256]{2,1,0:T(8,128)(2,1)S(1)}, u32[]{:S(2)}) %copy-start.1) | copy-done | bytes 1048600
  15.3 5.5 %all-to-all-start.1 = ((bf16[8,256,256]{2,1,0:T(8,128)(2,1)}), bf16[8,256,256]{2,1,0:T(8,128)(2,1)}, u32[]{:S(2)}, u32[]{:S(2)}) async-start(bf16[8,256,256]{2,1,0:T(8,128)(2,1)} %copy-done.1), calls=%async_computation.1 | async-start | bytes 2097152 | tf_op jit(solution)/shard_map/all_to_all | solution.py:241
  20.8 19.0 %all_gather.3 = bf16[1024,128]{1,0:T(8,128)(2,1)S(1)} all-gather(bf16[256,128]{1,0:T(8,128)(2,1)S(1)} %get-tuple-element.12), channel_id=1, replica_groups=mesh['xa'=2,'xb'=2,'yl'=2,'zh'=4,'zl'=2,'core'=2,'tp'=4] {'zh'}, dimensions={0}, use_global_device_ids=true | all-gather | bytes 327680 | tf_op jit(solution)/shard_map/all_gather | solution.py:242
  39.8 0.0 all-to-all-done.1.refs_1_
  39.8 4.0 %shard_map.48 = bf16[4,256,128]{2,1,0:T(8,128)(2,1)S(1)} custom-call(bf16[4,256,128]{2,1,0:T(8,128)(2,1)S(1)} %bitcast.4, bf16[8,256,256]{2,1,0:T(8,128)(2,1)} %all-to-all-done.1.refs_1_), custom_call_target="tpu_custom_call" | custom-call | tf_op jit(solution)/shard_map/pallas_call | solution.py:135
  43.8 16.3 %all_to_all.16 = bf16[16,64,128]{2,1,0:T(8,128)(2,1)S(1)} all-to-all(bf16[16,64,128]{2,1,0:T(8,128)(2,1)S(1)} %bitcast.5), channel_id=1, replica_groups=mesh['xa'=2,'xb'=2,'yl'=2,'zh'=4,'zl'=2,'core'=2,'tp'=4] {'zh','xa','zl'}, dimensions={0} | all-to-all | bytes 524288 | tf_op jit(solution)/shard_map/all_to_all | solution.py:245
  60.2 0.0 copy-done
  60.2 0.6 shard_map.49
  60.8 3.8 %collective-permute-start = (bf16[64,896]{1,0:T(8,128)(2,1)S(1)}, bf16[64,896]{1,0:T(8,128)(2,1)S(1)}, u32[]{:S(2)}, u32[]{:S(2)}) collective-permute-start(bf16[64,896]{1,0:T(8,128)(2,1)S(1)} %get-tuple-element.16), channel_id=1, source_target_pairs={{0,2},{1,3},{2,0},{3,1},{4,6},{5,7},{6,4},{7,5},{8,10},{9,11},{10,... | collective-permute-start | bytes 344072 | tf_op jit(solution)/shard_map/ppermute | solution.py:227
  64.6 0.5 shard_map.50
  65.2 5.7 %collective-permute-start.1 = (bf16[64,896]{1,0:T(8,128)(2,1)S(1)}, bf16[64,896]{1,0:T(8,128)(2,1)S(1)}, u32[]{:S(2)}, u32[]{:S(2)}) collective-permute-start(bf16[64,896]{1,0:T(8,128)(2,1)S(1)} %get-tuple-element.17), channel_id=1, source_target_pairs={{0,1},{1,2},{2,3},{3,0},{4,5},{5,6},{6,7},{7,4},{8,9},{9,10},{10,1... | collective-permute-start | bytes 344072 | tf_op jit(solution)/shard_map/ppermute | solution.py:227
  70.9 1.9 %collective-permute-start.2 = (bf16[64,896]{1,0:T(8,128)(2,1)S(1)}, bf16[64,896]{1,0:T(8,128)(2,1)S(1)}, u32[]{:S(2)}, u32[]{:S(2)}) collective-permute-start(bf16[64,896]{1,0:T(8,128)(2,1)S(1)} %get-tuple-element.18), channel_id=1, source_target_pairs={{0,3},{1,0},{2,1},{3,2},{4,7},{5,4},{6,5},{7,6},{8,11},{9,8},{10,9... | collective-permute-start | bytes 344072 | tf_op jit(solution)/shard_map/ppermute | solution.py:227
  72.8 0.3 collective-permute-done
  73.1 1.0 %collective-permute-done.1 = bf16[64,896]{1,0:T(8,128)(2,1)S(1)} collective-permute-done((bf16[64,896]{1,0:T(8,128)(2,1)S(1)}, bf16[64,896]{1,0:T(8,128)(2,1)S(1)}, u32[]{:S(2)}, u32[]{:S(2)}) %collective-permute-start.1) | collective-permute-done | bytes 114720 | tf_op jit(solution)/shard_map/ppermute | solution.py:227
  74.0 5.6 %collective-permute-done.2 = bf16[64,896]{1,0:T(8,128)(2,1)S(1)} collective-permute-done((bf16[64,896]{1,0:T(8,128)(2,1)S(1)}, bf16[64,896]{1,0:T(8,128)(2,1)S(1)}, u32[]{:S(2)}, u32[]{:S(2)}) %collective-permute-start.2) | collective-permute-done | bytes 114720 | tf_op jit(solution)/shard_map/ppermute | solution.py:227
  79.7 0.7 add_convert_fusion
Async XLA Ops:
  0.0 60.2 %copy-start = (bf16[448,3584]{1,0:T(8,128)(2,1)S(1)}, bf16[448,3584]{1,0:T(8,128)(2,1)}, u32[]{:S(2)}) copy-start(bf16[448,3584]{1,0:T(8,128)(2,1)} %weight_ref.3) | copy-start | bytes 9633796
  14.3 1.0 %copy-start.1 = (bf16[8,256,256]{2,1,0:T(8,128)(2,1)}, bf16[8,256,256]{2,1,0:T(8,128)(2,1)S(1)}, u32[]{:S(2)}) copy-start(bf16[8,256,256]{2,1,0:T(8,128)(2,1)S(1)} %get-tuple-element.13) | copy-start | bytes 3145732
  15.3 24.5 %all-to-all-start.1 = ((bf16[8,256,256]{2,1,0:T(8,128)(2,1)}), bf16[8,256,256]{2,1,0:T(8,128)(2,1)}, u32[]{:S(2)}, u32[]{:S(2)}) async-start(bf16[8,256,256]{2,1,0:T(8,128)(2,1)} %copy-done.1), calls=%async_computation.1 | async-start | bytes 2097152 | tf_op jit(solution)/shard_map/all_to_all | solution.py:241
  60.8 12.2 %collective-permute-start = (bf16[64,896]{1,0:T(8,128)(2,1)S(1)}, bf16[64,896]{1,0:T(8,128)(2,1)S(1)}, u32[]{:S(2)}, u32[]{:S(2)}) collective-permute-start(bf16[64,896]{1,0:T(8,128)(2,1)S(1)} %get-tuple-element.16), channel_id=1, source_target_pairs={{0,2},{1,3},{2,0},{3,1},{4,6},{5,7},{6,4},{7,5},{8,10},{9,11},{10,... | collective-permute-start | bytes 344072 | tf_op jit(solution)/shard_map/ppermute | solution.py:227
  65.2 8.9 %collective-permute-start.1 = (bf16[64,896]{1,0:T(8,128)(2,1)S(1)}, bf16[64,896]{1,0:T(8,128)(2,1)S(1)}, u32[]{:S(2)}, u32[]{:S(2)}) collective-permute-start(bf16[64,896]{1,0:T(8,128)(2,1)S(1)} %get-tuple-element.17), channel_id=1, source_target_pairs={{0,1},{1,2},{2,3},{3,0},{4,5},{5,6},{6,7},{7,4},{8,9},{9,10},{10,1... | collective-permute-start | bytes 344072 | tf_op jit(solution)/shard_map/ppermute | solution.py:227
  70.9 8.8 %collective-permute-start.2 = (bf16[64,896]{1,0:T(8,128)(2,1)S(1)}, bf16[64,896]{1,0:T(8,128)(2,1)S(1)}, u32[]{:S(2)}, u32[]{:S(2)}) collective-permute-start(bf16[64,896]{1,0:T(8,128)(2,1)S(1)} %get-tuple-element.18), channel_id=1, source_target_pairs={{0,3},{1,0},{2,1},{3,2},{4,7},{5,4},{6,5},{7,6},{8,11},{9,8},{10,9... | collective-permute-start | bytes 344072 | tf_op jit(solution)/shard_map/ppermute | solution.py:227

commit v12 on v9

--- a/solution.py
+++ b/solution.py
@@ -236,7 +236,7 @@
         partial.reshape(groups * heads, rows, LANES), RETURN_AXES, 0, 0, tiled=True
     )
     far = tp_size // 2
-    near = [step for step in range(1, tp_size) if step != far]
+    near = [step for step in range(tp_size - 1, 0, -1) if step != far]
     attention, far_share = project_far(
         returned.reshape(-1, LANES), out_weight, heads, groups, rows, far, tp_size
     )

time: 80.7 us -> 81.2 us (level)
  the two profiles are of different devices: /device:TPU:56 before, /device:TPU:64 now
where the time goes in v12:
time: 81.2 us; the launch traced here: 80.8 us
  blocking collectives  48.3 us (59%)
  starting transfers between devices  18.7 us (23%)
  waiting for transfers between devices  5.52 us (7%)
  Pallas kernels  5.43 us (7%)
  other arithmetic  1.77 us (2%)
  local copies, waits for them, and re-layouts  1.02 us (1%)
    all_to_all x1, blocking collectives, shards(): lax.all_to_all(partial.reshape(groups * heads, rows, LANES), RETURN_AXES,...  17.9 us
    all_gather x1, blocking collectives, shards(): got_q = lax.all_gather(own_q, 'zh', axis=0, tiled=True)  17.2 us
    ppermute x3, starting transfers between devices, to_member(): lax.ppermute(share, 'tp', [(i, (i + step) % tp_size) for i in range(tp_si...  14.5 us
    all_to_all x1, blocking collectives, shards(): lax.all_to_all(pack(queries, keys, values, heads), HEAD_AXES, 0, 0, tiled...  13.2 us
    ppermute x3, waiting for transfers between devices, to_member(): lax.ppermute(share, 'tp', [(i, (i + step) % tp_size) for i in range(tp_si...  5.52 us
    all_to_all x1, starting transfers between devices, shards(): got_kv = lax.all_to_all(sent_kv, KEY_AXES, 0, 0, tiled=True)  4.24 us
    pallas_call x1, Pallas kernels, attend(): pl.pallas_call(body, out_shape=jax.ShapeDtypeStruct(queries.shape, querie...  4.06 us
  transfers between devices with their start and end apart: 4, of which 2 were waited for; matrix products, arithmetic and copies ran while one was open for 0% of the time, Pallas kernels for 1%

profile of v12, /device:TPU:64, one launch (start us, length us, event | category | flops | bytes accessed | tf_op | source)
XLA Modules:
  0.0 80.8 jit_solution(9354986090771067025)
XLA Ops:
  0.0 0.0 copy-start
  0.0 1.1 %pad_maximum_fusion.held = bf16[192,448]{1,0:T(8,128)(2,1)S(1)} fusion(bf16[64,448]{1,0:T(8,128)(2,1)} %param.4, bf16[64,448]{1,0:T(8,128)(2,1)} %param.6, bf16[64,448]{1,0:T(8,128)(2,1)} %param.5), kind=kLoop, calls=%fused_computation.1 | loop fusion | flops 516096 | bytes 344064 | tf_op jit(solution)/shard_map/concatenate | solution.py:43
  1.1 0.1 shard_map.46
  1.2 13.2 %all_to_all.15 = bf16[4,64,384]{2,1,0:T(8,128)(2,1)S(1)} all-to-all(bf16[4,64,384]{2,1,0:T(8,128)(2,1)S(1)} %shard_map.46), channel_id=1, replica_groups=mesh['xa'=2,'xb'=2,'yl'=2,'zh'=4,'zl'=2,'core'=2,'tp'=4] {'xa','zl'}, dimensions={0} | all-to-all | bytes 393216 | tf_op jit(solution)/shard_map/all_to_all | solution.py:228
  14.4 0.1 shard_map.47
  14.5 0.0 copy-start.1
  14.5 1.0 %copy-done.1 = bf16[8,256,256]{2,1,0:T(8,128)(2,1)} copy-done((bf16[8,256,256]{2,1,0:T(8,128)(2,1)}, bf16[8,256,256]{2,1,0:T(8,128)(2,1)S(1)}, u32[]{:S(2)}) %copy-start.1) | copy-done | bytes 1048600
  15.5 4.2 %all-to-all-start.1 = ((bf16[8,256,256]{2,1,0:T(8,128)(2,1)}), bf16[8,256,256]{2,1,0:T(8,128)(2,1)}, u32[]{:S(2)}, u32[]{:S(2)}) async-start(bf16[8,256,256]{2,1,0:T(8,128)(2,1)} %copy-done.1), calls=%async_computation.1 | async-start | bytes 2097152 | tf_op jit(solution)/shard_map/all_to_all | solution.py:232
  19.7 17.2 %all_gather.3.refs_0_ = bf16[1024,128]{1,0:T(8,128)(2,1)S(1)} all-gather(bf16[256,128]{1,0:T(8,128)(2,1)S(1)} %get-tuple-element.12), channel_id=1, replica_groups=mesh['xa'=2,'xb'=2,'yl'=2,'zh'=4,'zl'=2,'core'=2,'tp'=4] {'zh'}, dimensions={0}, use_global_device_ids=true | all-gather | bytes 327680 | tf_op jit(solution)/shard_map/all_gather | solution.py:233
  37.0 0.0 all-to-all-done.1
  37.0 4.1 %shard_map.48 = bf16[1024,128]{1,0:T(8,128)(2,1)S(1)} custom-call(bf16[1024,128]{1,0:T(8,128)(2,1)S(1)} %all_gather.3.refs_0_, bf16[2048,256]{1,0:T(8,128)(2,1)} %bitcast.1.refs_1_), custom_call_target="tpu_custom_call" | custom-call | tf_op jit(solution)/shard_map/pallas_call | solution.py:130
  41.0 17.9 %all_to_all.16 = bf16[16,64,128]{2,1,0:T(8,128)(2,1)S(1)} all-to-all(bf16[16,64,128]{2,1,0:T(8,128)(2,1)S(1)} %bitcast.4), channel_id=1, replica_groups=mesh['xa'=2,'xb'=2,'yl'=2,'zh'=4,'zl'=2,'core'=2,'tp'=4] {'zh','xa','zl'}, dimensions={0} | all-to-all | bytes 524288 | tf_op jit(solution)/shard_map/all_to_all | solution.py:235
  58.9 0.0 copy-done
  58.9 0.6 shard_map.49
  59.6 7.7 %collective-permute-start = (bf16[64,896]{1,0:T(8,128)(2,1)S(1)}, bf16[64,896]{1,0:T(8,128)(2,1)S(1)}, u32[]{:S(2)}, u32[]{:S(2)}) collective-permute-start(bf16[64,896]{1,0:T(8,128)(2,1)S(1)} %get-tuple-element.16), channel_id=1, source_target_pairs={{0,2},{1,3},{2,0},{3,1},{4,6},{5,7},{6,4},{7,5},{8,10},{9,11},{10,... | collective-permute-start | bytes 344072 | tf_op jit(solution)/shard_map/ppermute | solution.py:218
  67.3 0.5 shard_map.50
  67.9 2.2 %collective-permute-start.1 = (bf16[64,896]{1,0:T(8,128)(2,1)S(1)}, bf16[64,896]{1,0:T(8,128)(2,1)S(1)}, u32[]{:S(2)}, u32[]{:S(2)}) collective-permute-start(bf16[64,896]{1,0:T(8,128)(2,1)S(1)} %get-tuple-element.17), channel_id=1, source_target_pairs={{0,3},{1,0},{2,1},{3,2},{4,7},{5,4},{6,5},{7,6},{8,11},{9,8},{10,9... | collective-permute-start | bytes 344072 | tf_op jit(solution)/shard_map/ppermute | solution.py:218
  70.1 4.5 %collective-permute-start.2 = (bf16[64,896]{1,0:T(8,128)(2,1)S(1)}, bf16[64,896]{1,0:T(8,128)(2,1)S(1)}, u32[]{:S(2)}, u32[]{:S(2)}) collective-permute-start(bf16[64,896]{1,0:T(8,128)(2,1)S(1)} %get-tuple-element.18), channel_id=1, source_target_pairs={{0,1},{1,2},{2,3},{3,0},{4,5},{5,6},{6,7},{7,4},{8,9},{9,10},{10,1... | collective-permute-start | bytes 344072 | tf_op jit(solution)/shard_map/ppermute | solution.py:218
  74.6 0.0 collective-permute-done
  74.6 3.3 %collective-permute-done.1 = bf16[64,896]{1,0:T(8,128)(2,1)S(1)} collective-permute-done((bf16[64,896]{1,0:T(8,128)(2,1)S(1)}, bf16[64,896]{1,0:T(8,128)(2,1)S(1)}, u32[]{:S(2)}, u32[]{:S(2)}) %collective-permute-start.1) | collective-permute-done | bytes 114720 | tf_op jit(solution)/shard_map/ppermute | solution.py:218
  78.0 2.2 %collective-permute-done.2 = bf16[64,896]{1,0:T(8,128)(2,1)S(1)} collective-permute-done((bf16[64,896]{1,0:T(8,128)(2,1)S(1)}, bf16[64,896]{1,0:T(8,128)(2,1)S(1)}, u32[]{:S(2)}, u32[]{:S(2)}) %collective-permute-start.2) | collective-permute-done | bytes 114720 | tf_op jit(solution)/shard_map/ppermute | solution.py:218
  80.1 0.7 add_convert_fusion
Async XLA Ops:
  0.0 58.9 %copy-start = (bf16[448,3584]{1,0:T(8,128)(2,1)S(1)}, bf16[448,3584]{1,0:T(8,128)(2,1)}, u32[]{:S(2)}) copy-start(bf16[448,3584]{1,0:T(8,128)(2,1)} %weight_ref.3) | copy-start | bytes 9633796
  14.5 1.0 %copy-start.1 = (bf16[8,256,256]{2,1,0:T(8,128)(2,1)}, bf16[8,256,256]{2,1,0:T(8,128)(2,1)S(1)}, u32[]{:S(2)}) copy-start(bf16[8,256,256]{2,1,0:T(8,128)(2,1)S(1)} %get-tuple-element.13) | copy-start | bytes 3145732
  15.5 21.5 %all-to-all-start.1 = ((bf16[8,256,256]{2,1,0:T(8,128)(2,1)}), bf16[8,256,256]{2,1,0:T(8,128)(2,1)}, u32[]{:S(2)}, u32[]{:S(2)}) async-start(bf16[8,256,256]{2,1,0:T(8,128)(2,1)} %copy-done.1), calls=%async_computation.1 | async-start | bytes 2097152 | tf_op jit(solution)/shard_map/all_to_all | solution.py:232
  59.6 15.0 %collective-permute-start = (bf16[64,896]{1,0:T(8,128)(2,1)S(1)}, bf16[64,896]{1,0:T(8,128)(2,1)S(1)}, u32[]{:S(2)}, u32[]{:S(2)}) collective-permute-start(bf16[64,896]{1,0:T(8,128)(2,1)S(1)} %get-tuple-element.16), channel_id=1, source_target_pairs={{0,2},{1,3},{2,0},{3,1},{4,6},{5,7},{6,4},{7,5},{8,10},{9,11},{10,... | collective-permute-start | bytes 344072 | tf_op jit(solution)/shard_map/ppermute | solution.py:218
  67.9 10.1 %collective-permute-start.1 = (bf16[64,896]{1,0:T(8,128)(2,1)S(1)}, bf16[64,896]{1,0:T(8,128)(2,1)S(1)}, u32[]{:S(2)}, u32[]{:S(2)}) collective-permute-start(bf16[64,896]{1,0:T(8,128)(2,1)S(1)} %get-tuple-element.17), channel_id=1, source_target_pairs={{0,3},{1,0},{2,1},{3,2},{4,7},{5,4},{6,5},{7,6},{8,11},{9,8},{10,9... | collective-permute-start | bytes 344072 | tf_op jit(solution)/shard_map/ppermute | solution.py:218
  70.1 10.0 %collective-permute-start.2 = (bf16[64,896]{1,0:T(8,128)(2,1)S(1)}, bf16[64,896]{1,0:T(8,128)(2,1)S(1)}, u32[]{:S(2)}, u32[]{:S(2)}) collective-permute-start(bf16[64,896]{1,0:T(8,128)(2,1)S(1)} %get-tuple-element.18), channel_id=1, source_target_pairs={{0,1},{1,2},{2,3},{3,0},{4,5},{5,6},{6,7},{7,4},{8,9},{9,10},{10,1... | collective-permute-start | bytes 344072 | tf_op jit(solution)/shard_map/ppermute | solution.py:218

commit v13 on v9

--- a/solution.py
+++ b/solution.py
@@ -16,7 +16,7 @@
 CTX = AXES[:6]
 HEAD_AXES = ("xa", "zl")
 KEY_AXES = ("xb", "yl", "core")
-RETURN_AXES = ("zh",) + HEAD_AXES
+RETURN_AXES = ("xa", "zh", "zl")
 VMEM_LIMIT = 48 * 1024 * 1024
 EXP2_SCALE = math.log2(math.e) / HEAD_DIM**0.5
 
@@ -119,8 +119,8 @@
             rounded = weighted.astype(jnp.bfloat16).astype(jnp.float32)
             weighted = jnp.where(lane == TOTAL_LOW, weighted - rounded, weighted)
             weighted = jnp.where(lane == SHIFT, shift, weighted).astype(out_ref.dtype)
-            for after, start in enumerate(starts):
-                out_ref[start : start + pair, :] = weighted[after * pair : (after + 1) * pair]
+            start = xa_at * (q_ref.shape[0] // 2) + zh_at * pair
+            out_ref[start : start + block, :] = weighted
 
 
 def attend(queries, keys_values, rows):
@@ -138,10 +138,8 @@
 def combine(parts_ref, attention_ref, heads, groups, rows):
     for head in range(heads):
         parts = [
-            parts_ref[
-                (group * heads + head) * rows : (group * heads + head + 1) * rows, :
-            ].astype(jnp.float32)
-            for group in range(groups)
+            parts_ref[at * rows : (at + 1) * rows, :].astype(jnp.float32)
+            for at in range(head // 2 * 2 * groups + head % 2, (head // 2 + 1) * 2 * groups, 2)
         ]
         shifts = [part[:, SHIFT : SHIFT + 1] for part in parts]
         top = shifts[0]

time: 80.7 us -> 80.6 us (level)
  no operation moved by 1% of the time
where the time goes in v13:
time: 80.6 us; the launch traced here: 80.3 us
  blocking collectives  48.2 us (60%)
  starting transfers between devices  16.9 us (21%)
  waiting for transfers between devices  6.9 us (9%)
  Pallas kernels  5.43 us (7%)
  other arithmetic  1.77 us (2%)
  local copies, waits for them, and re-layouts  1.02 us (1%)
    all_gather x1, blocking collectives, shards(): got_q = lax.all_gather(own_q, 'zh', axis=0, tiled=True)  19 us
    all_to_all x1, blocking collectives, shards(): lax.all_to_all(partial.reshape(groups * heads, rows, LANES), RETURN_AXES,...  16.2 us
    all_to_all x1, blocking collectives, shards(): lax.all_to_all(pack(queries, keys, values, heads), HEAD_AXES, 0, 0, tiled...  13 us
    ppermute x3, starting transfers between devices, to_member(): lax.ppermute(share, 'tp', [(i, (i + step) % tp_size) for i in range(tp_si...  11.4 us
    ppermute x3, waiting for transfers between devices, to_member(): lax.ppermute(share, 'tp', [(i, (i + step) % tp_size) for i in range(tp_si...  6.89 us
    all_to_all x1, starting transfers between devices, shards(): got_kv = lax.all_to_all(sent_kv, KEY_AXES, 0, 0, tiled=True)  5.47 us
    pallas_call x1, Pallas kernels, attend(): pl.pallas_call(body, out_shape=jax.ShapeDtypeStruct(queries.shape, querie...  4.06 us
  transfers between devices with their start and end apart: 4, of which 3 were waited for; matrix products, arithmetic and copies ran while one was open for 0% of the time, Pallas kernels for 1%

profile of v13, /device:TPU:56, one launch (start us, length us, event | category | flops | bytes accessed | tf_op | source)
XLA Modules:
  0.0 80.3 jit_solution(5955955842411785904)
XLA Ops:
  0.0 0.0 copy-start
  0.0 1.1 %pad_maximum_fusion.held = bf16[192,448]{1,0:T(8,128)(2,1)S(1)} fusion(bf16[64,448]{1,0:T(8,128)(2,1)} %param.4, bf16[64,448]{1,0:T(8,128)(2,1)} %param.6, bf16[64,448]{1,0:T(8,128)(2,1)} %param.5), kind=kLoop, calls=%fused_computation.1 | loop fusion | flops 516096 | bytes 344064 | tf_op jit(solution)/shard_map/concatenate | solution.py:43
  1.1 0.1 shard_map.46
  1.2 13.0 %all_to_all.15 = bf16[4,64,384]{2,1,0:T(8,128)(2,1)S(1)} all-to-all(bf16[4,64,384]{2,1,0:T(8,128)(2,1)S(1)} %shard_map.46), channel_id=1, replica_groups=mesh['xa'=2,'xb'=2,'yl'=2,'zh'=4,'zl'=2,'core'=2,'tp'=4] {'xa','zl'}, dimensions={0} | all-to-all | bytes 393216 | tf_op jit(solution)/shard_map/all_to_all | solution.py:226
  14.2 0.1 shard_map.47
  14.3 0.0 copy-start.1
  14.3 1.0 %copy-done.1 = bf16[8,256,256]{2,1,0:T(8,128)(2,1)} copy-done((bf16[8,256,256]{2,1,0:T(8,128)(2,1)}, bf16[8,256,256]{2,1,0:T(8,128)(2,1)S(1)}, u32[]{:S(2)}) %copy-start.1) | copy-done | bytes 1048600
  15.3 5.5 %all-to-all-start.1 = ((bf16[8,256,256]{2,1,0:T(8,128)(2,1)}), bf16[8,256,256]{2,1,0:T(8,128)(2,1)}, u32[]{:S(2)}, u32[]{:S(2)}) async-start(bf16[8,256,256]{2,1,0:T(8,128)(2,1)} %copy-done.1), calls=%async_computation.1 | async-start | bytes 2097152 | tf_op jit(solution)/shard_map/all_to_all | solution.py:230
  20.8 19.0 %all_gather.3.refs_0_ = bf16[1024,128]{1,0:T(8,128)(2,1)S(1)} all-gather(bf16[256,128]{1,0:T(8,128)(2,1)S(1)} %get-tuple-element.12), channel_id=1, replica_groups=mesh['xa'=2,'xb'=2,'yl'=2,'zh'=4,'zl'=2,'core'=2,'tp'=4] {'zh'}, dimensions={0}, use_global_device_ids=true | all-gather | bytes 327680 | tf_op jit(solution)/shard_map/all_gather | solution.py:231
  39.8 0.0 all-to-all-done.1
  39.8 4.1 %shard_map.48 = bf16[1024,128]{1,0:T(8,128)(2,1)S(1)} custom-call(bf16[1024,128]{1,0:T(8,128)(2,1)S(1)} %all_gather.3.refs_0_, bf16[2048,256]{1,0:T(8,128)(2,1)} %bitcast.1.refs_1_), custom_call_target="tpu_custom_call" | custom-call | tf_op jit(solution)/shard_map/pallas_call | solution.py:130
  43.9 16.2 %all_to_all.16 = bf16[16,64,128]{2,1,0:T(8,128)(2,1)S(1)} all-to-all(bf16[16,64,128]{2,1,0:T(8,128)(2,1)S(1)} %bitcast.4), channel_id=1, replica_groups=mesh['xa'=2,'xb'=2,'yl'=2,'zh'=4,'zl'=2,'core'=2,'tp'=4] {'xa','zh','zl'}, dimensions={0} | all-to-all | bytes 524288 | tf_op jit(solution)/shard_map/all_to_all | solution.py:233
  60.1 0.0 copy-done
  60.1 0.6 shard_map.49
  60.7 3.8 %collective-permute-start = (bf16[64,896]{1,0:T(8,128)(2,1)S(1)}, bf16[64,896]{1,0:T(8,128)(2,1)S(1)}, u32[]{:S(2)}, u32[]{:S(2)}) collective-permute-start(bf16[64,896]{1,0:T(8,128)(2,1)S(1)} %get-tuple-element.16), channel_id=1, source_target_pairs={{0,2},{1,3},{2,0},{3,1},{4,6},{5,7},{6,4},{7,5},{8,10},{9,11},{10,... | collective-permute-start | bytes 344072 | tf_op jit(solution)/shard_map/ppermute | solution.py:216
  64.5 0.5 shard_map.50
  65.1 5.7 %collective-permute-start.1 = (bf16[64,896]{1,0:T(8,128)(2,1)S(1)}, bf16[64,896]{1,0:T(8,128)(2,1)S(1)}, u32[]{:S(2)}, u32[]{:S(2)}) collective-permute-start(bf16[64,896]{1,0:T(8,128)(2,1)S(1)} %get-tuple-element.17), channel_id=1, source_target_pairs={{0,1},{1,2},{2,3},{3,0},{4,5},{5,6},{6,7},{7,4},{8,9},{9,10},{10,1... | collective-permute-start | bytes 344072 | tf_op jit(solution)/shard_map/ppermute | solution.py:216
  70.8 1.9 %collective-permute-start.2 = (bf16[64,896]{1,0:T(8,128)(2,1)S(1)}, bf16[64,896]{1,0:T(8,128)(2,1)S(1)}, u32[]{:S(2)}, u32[]{:S(2)}) collective-permute-start(bf16[64,896]{1,0:T(8,128)(2,1)S(1)} %get-tuple-element.18), channel_id=1, source_target_pairs={{0,3},{1,0},{2,1},{3,2},{4,7},{5,4},{6,5},{7,6},{8,11},{9,8},{10,9... | collective-permute-start | bytes 344072 | tf_op jit(solution)/shard_map/ppermute | solution.py:216
  72.7 0.4 collective-permute-done
  73.1 0.9 %collective-permute-done.1 = bf16[64,896]{1,0:T(8,128)(2,1)S(1)} collective-permute-done((bf16[64,896]{1,0:T(8,128)(2,1)S(1)}, bf16[64,896]{1,0:T(8,128)(2,1)S(1)}, u32[]{:S(2)}, u32[]{:S(2)}) %collective-permute-start.1) | collective-permute-done | bytes 114720 | tf_op jit(solution)/shard_map/ppermute | solution.py:216
  74.0 5.6 %collective-permute-done.2 = bf16[64,896]{1,0:T(8,128)(2,1)S(1)} collective-permute-done((bf16[64,896]{1,0:T(8,128)(2,1)S(1)}, bf16[64,896]{1,0:T(8,128)(2,1)S(1)}, u32[]{:S(2)}, u32[]{:S(2)}) %collective-permute-start.2) | collective-permute-done | bytes 114720 | tf_op jit(solution)/shard_map/ppermute | solution.py:216
  79.6 0.7 add_convert_fusion
Async XLA Ops:
  0.0 60.1 %copy-start = (bf16[448,3584]{1,0:T(8,128)(2,1)S(1)}, bf16[448,3584]{1,0:T(8,128)(2,1)}, u32[]{:S(2)}) copy-start(bf16[448,3584]{1,0:T(8,128)(2,1)} %weight_ref.3) | copy-start | bytes 9633796
  14.3 1.0 %copy-start.1 = (bf16[8,256,256]{2,1,0:T(8,128)(2,1)}, bf16[8,256,256]{2,1,0:T(8,128)(2,1)S(1)}, u32[]{:S(2)}) copy-start(bf16[8,256,256]{2,1,0:T(8,128)(2,1)S(1)} %get-tuple-element.13) | copy-start | bytes 3145732
  15.3 24.5 %all-to-all-start.1 = ((bf16[8,256,256]{2,1,0:T(8,128)(2,1)}), bf16[8,256,256]{2,1,0:T(8,128)(2,1)}, u32[]{:S(2)}, u32[]{:S(2)}) async-start(bf16[8,256,256]{2,1,0:T(8,128)(2,1)} %copy-done.1), calls=%async_computation.1 | async-start | bytes 2097152 | tf_op jit(solution)/shard_map/all_to_all | solution.py:230
  60.7 12.4 %collective-permute-start = (bf16[64,896]{1,0:T(8,128)(2,1)S(1)}, bf16[64,896]{1,0:T(8,128)(2,1)S(1)}, u32[]{:S(2)}, u32[]{:S(2)}) collective-permute-start(bf16[64,896]{1,0:T(8,128)(2,1)S(1)} %get-tuple-element.16), channel_id=1, source_target_pairs={{0,2},{1,3},{2,0},{3,1},{4,6},{5,7},{6,4},{7,5},{8,10},{9,11},{10,... | collective-permute-start | bytes 344072 | tf_op jit(solution)/shard_map/ppermute | solution.py:216
  65.1 8.9 %collective-permute-start.1 = (bf16[64,896]{1,0:T(8,128)(2,1)S(1)}, bf16[64,896]{1,0:T(8,128)(2,1)S(1)}, u32[]{:S(2)}, u32[]{:S(2)}) collective-permute-start(bf16[64,896]{1,0:T(8,128)(2,1)S(1)} %get-tuple-element.17), channel_id=1, source_target_pairs={{0,1},{1,2},{2,3},{3,0},{4,5},{5,6},{6,7},{7,4},{8,9},{9,10},{10,1... | collective-permute-start | bytes 344072 | tf_op jit(solution)/shard_map/ppermute | solution.py:216
  70.8 8.8 %collective-permute-start.2 = (bf16[64,896]{1,0:T(8,128)(2,1)S(1)}, bf16[64,896]{1,0:T(8,128)(2,1)S(1)}, u32[]{:S(2)}, u32[]{:S(2)}) collective-permute-start(bf16[64,896]{1,0:T(8,128)(2,1)S(1)} %get-tuple-element.18), channel_id=1, source_target_pairs={{0,3},{1,0},{2,1},{3,2},{4,7},{5,4},{6,5},{7,6},{8,11},{9,8},{10,9... | collective-permute-start | bytes 344072 | tf_op jit(solution)/shard_map/ppermute | solution.py:216

commit v14 on v10

--- a/solution.py
+++ b/solution.py
@@ -156,68 +156,25 @@
         ).astype(attention_ref.dtype)
 
 
-def share_of(attention_ref, weight_ref, step, tp_size):
-    width = weight_ref.shape[1] // tp_size
-    member = lax.rem(lax.axis_index("tp") + step, tp_size)
-    columns = pl.ds(pl.multiple_of(member * width, LANES), width)
-    return jnp.dot(
-        attention_ref[...], weight_ref[:, columns], preferred_element_type=jnp.float32
-    )
-
-
-def project_first(parts, out_weight, heads, groups, rows, steps, tp_size):
+def project(parts, out_weight, heads, groups, rows, tp_size):
     features, columns = out_weight.shape
     width = columns // tp_size
 
-    def body(parts_ref, weight_ref, attention_ref, *out_refs):
+    def body(parts_ref, weight_ref, out_ref, attention_ref):
         combine(parts_ref, attention_ref, heads, groups, rows)
-        for step, out_ref in zip(steps, out_refs):
-            out_ref[...] = share_of(attention_ref, weight_ref, step, tp_size).astype(
-                out_ref.dtype
-            )
-
-    return pl.pallas_call(
-        body,
-        out_shape=[jax.ShapeDtypeStruct((rows, features), jnp.bfloat16)]
-        + [jax.ShapeDtypeStruct((rows, width), jnp.bfloat16) for _ in steps],
-        cost_estimate=pl.CostEstimate(
-            flops=2 * rows * features * width * len(steps),
-            bytes_accessed=2 * features * columns,
-            transcendentals=0,
-        ),
+        for member in range(tp_size):
+            out_ref[member] = jnp.dot(
+                attention_ref[...],
+                weight_ref[:, member * width : (member + 1) * width],
+                preferred_element_type=jnp.float32,
+            ).astype(out_ref.dtype)
+
+    return pl.pallas_call(
+        body,
+        out_shape=jax.ShapeDtypeStruct((tp_size, rows, width), jnp.bfloat16),
+        scratch_shapes=[pltpu.VMEM((rows, features), jnp.bfloat16)],
         compiler_params=pltpu.CompilerParams(vmem_limit_bytes=VMEM_LIMIT),
     )(parts, out_weight)
-
-
-def project_rest(attention, out_weight, steps, tp_size):
-    rows, features = attention.shape
-    columns = out_weight.shape[1]
-
-    def body(attention_ref, weight_ref, *out_refs):
-        for step, out_ref in zip(steps, out_refs):
-            out_ref[...] = share_of(attention_ref, weight_ref, step, tp_size).astype(
-                out_ref.dtype
-            )
-
-    return pl.pallas_call(
-        body,
-        out_shape=[
-            jax.ShapeDtypeStruct(
-                (rows, columns // tp_size), jnp.bfloat16 if step else jnp.float32
-            )
-            for step in steps
-        ],
-        cost_estimate=pl.CostEstimate(
-            flops=2 * rows * features * len(steps) * (columns // tp_size),
-            bytes_accessed=2 * features * columns,
-            transcendentals=0,
-        ),
-        compiler_params=pltpu.CompilerParams(vmem_limit_bytes=VMEM_LIMIT),
-    )(attention, out_weight)
-
-
-def to_member(share, step, tp_size):
-    return lax.ppermute(share, "tp", [(i, (i + step) % tp_size) for i in range(tp_size)])
 
 
 def shards(queries, keys, values, out_weight):
@@ -237,18 +194,9 @@
     returned = lax.all_to_all(
         partial.reshape(groups * heads, rows, LANES), RETURN_AXES, 0, 0, tiled=True
     )
-    far = tp_size // 2
-    near = [step for step in range(1, tp_size) if step != far]
-    attention, *near_shares = project_first(
-        returned.reshape(-1, LANES), out_weight, heads, groups, rows, near, tp_size
-    )
-    arrived = [to_member(share, step, tp_size) for share, step in zip(near_shares, near)]
-    far_share, own_share = project_rest(attention, out_weight, [far, 0], tp_size)
-    arrived.append(to_member(far_share, far, tp_size))
-    total = own_share
-    for share in arrived:
-        total = total + share.astype(jnp.float32)
-    return total.astype(jnp.bfloat16)
+    shares = project(returned.reshape(-1, LANES), out_weight, heads, groups, rows, tp_size)
+    arrived = lax.all_to_all(shares, "tp", 0, 0, tiled=True)
+    return jnp.sum(arrived.astype(jnp.float32), axis=0).astype(jnp.bfloat16)
 
 
 def solution(mesh):

time: 81.8 us -> 80.6 us (0.985)
  the two profiles are of different devices: /device:TPU:56 before, /device:TPU:72 now
where the time goes in v14:
time: 80.6 us; the launch traced here: 80.2 us
  blocking collectives  65.9 us (82%)
  starting transfers between devices  5.75 us (7%)
  Pallas kernels  5.02 us (6%)
  local copies, waits for them, and re-layouts  1.91 us (2%)
  other arithmetic  1.64 us (2%)
    all_to_all x1, blocking collectives, shards(): arrived = lax.all_to_all(shares, 'tp', 0, 0, tiled=True)  19.8 us
    all_to_all x1, blocking collectives, shards(): lax.all_to_all(partial.reshape(groups * heads, rows, LANES), RETURN_AXES,...  17.5 us
    all_gather x1, blocking collectives, shards(): got_q = lax.all_gather(own_q, 'zh', axis=0, tiled=True)  17.3 us
    all_to_all x1, blocking collectives, shards(): lax.all_to_all(pack(queries, keys, values, heads), HEAD_AXES, 0, 0, tiled...  11.3 us
    all_to_all x1, starting transfers between devices, shards(): got_kv = lax.all_to_all(sent_kv, KEY_AXES, 0, 0, tiled=True)  5.75 us
    pallas_call x1, Pallas kernels, attend(): pl.pallas_call(body, out_shape=jax.ShapeDtypeStruct(queries.shape, querie...  2.83 us
    unnamed x2, local copies, waits for them, and re-layouts  1.91 us
  transfers between devices with their start and end apart: 1, of which 0 were waited for; matrix products, arithmetic and copies ran while one was open for 0% of the time, Pallas kernels for 0%

profile of v14, /device:TPU:72, one launch (start us, length us, event | category | flops | bytes accessed | tf_op | source)
XLA Modules:
  0.0 80.2 jit_solution(9913764732995178337)
XLA Ops:
  0.0 0.9 %pad_maximum_fusion.held = bf16[192,448]{1,0:T(8,128)(2,1)S(1)} fusion(bf16[64,448]{1,0:T(8,128)(2,1)} %param.4, bf16[64,448]{1,0:T(8,128)(2,1)} %param.6, bf16[64,448]{1,0:T(8,128)(2,1)} %param.5), kind=kLoop, calls=%fused_computation | loop fusion | flops 516096 | bytes 344064 | tf_op jit(solution)/shard_map/concatenate | solution.py:43
  0.9 0.1 shard_map.46
  1.1 11.3 %all_to_all.20 = bf16[4,64,384]{2,1,0:T(8,128)(2,1)S(1)} all-to-all(bf16[4,64,384]{2,1,0:T(8,128)(2,1)S(1)} %shard_map.46), channel_id=1, replica_groups=mesh['xa'=2,'xb'=2,'yl'=2,'zh'=4,'zl'=2,'core'=2,'tp'=4] {'xa','zl'}, dimensions={0} | all-to-all | bytes 393216 | tf_op jit(solution)/shard_map/all_to_all | solution.py:187
  12.4 1.1 %shard_map.47 = (bf16[256,128]{1,0:T(8,128)(2,1)S(1)}, bf16[8,256,256]{2,1,0:T(8,128)(2,1)}) custom-call(bf16[256,384]{1,0:T(8,128)(2,1)S(1)} %bitcast.7), custom_call_target="tpu_custom_call" | custom-call | tf_op jit(solution)/shard_map/pallas_call | solution.py:56
  13.5 5.8 %all-to-all-start.1 = ((bf16[8,256,256]{2,1,0:T(8,128)(2,1)}), bf16[8,256,256]{2,1,0:T(8,128)(2,1)S(1)}, u32[]{:S(2)}, u32[]{:S(2)}) async-start(bf16[8,256,256]{2,1,0:T(8,128)(2,1)} %get-tuple-element.8), calls=%async_computation.1 | async-start | bytes 2097152 | tf_op jit(solution)/shard_map/all_to_all | solution.py:191
  19.2 17.3 %all_gather.3.refs_0_ = bf16[1024,128]{1,0:T(8,128)(2,1)S(1)} all-gather(bf16[256,128]{1,0:T(8,128)(2,1)S(1)} %get-tuple-element.7), channel_id=1, replica_groups=mesh['xa'=2,'xb'=2,'yl'=2,'zh'=4,'zl'=2,'core'=2,'tp'=4] {'zh'}, dimensions={0}, use_global_device_ids=true | all-gather | bytes 327680 | tf_op jit(solution)/shard_map/all_gather | solution.py:192
  36.5 0.0 all-to-all-done.1
  36.5 2.8 %shard_map.48 = bf16[1024,128]{1,0:T(8,128)(2,1)S(1)} custom-call(bf16[1024,128]{1,0:T(8,128)(2,1)S(1)} %all_gather.3.refs_0_, bf16[2048,256]{1,0:T(8,128)(2,1)S(1)} %bitcast.4), custom_call_target="tpu_custom_call" | custom-call | tf_op jit(solution)/shard_map/pallas_call | solution.py:130
  39.3 17.5 %all_to_all.21 = bf16[16,64,128]{2,1,0:T(8,128)(2,1)S(1)} all-to-all(bf16[16,64,128]{2,1,0:T(8,128)(2,1)S(1)} %bitcast.5), channel_id=1, replica_groups=mesh['xa'=2,'xb'=2,'yl'=2,'zh'=4,'zl'=2,'core'=2,'tp'=4] {'zh','xa','zl'}, dimensions={0} | all-to-all | bytes 524288 | tf_op jit(solution)/shard_map/all_to_all | solution.py:194
  56.8 0.0 copy-start
  56.8 1.9 %copy-done = bf16[448,3584]{1,0:T(8,128)(2,1)S(1)} copy-done((bf16[448,3584]{1,0:T(8,128)(2,1)S(1)}, bf16[448,3584]{1,0:T(8,128)(2,1)}, u32[]{:S(2)}) %copy-start) | copy-done | bytes 3211288
  58.7 1.0 %shard_map.49 = bf16[4,64,896]{2,1,0:T(8,128)(2,1)S(1)} custom-call(bf16[1024,128]{1,0:T(8,128)(2,1)S(1)} %bitcast.6, bf16[448,3584]{1,0:T(8,128)(2,1)S(1)} %copy-done), custom_call_target="tpu_custom_call" | custom-call | tf_op jit(solution)/shard_map/pallas_call | solution.py:172
  59.7 19.8 %all_to_all.22 = bf16[4,64,896]{2,1,0:T(8,128)(2,1)S(1)} all-to-all(bf16[4,64,896]{2,1,0:T(8,128)(2,1)S(1)} %shard_map.49), channel_id=1, replica_groups=mesh['xa'=2,'xb'=2,'yl'=2,'zh'=4,'zl'=2,'core'=2,'tp'=4] {'tp'}, dimensions={0} | all-to-all | bytes 917504 | tf_op jit(solution)/shard_map/all_to_all | solution.py:198
  79.5 0.7 reduce_sum.12
Async XLA Ops:
  13.5 23.0 %all-to-all-start.1 = ((bf16[8,256,256]{2,1,0:T(8,128)(2,1)}), bf16[8,256,256]{2,1,0:T(8,128)(2,1)S(1)}, u32[]{:S(2)}, u32[]{:S(2)}) async-start(bf16[8,256,256]{2,1,0:T(8,128)(2,1)} %get-tuple-element.8), calls=%async_computation.1 | async-start | bytes 2097152 | tf_op jit(solution)/shard_map/all_to_all | solution.py:191
  56.8 1.9 %copy-start = (bf16[448,3584]{1,0:T(8,128)(2,1)S(1)}, bf16[448,3584]{1,0:T(8,128)(2,1)}, u32[]{:S(2)}) copy-start(bf16[448,3584]{1,0:T(8,128)(2,1)} %weight_ref.1) | copy-start | bytes 9633796

commit v15 on v14

--- a/solution.py
+++ b/solution.py
@@ -160,19 +160,33 @@
     features, columns = out_weight.shape
     width = columns // tp_size
 
-    def body(parts_ref, weight_ref, out_ref, attention_ref):
+    def body(parts_ref, weight_hbm, out_ref, attention_ref, weight_ref, arrived):
+        loads = [
+            pltpu.make_async_copy(
+                weight_hbm.at[:, member * width : (member + 1) * width],
+                weight_ref.at[member],
+                arrived.at[member],
+            )
+            for member in range(tp_size)
+        ]
+        for load in loads:
+            load.start()
         combine(parts_ref, attention_ref, heads, groups, rows)
-        for member in range(tp_size):
+        for member, load in enumerate(loads):
+            load.wait()
             out_ref[member] = jnp.dot(
-                attention_ref[...],
-                weight_ref[:, member * width : (member + 1) * width],
-                preferred_element_type=jnp.float32,
+                attention_ref[...], weight_ref[member], preferred_element_type=jnp.float32
             ).astype(out_ref.dtype)
 
     return pl.pallas_call(
         body,
+        in_specs=[pl.BlockSpec(memory_space=pltpu.VMEM), pl.BlockSpec(memory_space=pl.ANY)],
         out_shape=jax.ShapeDtypeStruct((tp_size, rows, width), jnp.bfloat16),
-        scratch_shapes=[pltpu.VMEM((rows, features), jnp.bfloat16)],
+        scratch_shapes=[
+            pltpu.VMEM((rows, features), jnp.bfloat16),
+            pltpu.VMEM((tp_size, features, width), jnp.bfloat16),
+            pltpu.SemaphoreType.DMA((tp_size,)),
+        ],
         compiler_params=pltpu.CompilerParams(vmem_limit_bytes=VMEM_LIMIT),
     )(parts, out_weight)
 

time: 80.6 us -> 81.5 us (1.011)
  Pallas kernels: 5.02 us -> 5.92 us
    pallas_call x1, Pallas kernels: 0.99 us -> 1.89 us  [project(): pl.pallas_call(body, in_specs=[pl.BlockSpec(memory_space=pltpu.VMEM), pl....]
where the time goes in v15:
time: 81.5 us; the launch traced here: 81.1 us
  blocking collectives  65.9 us (81%)
  Pallas kernels  5.92 us (7%)
  starting transfers between devices  5.75 us (7%)
  local copies, waits for them, and re-layouts  1.91 us (2%)
  other arithmetic  1.64 us (2%)
    all_to_all x1, blocking collectives, shards(): arrived = lax.all_to_all(shares, 'tp', 0, 0, tiled=True)  19.8 us
    all_to_all x1, blocking collectives, shards(): lax.all_to_all(partial.reshape(groups * heads, rows, LANES), RETURN_AXES,...  17.5 us
    all_gather x1, blocking collectives, shards(): got_q = lax.all_gather(own_q, 'zh', axis=0, tiled=True)  17.3 us
    all_to_all x1, blocking collectives, shards(): lax.all_to_all(pack(queries, keys, values, heads), HEAD_AXES, 0, 0, tiled...  11.3 us
    all_to_all x1, starting transfers between devices, shards(): got_kv = lax.all_to_all(sent_kv, KEY_AXES, 0, 0, tiled=True)  5.75 us
    pallas_call x1, Pallas kernels, attend(): pl.pallas_call(body, out_shape=jax.ShapeDtypeStruct(queries.shape, querie...  2.83 us
    unnamed x2, local copies, waits for them, and re-layouts  1.91 us
    pallas_call x1, Pallas kernels, project(): pl.pallas_call(body, in_specs=[pl.BlockSpec(memory_space=pltpu.VMEM), pl....  1.89 us
  transfers between devices with their start and end apart: 1, of which 0 were waited for; matrix products, arithmetic and copies ran while one was open for 0% of the time, Pallas kernels for 0%

profile of v15, /device:TPU:72, one launch (start us, length us, event | category | flops | bytes accessed | tf_op | source)
XLA Modules:
  0.0 81.1 jit_solution(14973517717295467730)
XLA Ops:
  0.0 0.9 %pad_maximum_fusion.held = bf16[192,448]{1,0:T(8,128)(2,1)S(1)} fusion(bf16[64,448]{1,0:T(8,128)(2,1)} %param.4, bf16[64,448]{1,0:T(8,128)(2,1)} %param.6, bf16[64,448]{1,0:T(8,128)(2,1)} %param.5), kind=kLoop, calls=%fused_computation | loop fusion | flops 516096 | bytes 344064 | tf_op jit(solution)/shard_map/concatenate | solution.py:43
  0.9 0.1 shard_map.46
  1.1 11.3 %all_to_all.20 = bf16[4,64,384]{2,1,0:T(8,128)(2,1)S(1)} all-to-all(bf16[4,64,384]{2,1,0:T(8,128)(2,1)S(1)} %shard_map.46), channel_id=1, replica_groups=mesh['xa'=2,'xb'=2,'yl'=2,'zh'=4,'zl'=2,'core'=2,'tp'=4] {'xa','zl'}, dimensions={0} | all-to-all | bytes 393216 | tf_op jit(solution)/shard_map/all_to_all | solution.py:201
  12.4 1.1 %shard_map.47 = (bf16[256,128]{1,0:T(8,128)(2,1)S(1)}, bf16[8,256,256]{2,1,0:T(8,128)(2,1)}) custom-call(bf16[256,384]{1,0:T(8,128)(2,1)S(1)} %bitcast.7), custom_call_target="tpu_custom_call" | custom-call | tf_op jit(solution)/shard_map/pallas_call | solution.py:56
  13.5 5.8 %all-to-all-start.1 = ((bf16[8,256,256]{2,1,0:T(8,128)(2,1)}), bf16[8,256,256]{2,1,0:T(8,128)(2,1)S(1)}, u32[]{:S(2)}, u32[]{:S(2)}) async-start(bf16[8,256,256]{2,1,0:T(8,128)(2,1)} %get-tuple-element.8), calls=%async_computation.1 | async-start | bytes 2097152 | tf_op jit(solution)/shard_map/all_to_all | solution.py:205
  19.2 17.3 %all_gather.3.refs_0_ = bf16[1024,128]{1,0:T(8,128)(2,1)S(1)} all-gather(bf16[256,128]{1,0:T(8,128)(2,1)S(1)} %get-tuple-element.7), channel_id=1, replica_groups=mesh['xa'=2,'xb'=2,'yl'=2,'zh'=4,'zl'=2,'core'=2,'tp'=4] {'zh'}, dimensions={0}, use_global_device_ids=true | all-gather | bytes 327680 | tf_op jit(solution)/shard_map/all_gather | solution.py:206
  36.5 0.0 all-to-all-done.1
  36.5 2.8 %shard_map.48 = bf16[1024,128]{1,0:T(8,128)(2,1)S(1)} custom-call(bf16[1024,128]{1,0:T(8,128)(2,1)S(1)} %all_gather.3.refs_0_, bf16[2048,256]{1,0:T(8,128)(2,1)S(1)} %bitcast.4), custom_call_target="tpu_custom_call" | custom-call | tf_op jit(solution)/shard_map/pallas_call | solution.py:130
  39.3 17.5 %all_to_all.21 = bf16[16,64,128]{2,1,0:T(8,128)(2,1)S(1)} all-to-all(bf16[16,64,128]{2,1,0:T(8,128)(2,1)S(1)} %bitcast.5), channel_id=1, replica_groups=mesh['xa'=2,'xb'=2,'yl'=2,'zh'=4,'zl'=2,'core'=2,'tp'=4] {'zh','xa','zl'}, dimensions={0} | all-to-all | bytes 524288 | tf_op jit(solution)/shard_map/all_to_all | solution.py:208
  56.8 0.0 copy-start
  56.8 1.9 %copy-done = bf16[448,3584]{1,0:T(8,128)(2,1)S(1)} copy-done((bf16[448,3584]{1,0:T(8,128)(2,1)S(1)}, bf16[448,3584]{1,0:T(8,128)(2,1)}, u32[]{:S(2)}) %copy-start) | copy-done | bytes 3211288
  58.7 1.9 %shard_map.49 = bf16[4,64,896]{2,1,0:T(8,128)(2,1)S(1)} custom-call(bf16[1024,128]{1,0:T(8,128)(2,1)S(1)} %bitcast.6, bf16[448,3584]{1,0:T(8,128)(2,1)S(1)} %copy-done), custom_call_target="tpu_custom_call" | custom-call | tf_op jit(solution)/shard_map/pallas_call | solution.py:181
  60.6 19.8 %all_to_all.22 = bf16[4,64,896]{2,1,0:T(8,128)(2,1)S(1)} all-to-all(bf16[4,64,896]{2,1,0:T(8,128)(2,1)S(1)} %shard_map.49), channel_id=1, replica_groups=mesh['xa'=2,'xb'=2,'yl'=2,'zh'=4,'zl'=2,'core'=2,'tp'=4] {'tp'}, dimensions={0} | all-to-all | bytes 917504 | tf_op jit(solution)/shard_map/all_to_all | solution.py:212
  80.4 0.7 reduce_sum.12
Async XLA Ops:
  13.5 23.0 %all-to-all-start.1 = ((bf16[8,256,256]{2,1,0:T(8,128)(2,1)}), bf16[8,256,256]{2,1,0:T(8,128)(2,1)S(1)}, u32[]{:S(2)}, u32[]{:S(2)}) async-start(bf16[8,256,256]{2,1,0:T(8,128)(2,1)} %get-tuple-element.8), calls=%async_computation.1 | async-start | bytes 2097152 | tf_op jit(solution)/shard_map/all_to_all | solution.py:205
  56.8 1.9 %copy-start = (bf16[448,3584]{1,0:T(8,128)(2,1)S(1)}, bf16[448,3584]{1,0:T(8,128)(2,1)}, u32[]{:S(2)}) copy-start(bf16[448,3584]{1,0:T(8,128)(2,1)} %weight_hbm.1) | copy-start | bytes 9633796
